TPU v7x, 512 devices: a whole 4x8x8 slice. The times are simulated.
512 devices in a mesh: region: 16 (over z, core), block: 32 (over x, y).
Axes of the slice: x: 4, y: 8, z: 8, core: 2. Of those that a mesh axis runs over, the one named last changes fastest.
Arguments:
- features: bfloat16 [2048, 64, 512], P(('region', 'block')), may hold values from -6 to 6
- counts: int32 [2048], P(('region', 'block')), may hold values from 0 to 512, as said below
- rebalance: int32 [2048], P(('region', 'block')), may hold values from -1 to 1023, as said below
- neighbors: int32 [2048, 26], P(('region', 'block')), may hold values from -1 to 2047, as said below
- coarse_owner: int32 [2048], P(('region', 'block')), may hold values from -1 to 15, as said below
- conv_weight: bfloat16 [27, 64, 128], replicated, may hold values from -0.15625 to 0.15625
- convolution_bias_vector: float32 [128], replicated, may hold values from -3 to 3
- merged_adjoint: bfloat16 [1024, 8192], P(('region', 'block')), may hold values from -0.119628906 to 0.119628906
Outputs:
- pooled: bfloat16 [1024, 8192], P(('region', 'block'))
- weight_grad: float32 [27, 64, 128], replicated
- bias_grad: float32 [128], replicated
Inputs may be any that keep to these rules, and one draw needn't show every extreme that they name: `counts`: 0 marks an empty block; exactly half of each region group's blocks are occupied. `rebalance`: -1 for an empty block; else a row of the block's own region group, each row of a group taken by exactly one block; of the blocks of one device at most 1 have rows on one same device. `neighbors`: -1 where an offset has no occupied neighbour and at every offset of an empty block; neighbours at offsets with ea = 0 lie on the same device, the others on the same device or one of the two beside it along block in the same region group. `coarse_owner`: -1 for an empty block; of the blocks on one device of the working layout at most 1 have the same coarse owner.
All inputs are finite; a program needn't handle non-finite values.
Results may differ from a plain program's by a relative error of at most 0.0029.
Values may be sent and summed in bfloat16 or wider, within the bound.
No kernel may reach another device: no remote copies, remote signals or barrier semaphores. Data moves between devices by JAX's collectives and lax.ppermute only.
A program may use at most 128 MiB of HBM per device.

v0:
```python
import math

import jax
import jax.numpy as jnp
from jax import lax
from jax.sharding import PartitionSpec as P


def extended_2(array, sides, width):
    for axis, dim in sides:
        size, length = (lax.axis_size(axis), array.shape[dim])
        up = [(i, (i + 1) % size) for i in range(size - 1)]
        down = [(j, i) for i, j in up]
        last = lax.slice_in_dim(array, length - width, length, axis=dim)
        leading = lax.slice_in_dim(array, 0, width, axis=dim)
        before = lax.ppermute(last, axis, up)
        after = lax.ppermute(leading, axis, down)
        array = jnp.concatenate([before, array, after], axis=dim)
    return array


def filled_fraction(block_counts):
    hashed = jnp.arange(512, dtype=jnp.int32) * 167 % 512
    return hashed[None, :] < block_counts[:, None]


def offset_list():
    return [
        (ea, eb, ec)
        for ea in (-1, 0, 1)
        for eb in (-1, 0, 1)
        for ec in (-1, 0, 1)
        if (ea, eb, ec) != (0, 0, 0)
    ]


def source_range(step):
    return (7, 8) if step < 0 else (0, 1) if step > 0 else (0, 8)


def target_range(step):
    return (0, 1) if step < 0 else (9, 10) if step > 0 else (1, 9)


def padded_cube(blocks_in, shell_in):
    rows_now, channels = (blocks_in.shape[0], blocks_in.shape[1])
    cube = jnp.zeros((rows_now, channels, 10, 10, 10), blocks_in.dtype)
    cube = cube.at[:, :, 1:9, 1:9, 1:9].set(blocks_in.reshape(rows_now, channels, 8, 8, 8))
    pointer = 0
    for offset in offset_list():
        a_low, a_high = target_range(offset[0])
        b_low, b_high = target_range(offset[1])
        c_low, c_high = target_range(offset[2])
        extent = (a_high - a_low) * (b_high - b_low) * (c_high - c_low)
        piece = shell_in[:, :, pointer : pointer + extent].reshape(
            rows_now, channels, a_high - a_low, b_high - b_low, c_high - c_low
        )
        cube = cube.at[:, :, a_low:a_high, b_low:b_high, c_low:c_high].set(piece)
        pointer = pointer + extent
    return cube


def taps(blocks_in, shell_in):
    rows_now, channels = (blocks_in.shape[0], blocks_in.shape[1])
    cube = padded_cube(blocks_in, shell_in)
    pieces = []
    for ea in (-1, 0, 1):
        for eb in (-1, 0, 1):
            for ec in (-1, 0, 1):
                window = cube[:, :, 1 + ea : 9 + ea, 1 + eb : 9 + eb, 1 + ec : 9 + ec]
                pieces.append(window.reshape(rows_now, channels, 512))
    return jnp.concatenate(pieces, axis=1)


def pool_table():
    voxels = jnp.arange(512, dtype=jnp.int32)
    cell_index = (voxels // 128 * 4 + voxels // 16 % 4) * 4 + voxels % 8 // 2
    return jnp.where(
        cell_index[:, None] == jnp.arange(64, dtype=jnp.int32)[None, :], 0.125, 0.0
    ).astype(jnp.float32)


def positions(destination, usable, capacity):
    same_dest = (destination[:, None] == destination[None, :]) & usable[:, None] & usable[None, :]
    ranking = jnp.sum(jnp.tril(same_dest.astype(jnp.int32), -1), axis=1)
    return jnp.where(usable, destination * capacity + ranking, -1)


def route(position, slot_total):
    matches = position[:, None] == jnp.arange(slot_total, dtype=jnp.int32)[None, :]
    row_ids = jnp.arange(position.shape[0], dtype=jnp.int32)[:, None]
    return (jnp.sum(jnp.where(matches, row_ids, 0), axis=0), jnp.any(matches, axis=0))


def pick(values, source, filled):
    taken = jnp.take(values, source, axis=0)
    shaped = filled.reshape((-1,) + (1,) * (values.ndim - 1))
    return jnp.where(shaped, taken, jnp.zeros_like(taken))


def forward_blocks(
    blocks_in, shell_in, block_counts, flattened_weight, convolution_bias_vector, table
):
    block_total = blocks_in.shape[0]
    sample_number = math.gcd(block_total, 4)
    result_feature_count = convolution_bias_vector.shape[0]

    def forward_advance(component):
        part_blocks, part_shell, part_counts = component
        stacked_layers = taps(part_blocks, part_shell)
        before_activation = (
            jnp.einsum(
                "esh,sb->ebh", stacked_layers, flattened_weight, preferred_element_type=jnp.float32
            )
            + convolution_bias_vector[None, :, None]
        )
        activation = jnp.where(
            filled_fraction(part_counts)[:, None, :], jax.nn.silu(before_activation), 0.0
        )
        pooled_part = jnp.einsum("ncv,vp->ncp", activation, table, precision=lax.Precision.HIGHEST)
        return pooled_part.reshape(sample_number, result_feature_count * 64).astype(jnp.bfloat16)

    turns = block_total // sample_number
    elements = (
        blocks_in.reshape((turns, sample_number) + blocks_in.shape[1:]),
        shell_in.reshape((turns, sample_number) + shell_in.shape[1:]),
        block_counts.reshape(turns, sample_number),
    )
    return lax.map(forward_advance, elements).reshape(block_total, result_feature_count * 64)


def backward_blocks(
    blocks_in, shell_in, block_counts, gradient, flattened_weight, convolution_bias_vector, table
):
    block_total = blocks_in.shape[0]
    sample_number = math.gcd(block_total, 4)
    result_feature_count = convolution_bias_vector.shape[0]

    def backward_advance(running, component):
        part_blocks, part_shell, part_counts, part_grad = component
        stacked_layers = taps(part_blocks, part_shell)
        before_activation = (
            jnp.einsum(
                "esh,sb->ebh", stacked_layers, flattened_weight, preferred_element_type=jnp.float32
            )
            + convolution_bias_vector[None, :, None]
        )
        mask_view = filled_fraction(part_counts)[:, None, :]
        spread_grad = jnp.einsum(
            "ncp,vp->ncv",
            part_grad.reshape(sample_number, result_feature_count, 64).astype(jnp.float32),
            table,
            precision=lax.Precision.HIGHEST,
        )
        sigmoid_value = jax.nn.sigmoid(before_activation)
        grad_pre = jnp.where(
            mask_view,
            spread_grad * sigmoid_value * (1.0 + before_activation * (1.0 - sigmoid_value)),
            0.0,
        )
        gradient_lower_bits = grad_pre.astype(jnp.bfloat16)
        partial_weight = jnp.einsum(
            "sez,stz->et", stacked_layers, gradient_lower_bits, preferred_element_type=jnp.float32
        )
        return ((running[0] + partial_weight, running[1] + jnp.sum(grad_pre, axis=(0, 2))), None)

    turns = block_total // sample_number
    elements = (
        blocks_in.reshape((turns, sample_number) + blocks_in.shape[1:]),
        shell_in.reshape((turns, sample_number) + shell_in.shape[1:]),
        block_counts.reshape(turns, sample_number),
        gradient.reshape(turns, sample_number, gradient.shape[1]),
    )
    start_state = (
        jnp.zeros(flattened_weight.shape, jnp.float32),
        jnp.zeros((result_feature_count,), jnp.float32),
    )
    totals, _ = lax.scan(backward_advance, start_state, elements)
    return totals


def owners(pooled_work, work_owner, merged_adjoint, region_count):
    work_slots = pooled_work.shape[0]
    owner_limit = (work_slots + region_count - 1) // region_count
    position = positions(work_owner, jnp.ones((work_slots,), bool), owner_limit)
    source, filled = route(position, region_count * owner_limit)
    send_rows = pick(pooled_work, source, filled).reshape(region_count, owner_limit, -1)
    slot_tags = jnp.where(filled, source, -1).reshape(region_count, owner_limit)
    received, received_slot = (
        lax.all_to_all(send_rows, "region", split_axis=0, concat_axis=0, tiled=True),
        lax.all_to_all(slot_tags, "region", split_axis=0, concat_axis=0, tiled=True),
    )
    received_slot = received_slot.reshape(-1)
    arrival, _ = route(received_slot, work_slots)
    pooled = jnp.take(received.reshape(region_count * owner_limit, -1), arrival, axis=0)
    returned_cot = pick(
        merged_adjoint, jnp.clip(received_slot, 0, work_slots - 1), received_slot >= 0
    )
    returned = lax.all_to_all(
        returned_cot.reshape(region_count, owner_limit, -1),
        "region",
        split_axis=0,
        concat_axis=0,
        tiled=True,
    )
    return (pooled, jnp.take(returned.reshape(region_count * owner_limit, -1), position, axis=0))


def per_device(
    features,
    counts,
    rebalance,
    neighbors,
    coarse_owner,
    conv_weight,
    convolution_bias_vector,
    merged_adjoint,
):
    home_slots = features.shape[0]
    channels = features.shape[1]
    block_count = lax.axis_size("block")
    region_count = lax.axis_size("region")
    work_slots = home_slots // 2
    send_cap = (home_slots + block_count - 1) // block_count
    first_block = (lax.axis_index("region") * block_count + lax.axis_index("block")) * home_slots
    occupied_mask = filled_fraction(counts)
    masked = jnp.where(occupied_mask[:, None, :], features, jnp.zeros_like(features))
    masked_cube = masked.reshape(home_slots, channels, 8, 8, 8)
    layers = jnp.stack([masked_cube[:, :, 0], masked_cube[:, :, 7]], axis=1).reshape(
        home_slots, 2, channels * 64
    )
    extended = extended_2(layers, (("block", 0),), home_slots)
    extended = extended.reshape(3 * home_slots, 2, channels, 8, 8)
    shell_parts = []
    for column, offset in enumerate(offset_list()):
        target = neighbors[:, column]
        b_low, b_high = source_range(offset[1])
        c_low, c_high = source_range(offset[2])
        if offset[0] != 0:
            layer_view = extended[:, 1 if offset[0] < 0 else 0]
            source_all = layer_view[:, :, b_low:b_high, c_low:c_high].reshape(
                3 * home_slots, channels, -1
            )
            lookup = jnp.clip(target - (first_block - home_slots), 0, 3 * home_slots - 1)
        else:
            source_all = masked_cube[:, :, :, b_low:b_high, c_low:c_high].reshape(
                home_slots, channels, -1
            )
            lookup = jnp.clip(target - first_block, 0, home_slots - 1)
        piece = jnp.take(source_all, lookup, axis=0)
        shell_parts.append(jnp.where((target >= 0)[:, None, None], piece, jnp.zeros_like(piece)))
    shells = jnp.concatenate(shell_parts, axis=2)
    flattened_weight = conv_weight.reshape(-1, conv_weight.shape[2])
    table = pool_table()
    occupied = rebalance >= 0
    work_device = rebalance // work_slots % block_count
    work_slot = rebalance % work_slots
    position = positions(work_device, occupied, send_cap)
    source, filled = route(position, block_count * send_cap)
    slot_tag = jnp.where(filled, jnp.take(work_slot, source), -1)
    tag_rows = jnp.stack(
        [slot_tag, jnp.take(counts, source), jnp.take(coarse_owner, source)], axis=1
    )
    send_blocks = pick(masked, source, filled).reshape((block_count, send_cap) + masked.shape[1:])
    send_shells = pick(shells, source, filled).reshape((block_count, send_cap) + shells.shape[1:])
    got_blocks, got_shells, got_tags = (
        lax.all_to_all(send_blocks, "block", split_axis=0, concat_axis=0, tiled=True),
        lax.all_to_all(send_shells, "block", split_axis=0, concat_axis=0, tiled=True),
        lax.all_to_all(
            tag_rows.reshape(block_count, send_cap, 3),
            "block",
            split_axis=0,
            concat_axis=0,
            tiled=True,
        ),
    )
    got_tags = got_tags.reshape(block_count * send_cap, 3)
    arrival, _ = route(got_tags[:, 0], work_slots)
    work_blocks = jnp.take(
        got_blocks.reshape((block_count * send_cap,) + masked.shape[1:]), arrival, axis=0
    )
    work_shells = jnp.take(
        got_shells.reshape((block_count * send_cap,) + shells.shape[1:]), arrival, axis=0
    )
    labour_tallies = jnp.take(got_tags[:, 1], arrival)
    work_owner = jnp.take(got_tags[:, 2], arrival)
    pooled_work = forward_blocks(
        work_blocks, work_shells, labour_tallies, flattened_weight, convolution_bias_vector, table
    )
    pooled, grad_work = owners(pooled_work, work_owner, merged_adjoint, region_count)
    weight_grad, bias_grad = backward_blocks(
        work_blocks,
        work_shells,
        labour_tallies,
        grad_work,
        flattened_weight,
        convolution_bias_vector,
        table,
    )
    weight_total, bias_total = lax.psum((weight_grad, bias_grad), ("region", "block"))
    return (pooled, weight_total.reshape(conv_weight.shape[0], channels, -1), bias_total)


def solution(mesh):
    in_specs = (
        P(("region", "block"), None, None),
        P(("region", "block")),
        P(("region", "block")),
        P(("region", "block"), None),
        P(("region", "block")),
        P(),
        P(),
        P(("region", "block"), None),
    )
    out_specs = (P(("region", "block"), None), P(), P())
    return jax.shard_map(
        per_device, mesh=mesh, in_specs=in_specs, out_specs=out_specs, check_vma=False
    )
```

profile of v0, /device:TPU:1, one launch (start us, length us, event | category | flops | bytes accessed | tf_op | source)
XLA Modules:
  0.0 621.3 jit_solution(9635796547931699754)
XLA Ops:
  12.9 4.7 collective-permute-start
  19.9 7.5 %fusion.59 = (s32[32,1]{0,1:T(1,128)S(1)}, s32[32,1]{0,1:T(1,128)S(1)}, s32[32,1]{0,1:T(1,128)S(1)}) fusion(pred[32]{0:T(512)(128)(4,1)S(1)} %fusion.39, s32[]{:T(128)} %bitcast.3, s32[]{:T(128)} %bitcast.2, s32[]{:T(128)} %bitcast.1, s32[]{:T(128)} %bitcast, s32[32]{0:T(128)S(1)} %select_reduce_fusion, s32[]{:T(128)} %bitcast.8, s32[]{:T(128)} %bitcast.7, ...), kind=kLoop, calls=%fused_computation.405 | loop fusion | flops 704 | bytes 592 | tf_op jit(solution)/shard_map/stack | solution.py:261
  28.1 9.8 %all-to-all-start = ((s32[32,1,3]{2,1,0:T(1,128)}), s32[32,1,3]{2,1,0:T(1,128)S(1)}, u32[]{:S(2)}, u32[]{:S(2)}) async-start(s32[32,1,3]{2,1,0:T(1,128)} %copy.466), calls=%async_computation | async-start | bytes 32768 | tf_op jit(solution)/shard_map/all_to_all | solution.py:269
  62.2 11.8 %all-to-all-start.4 = ((s32[16,1,1]{2,1,0:T(1,128)}), s32[16,1,1]{2,1,0:T(1,128)S(1)}, u32[]{:S(2)}, u32[]{:S(2)}) async-start(s32[16,1,1]{2,1,0:T(1,128)} %copy.468), calls=%async_computation.4 | async-start | bytes 16384 | tf_op jit(solution)/shard_map/all_to_all | solution.py:191
  75.5 5.5 all-to-all-done.4
  84.9 4.6 all-to-all-start.5
  89.6 4.8 reshape.4870
  94.4 3.3 fusion.65
  97.7 2.8 copy.593
  137.5 9.5 %all-to-all-start.2 = ((bf16[32,1,64,488]{3,2,1,0:T(8,128)(2,1)}), bf16[32,1,64,488]{3,2,1,0:T(8,128)(2,1)S(1)}, u32[]{:S(2)}, u32[]{:S(2)}) async-start(bf16[32,1,64,488]{3,2,1,0:T(8,128)(2,1)} %fusion.2), calls=%async_computation.2 | async-start | bytes 4194304 | tf_op jit(solution)/shard_map/all_to_all | solution.py:268
  147.0 3.0 gather_fusion
  150.0 4.6 fusion
  154.6 4.8 copy.470
  160.7 35.0 %all-to-all-done.2 = bf16[32,1,64,488]{3,2,1,0:T(8,128)(2,1)S(1)} async-done(((bf16[32,1,64,488]{3,2,1,0:T(8,128)(2,1)}), bf16[32,1,64,488]{3,2,1,0:T(8,128)(2,1)S(1)}, u32[]{:S(2)}, u32[]{:S(2)}) %all-to-all-start.2) | async-done | bytes 1998880 | tf_op jit(solution)/shard_map/all_to_all | solution.py:268
  197.1 7.2 %all-to-all-start.1 = ((bf16[32,1,64,512]{3,2,1,0:T(8,128)(2,1)}), bf16[32,1,64,512]{3,2,1,0:T(8,128)(2,1)S(1)}, u32[]{:S(2)}, u32[]{:S(2)}) async-start(bf16[32,1,64,512]{3,2,1,0:T(8,128)(2,1)} %copy.470), calls=%async_computation.1 | async-start | bytes 4194304 | tf_op jit(solution)/shard_map/all_to_all | solution.py:267
  207.4 2.2 reshape.4935
  210.7 2.1 gather_fusion.3
  215.4 37.6 %all-to-all-done.1 = bf16[32,1,64,512]{3,2,1,0:T(8,128)(2,1)S(1)} async-done(((bf16[32,1,64,512]{3,2,1,0:T(8,128)(2,1)}), bf16[32,1,64,512]{3,2,1,0:T(8,128)(2,1)S(1)}, u32[]{:S(2)}, u32[]{:S(2)}) %all-to-all-start.1) | async-done | bytes 2097184 | tf_op jit(solution)/shard_map/all_to_all | solution.py:267
  260.5 2.1 fusion.66
  262.6 1.8 copy.551
  264.4 1.8 copy.550
  273.0 1.7 copy.545
  279.3 1.7 copy.568
  281.0 1.7 copy.567
  284.5 1.7 copy.565
  287.9 1.7 copy.563
  319.9 3.2 fusion.3
  326.5 9.4 %all-to-all-start.3 = ((bf16[16,2,4096]{2,1,0:T(2,128)(2,1)}), bf16[16,2,4096]{2,1,0:T(2,128)(2,1)S(1)}, u32[]{:S(2)}, u32[]{:S(2)}) async-start(bf16[16,2,4096]{2,1,0:T(2,128)(2,1)} %reshape.4932), calls=%async_computation.3 | async-start | bytes 524288 | tf_op jit(solution)/shard_map/all_to_all | solution.py:190
  336.6 4.0 fusion.10
  340.6 97.8 %psum.15 = f32[128]{0:T(128)} all-reduce(f32[128]{0:T(128)S(1)} %get-tuple-element.1146), channel_id=1, replica_groups=mesh['region'=16,'block'=32] {'region','block'}, use_global_device_ids=true, to_apply=%region_10.20 | all-reduce | flops 128 | bytes 1024 | tf_op jit(solution)/shard_map/psum | solution.py:300
  440.4 171.9 %all-reduce.3.cloned.1.call-done = f32[27,64,128]{2,1,0:T(8,128)} async-done(((f32[27,64,128]{2,1,0:T(8,128)}), f32[27,64,128]{2,1,0:T(8,128)}) %all-reduce.3.cloned.1.call-update) | async-done | bytes 884752 | tf_op jit(solution)/shard_map/psum | solution.py:300
  612.3 2.2 copy.660
  (455 shorter events, 142.4 us)
Async XLA Ops:
  7.2 312.7 %copy-start = (bf16[27,64,128]{2,1,0:T(8,128)(2,1)S(1)}, bf16[27,64,128]{2,1,0:T(8,128)(2,1)}, u32[]{:S(2)}) copy-start(bf16[27,64,128]{2,1,0:T(8,128)(2,1)} %param.139) | copy-start | bytes 1327108
  7.2 31.2 %copy-start.2 = (s32[4,26]{1,0:T(4,128)S(1)}, s32[4,26]{1,0:T(4,128)}, u32[]{:S(2)}) copy-start(s32[4,26]{1,0:T(4,128)} %param.137) | copy-start | bytes 1252
  10.0 71.9 %copy-start.1 = (bf16[2,8192]{1,0:T(2,128)(2,1)S(1)}, bf16[2,8192]{1,0:T(2,128)(2,1)}, u32[]{:S(2)}) copy-start(bf16[2,8192]{1,0:T(2,128)(2,1)} %param.141) | copy-start | bytes 98308
  11.6 77.9 %collective-permute-start.1 = (bf16[4,2,4096]{2,0,1:T(4,128)(2,1)S(1)}, bf16[4,2,4096]{2,0,1:T(4,128)(2,1)S(1)}, u32[]{:S(2)}, u32[]{:S(2)}) collective-permute-start(bf16[4,2,4096]{2,0,1:T(4,128)(2,1)S(1)} %constant_dynamic-update-slice_fusion), channel_id=1, source_target_pairs={{1,0},{2,1},{3,2},{4,3},{5,4},{6,5},{7,6},{8,7},{9,8},{10,9},{11,1... | collective-permute-start | bytes 196616 | tf_op jit(solution)/shard_map/ppermute | solution.py:17
  12.9 76.6 %collective-permute-start = (bf16[4,2,4096]{2,0,1:T(4,128)(2,1)S(1)}, bf16[4,2,4096]{2,0,1:T(4,128)(2,1)S(1)}, u32[]{:S(2)}, u32[]{:S(2)}) collective-permute-start(bf16[4,2,4096]{2,0,1:T(4,128)(2,1)S(1)} %constant_dynamic-update-slice_fusion), channel_id=1, source_target_pairs={{0,1},{1,2},{2,3},{3,4},{4,5},{5,6},{6,7},{7,8},{8,9},{9,10},{10,1... | collective-permute-start | bytes 196616 | tf_op jit(solution)/shard_map/ppermute | solution.py:16
  17.9 29.1 %copy-start.24 = (pred[32]{0:T(512)(128)(4,1)}, pred[32]{0:T(512)(128)(4,1)S(1)}, u32[]{:S(2)}) copy-start(pred[32]{0:T(512)(128)(4,1)S(1)} %fusion.39) | copy-start | bytes 100
  28.1 30.6 %all-to-all-start = ((s32[32,1,3]{2,1,0:T(1,128)}), s32[32,1,3]{2,1,0:T(1,128)S(1)}, u32[]{:S(2)}, u32[]{:S(2)}) async-start(s32[32,1,3]{2,1,0:T(1,128)} %copy.466), calls=%async_computation | async-start | bytes 32768 | tf_op jit(solution)/shard_map/all_to_all | solution.py:269
  60.8 20.2 %copy-start.47 = (s32[2]{0:T(128)}, s32[2]{0:T(128)S(1)}, u32[]{:S(2)}) copy-start(s32[2]{0:T(128)S(1)} %get-tuple-element.1045) | copy-start | bytes 28
  62.2 18.8 %all-to-all-start.4 = ((s32[16,1,1]{2,1,0:T(1,128)}), s32[16,1,1]{2,1,0:T(1,128)S(1)}, u32[]{:S(2)}, u32[]{:S(2)}) async-start(s32[16,1,1]{2,1,0:T(1,128)} %copy.468), calls=%async_computation.4 | async-start | bytes 16384 | tf_op jit(solution)/shard_map/all_to_all | solution.py:191
  84.9 52.6 %all-to-all-start.5 = ((bf16[16,2,4096]{2,1,0:T(2,128)(2,1)}), bf16[16,2,4096]{2,1,0:T(2,128)(2,1)}, u32[]{:S(2)}, u32[]{:S(2)}) async-start(bf16[16,2,4096]{2,1,0:T(2,128)(2,1)} %reshape.4934), calls=%async_computation.5 | async-start | bytes 524288 | tf_op jit(solution)/shard_map/all_to_all | solution.py:199
  137.5 58.3 %all-to-all-start.2 = ((bf16[32,1,64,488]{3,2,1,0:T(8,128)(2,1)}), bf16[32,1,64,488]{3,2,1,0:T(8,128)(2,1)S(1)}, u32[]{:S(2)}, u32[]{:S(2)}) async-start(bf16[32,1,64,488]{3,2,1,0:T(8,128)(2,1)} %fusion.2), calls=%async_computation.2 | async-start | bytes 4194304 | tf_op jit(solution)/shard_map/all_to_all | solution.py:268
  159.4 44.9 %copy-start.36 = (s32[16]{0:T(128)S(1)}, s32[16]{0:T(128)}, u32[]{:S(2)}) copy-start(s32[16]{0:T(128)} %get-tuple-element.1128) | copy-start | bytes 196
  159.4 45.5 %copy-start.44 = (s32[16]{0:T(128)S(1)}, s32[16]{0:T(128)}, u32[]{:S(2)}) copy-start(s32[16]{0:T(128)} %copy-done.43) | copy-start | bytes 196
  159.4 46.0 %copy-start.26 = (pred[2]{0:T(512)(128)(4,1)S(1)}, pred[2]{0:T(512)(128)(4,1)}, u32[]{:S(2)}) copy-start(pred[2]{0:T(512)(128)(4,1)} %get-tuple-element.1049) | copy-start | bytes 10
  159.4 46.7 %copy-start.38 = (s32[16]{0:T(128)S(1)}, s32[16]{0:T(128)}, u32[]{:S(2)}) copy-start(s32[16]{0:T(128)} %copy-done.37) | copy-start | bytes 196
  159.4 51.0 %copy-start.29 = (pred[2]{0:T(512)(128)(4,1)S(1)}, pred[2]{0:T(512)(128)(4,1)}, u32[]{:S(2)}) copy-start(pred[2]{0:T(512)(128)(4,1)} %get-tuple-element.1044) | copy-start | bytes 10
  197.1 55.9 %all-to-all-start.1 = ((bf16[32,1,64,512]{3,2,1,0:T(8,128)(2,1)}), bf16[32,1,64,512]{3,2,1,0:T(8,128)(2,1)S(1)}, u32[]{:S(2)}, u32[]{:S(2)}) async-start(bf16[32,1,64,512]{3,2,1,0:T(8,128)(2,1)} %copy.470), calls=%async_computation.1 | async-start | bytes 4194304 | tf_op jit(solution)/shard_map/all_to_all | solution.py:267
  262.6 27.0 %copy-start.6 = (bf16[2,64,8,8,8]{1,4,3,2,0:T(8,128)(2,1)S(1)}, bf16[2,64,8,8,8]{1,4,3,2,0:T(8,128)(2,1)}, u32[]{:S(2)}) copy-start(bf16[2,64,8,8,8]{1,4,3,2,0:T(8,128)(2,1)} %get-tuple-element.1060) | copy-start | bytes 393220
  262.6 27.8 %copy-start.5 = (bf16[2,64,8,8,8]{1,4,3,2,0:T(8,128)(2,1)S(1)}, bf16[2,64,8,8,8]{1,4,3,2,0:T(8,128)(2,1)}, u32[]{:S(2)}) copy-start(bf16[2,64,8,8,8]{1,4,3,2,0:T(8,128)(2,1)} %get-tuple-element.1061) | copy-start | bytes 393220
  264.4 26.8 %copy-start.4 = (bf16[2,64,8,8,8]{1,4,3,2,0:T(8,128)(2,1)S(1)}, bf16[2,64,8,8,8]{1,4,3,2,0:T(8,128)(2,1)}, u32[]{:S(2)}) copy-start(bf16[2,64,8,8,8]{1,4,3,2,0:T(8,128)(2,1)} %get-tuple-element.1062) | copy-start | bytes 393220
  292.8 21.1 %copy-start.15 = (bf16[2,64,512]{2,1,0:T(8,128)(2,1)S(1)}, bf16[2,64,512]{2,1,0:T(8,128)(2,1)}, u32[]{:S(2)}) copy-start(bf16[2,64,512]{2,1,0:T(8,128)(2,1)} %copy.562) | copy-start | bytes 393220
  293.6 21.0 %copy-start.13 = (bf16[2,64,512]{2,1,0:T(8,128)(2,1)S(1)}, bf16[2,64,512]{2,1,0:T(8,128)(2,1)}, u32[]{:S(2)}) copy-start(bf16[2,64,512]{2,1,0:T(8,128)(2,1)} %copy.563) | copy-start | bytes 393220
  294.3 20.9 %copy-start.12 = (bf16[2,64,512]{2,1,0:T(8,128)(2,1)S(1)}, bf16[2,64,512]{2,1,0:T(8,128)(2,1)}, u32[]{:S(2)}) copy-start(bf16[2,64,512]{2,1,0:T(8,128)(2,1)} %copy.564) | copy-start | bytes 393220
  294.3 21.6 %copy-start.11 = (bf16[2,64,512]{2,1,0:T(8,128)(2,1)S(1)}, bf16[2,64,512]{2,1,0:T(8,128)(2,1)}, u32[]{:S(2)}) copy-start(bf16[2,64,512]{2,1,0:T(8,128)(2,1)} %copy.565) | copy-start | bytes 393220
  295.1 21.4 %copy-start.10 = (bf16[2,64,512]{2,1,0:T(8,128)(2,1)S(1)}, bf16[2,64,512]{2,1,0:T(8,128)(2,1)}, u32[]{:S(2)}) copy-start(bf16[2,64,512]{2,1,0:T(8,128)(2,1)} %copy.566) | copy-start | bytes 393220
  295.9 21.3 %copy-start.9 = (bf16[2,64,512]{2,1,0:T(8,128)(2,1)S(1)}, bf16[2,64,512]{2,1,0:T(8,128)(2,1)}, u32[]{:S(2)}) copy-start(bf16[2,64,512]{2,1,0:T(8,128)(2,1)} %copy.567) | copy-start | bytes 393220
  295.9 22.0 %copy-start.8 = (bf16[2,64,512]{2,1,0:T(8,128)(2,1)S(1)}, bf16[2,64,512]{2,1,0:T(8,128)(2,1)}, u32[]{:S(2)}) copy-start(bf16[2,64,512]{2,1,0:T(8,128)(2,1)} %copy.568) | copy-start | bytes 393220
  296.0 22.5 %copy-start.7 = (bf16[2,64,512]{2,1,0:T(8,128)(2,1)S(1)}, bf16[2,64,512]{2,1,0:T(8,128)(2,1)}, u32[]{:S(2)}) copy-start(bf16[2,64,512]{2,1,0:T(8,128)(2,1)} %copy.569) | copy-start | bytes 393220
  296.2 23.7 %copy-start.27 = (f32[128]{0:T(128)S(1)}, f32[128]{0:T(128)}, u32[]{:S(2)}) copy-start(f32[128]{0:T(128)} %param.140) | copy-start | bytes 1540
  326.5 111.8 %all-to-all-start.3 = ((bf16[16,2,4096]{2,1,0:T(2,128)(2,1)}), bf16[16,2,4096]{2,1,0:T(2,128)(2,1)S(1)}, u32[]{:S(2)}, u32[]{:S(2)}) async-start(bf16[16,2,4096]{2,1,0:T(2,128)(2,1)} %reshape.4932), calls=%async_computation.3 | async-start | bytes 524288 | tf_op jit(solution)/shard_map/all_to_all | solution.py:190
  336.0 276.3 %all-reduce.3.cloned.1.call-start = ((), (), s32[]{:S(2)}) async-start(), calls=%async_computation.6 | async-start | bytes 1769472 | tf_op jit(solution)/shard_map/psum | solution.py:300
  336.6 103.1 %copy-start.41 = (pred[2]{0:T(512)(128)(4,1)S(1)}, pred[2]{0:T(512)(128)(4,1)}, u32[]{:S(2)}) copy-start(pred[2]{0:T(512)(128)(4,1)} %compare_and_fusion.2) | copy-start | bytes 10
  (27 other events, 250.9 us)
Sparse Core Ops, SparseCore 0:
  342.4 269.8 all-reduce.2
where the time goes:
time: 624 us; the launch traced here: 621 us
  waiting for transfers between devices  250 us (40%)
  local copies, waits for them, and re-layouts  139 us (22%)
  blocking collectives  97.8 us (16%)
  starting transfers between devices  58.4 us (9%)
  other arithmetic  52.3 us (8%)
  between operations  15.4 us (2%)
  matrix products  8.32 us (1%)
    psum x1, waiting for transfers between devices, per_device(): lax.psum((weight_grad, bias_grad), ('region', 'block'))  172 us
    psum x1, blocking collectives, per_device(): lax.psum((weight_grad, bias_grad), ('region', 'block'))  97.8 us
    unnamed x140, local copies, waits for them, and re-layouts  38.3 us
    all_to_all x1, waiting for transfers between devices, per_device(): lax.all_to_all(send_blocks, 'block', split_axis=0, concat_axis=0, tiled=T...  37.6 us
    all_to_all x1, waiting for transfers between devices, per_device(): lax.all_to_all(send_shells, 'block', split_axis=0, concat_axis=0, tiled=T...  35 us
    reshape x27, local copies, waits for them, and re-layouts, taps(): pieces.append(window.reshape(rows_now, channels, 512))  32.9 us
    gather x26, local copies, waits for them, and re-layouts, per_device(): piece = jnp.take(source_all, lookup, axis=0)  16.4 us
    select_n x26, other arithmetic, per_device(): jnp.where((target >= 0)[:, None, None], piece, jnp.zeros_like(piece))  13.6 us
  transfers between devices with their start and end apart: 9, of which 4 were waited for; matrix products, arithmetic and copies ran while one was open for 19% of the time, Pallas kernels for 0%

commit v1 on v0

v1 whole, which is shorter than its diff:
```python
import functools

import jax
import jax.numpy as jnp
from jax import lax
from jax.experimental import pallas as pl
from jax.experimental.pallas import tpu as pltpu
from jax.sharding import PartitionSpec as P

SLOTS = 4
CH = 64
OUT = 128
VOX = 512
FRAME = 768
EDGES = ((-1, -1), (-1, 0), (-1, 1), (0, -1), (0, 0), (0, 1), (1, -1), (1, 0), (1, 1))


def voxel_mask(count):
    lanes = lax.broadcasted_iota(jnp.int32, (1, VOX), 1)
    return ((lanes * 167) & 511) < count


def layer_pair(block):
    lanes = lax.broadcasted_iota(jnp.int32, (CH, 128), 1)
    return jnp.where(lanes < 64, block[:, :128], block[:, VOX - 128 :])


def layers_kernel(counts_ref, features_ref, layers_ref):
    for slot in range(SLOTS):
        block = features_ref[slot].astype(jnp.float32)
        block = jnp.where(voxel_mask(counts_ref[slot]), block, 0.0)
        layers_ref[slot] = layer_pair(block).astype(jnp.bfloat16)


def column_of(ea, eb, ec):
    tap = 9 * (ea + 1) + 3 * (eb + 1) + (ec + 1)
    return tap if tap < 13 else tap - 1


def pool_table(rows_are_voxels):
    shape = (VOX, 64) if rows_are_voxels else (64, VOX)
    voxel = lax.broadcasted_iota(jnp.int32, shape, 0 if rows_are_voxels else 1)
    cell = lax.broadcasted_iota(jnp.int32, shape, 1 if rows_are_voxels else 0)
    index = ((voxel >> 7) << 4) | (((voxel >> 4) & 3) << 2) | ((voxel & 7) >> 1)
    return jnp.where(index == cell, 0.125, 0.0).astype(jnp.bfloat16)


def pick_rows(odd, transposed):
    shape = (OUT, 64) if transposed else (64, OUT)
    channel = lax.broadcasted_iota(jnp.int32, shape, 0 if transposed else 1)
    row = lax.broadcasted_iota(jnp.int32, shape, 1 if transposed else 0)
    return jnp.where(channel == 2 * row + odd, 1.0, 0.0).astype(jnp.bfloat16)


def dot(a, b):
    return jnp.dot(a, b, preferred_element_type=jnp.float32)


def forward_kernel(
    counts_ref,
    neighbors_ref,
    features_ref,
    layers_ref,
    before_ref,
    after_ref,
    weight_ref,
    bias_ref,
    pooled_ref,
    stacked_ref,
    slope_ref,
    blocks_ref,
    rims_ref,
):
    slot = pl.program_id(0)
    first = (lax.axis_index("region") * lax.axis_size("block") + lax.axis_index("block")) * SLOTS

    @pl.when(slot == 0)
    def _():
        for index in range(SLOTS):
            block = features_ref[index].astype(jnp.float32)
            blocks_ref[index] = jnp.where(voxel_mask(counts_ref[index]), block, 0.0)
            rims_ref[index] = before_ref[index].astype(jnp.float32)
            rims_ref[SLOTS + index] = layers_ref[index].astype(jnp.float32)
            rims_ref[2 * SLOTS + index] = after_ref[index].astype(jnp.float32)
        blocks_ref[SLOTS] = jnp.zeros((CH, VOX), jnp.float32)
        rims_ref[3 * SLOTS] = jnp.zeros((CH, 128), jnp.float32)

    def rim(ea, eb, ec):
        target = neighbors_ref[slot, column_of(ea, eb, ec)]
        place = jnp.clip(target - (first - SLOTS), 0, 3 * SLOTS - 1)
        return rims_ref[jnp.where(target >= 0, place, 3 * SLOTS)]

    def inner(eb, ec):
        if eb == 0 and ec == 0:
            return blocks_ref[slot]
        target = neighbors_ref[slot, column_of(0, eb, ec)]
        place = jnp.clip(target - first, 0, SLOTS - 1)
        return blocks_ref[jnp.where(target >= 0, place, SLOTS)]

    def frame(eb, ec):
        return jnp.concatenate([rim(-1, eb, ec), inner(eb, ec), rim(1, eb, ec)], axis=1)

    lanes = lax.broadcasted_iota(jnp.int32, (CH, FRAME), 1)
    at_c = lanes & 7
    at_b = (lanes >> 3) & 7

    def moved(array, steps):
        return pltpu.roll(array, (-steps) % FRAME, 1)

    along_c = {}
    for eb in (-1, 0, 1):
        middle = frame(eb, 0)
        along_c[eb, 0] = middle
        along_c[eb, -1] = jnp.where(at_c == 0, moved(frame(eb, -1), 7), moved(middle, -1))
        along_c[eb, 1] = jnp.where(at_c == 7, moved(frame(eb, 1), -7), moved(middle, 1))
    for index, (eb, ec) in enumerate(EDGES):
        if eb == 0:
            value = along_c[0, ec]
        elif eb < 0:
            value = jnp.where(at_b == 0, moved(along_c[-1, ec], 56), moved(along_c[0, ec], -8))
        else:
            value = jnp.where(at_b == 7, moved(along_c[1, ec], -56), moved(along_c[0, ec], 8))
        stacked_ref[0, index * CH : (index + 1) * CH, :] = value.astype(jnp.bfloat16)

    product = dot(weight_ref[...], stacked_ref[0])
    sides = product[:OUT, : FRAME - 128] + product[2 * OUT :, 128:]
    sides = pltpu.roll(sides, FRAME - 128 - 64, 1)[:, :VOX]
    preact = product[OUT : 2 * OUT, 128 : 128 + VOX] + sides + bias_ref[...]
    mask = voxel_mask(counts_ref[slot])
    sigmoid = jax.nn.sigmoid(preact)
    slope = sigmoid * (1.0 + preact * (1.0 - sigmoid))
    slope_ref[0] = jnp.where(mask, slope, 0.0)
    activation = jnp.where(mask, preact * sigmoid, 0.0)
    high = activation.astype(jnp.bfloat16)
    low = (activation - high.astype(jnp.float32)).astype(jnp.bfloat16)
    table = pool_table(True)
    pooled = (dot(high, table) + dot(low, table)).astype(jnp.bfloat16)
    even = dot(pick_rows(0, False), pooled)
    odd = dot(pick_rows(1, False), pooled)
    pooled_ref[0] = jnp.concatenate([even, odd], axis=1).astype(jnp.bfloat16)


def backward_kernel(rows_ref, filled_ref, row_ref, stacked_ref, slope_ref, weight_grad_ref, bias_grad_ref):
    slot = pl.program_id(0)

    @pl.when(slot == 0)
    def _():
        weight_grad_ref[...] = jnp.zeros_like(weight_grad_ref)
        bias_grad_ref[...] = jnp.zeros_like(bias_grad_ref)

    @pl.when(filled_ref[slot] > 0)
    def _():
        row = row_ref[0]
        cells = dot(pick_rows(0, True), row[:, :64]) + dot(pick_rows(1, True), row[:, 64:])
        spread = dot(cells.astype(jnp.bfloat16), pool_table(False))
        grad = spread * slope_ref[0]
        bias_grad_ref[...] += jnp.sum(grad, axis=1, keepdims=True)
        grad = grad.astype(jnp.bfloat16).astype(jnp.float32)
        wide = jnp.concatenate([grad, jnp.zeros((OUT, 128), jnp.float32)], axis=1)
        shifted = pltpu.roll(wide, 64, 1).astype(jnp.bfloat16)
        grad = grad.astype(jnp.bfloat16)

        def outer(start, width, value):
            return lax.dot_general(
                stacked_ref[0, :, start : start + width],
                value,
                (((1,), (1,)), ((), ())),
                preferred_element_type=jnp.float32,
            )

        weight_grad_ref[0] += outer(0, FRAME - 128, shifted)
        weight_grad_ref[1] += outer(128, VOX, grad)
        weight_grad_ref[2] += outer(128, FRAME - 128, shifted)


VMEM = pltpu.VMEM


def make_layers(counts, features):
    return pl.pallas_call(
        layers_kernel,
        out_shape=jax.ShapeDtypeStruct((SLOTS, CH, 128), jnp.bfloat16),
        in_specs=[pl.BlockSpec(memory_space=pltpu.SMEM), pl.BlockSpec(memory_space=VMEM)],
        out_specs=pl.BlockSpec(memory_space=VMEM),
        name="layers",
    )(counts, features)


def forward(counts, neighbors, features, layers, before, after, weight, bias):
    def whole(shape):
        return pl.BlockSpec(shape, lambda i, *_: (0,) * len(shape))

    def per_slot(shape):
        return pl.BlockSpec((1,) + shape, lambda i, *_: (i, 0, 0))

    return pl.pallas_call(
        forward_kernel,
        grid_spec=pltpu.PrefetchScalarGridSpec(
            num_scalar_prefetch=2,
            grid=(SLOTS,),
            in_specs=[
                whole((SLOTS, CH, VOX)),
                whole((SLOTS, CH, 128)),
                whole((SLOTS, CH, 128)),
                whole((SLOTS, CH, 128)),
                whole((3 * OUT, 9 * CH)),
                whole((OUT, 1)),
            ],
            out_specs=[
                per_slot((CH, 128)),
                per_slot((9 * CH, FRAME)),
                per_slot((OUT, VOX)),
            ],
            scratch_shapes=[
                pltpu.VMEM((SLOTS + 1, CH, VOX), jnp.float32),
                pltpu.VMEM((3 * SLOTS + 1, CH, 128), jnp.float32),
            ],
        ),
        out_shape=[
            jax.ShapeDtypeStruct((SLOTS, CH, 128), jnp.bfloat16),
            jax.ShapeDtypeStruct((SLOTS, 9 * CH, FRAME), jnp.bfloat16),
            jax.ShapeDtypeStruct((SLOTS, OUT, VOX), jnp.float32),
        ],
        compiler_params=pltpu.CompilerParams(vmem_limit_bytes=32 * 1024 * 1024),
        cost_estimate=pl.CostEstimate(flops=3_500_000_000, bytes_accessed=6_000_000, transcendentals=300_000),
        name="forward",
    )(counts, neighbors, features, layers, before, after, weight, bias)


def backward(lines, filled, rows, stacked, slope):
    def per_slot(shape):
        return pl.BlockSpec((1,) + shape, lambda i, *_: (i, 0, 0))

    return pl.pallas_call(
        backward_kernel,
        grid_spec=pltpu.PrefetchScalarGridSpec(
            num_scalar_prefetch=2,
            grid=(SLOTS,),
            in_specs=[
                pl.BlockSpec((1, CH, 128), lambda i, lines_ref, filled_ref: (lines_ref[i], 0, 0)),
                per_slot((9 * CH, FRAME)),
                per_slot((OUT, VOX)),
            ],
            out_specs=[
                pl.BlockSpec((3, 9 * CH, OUT), lambda i, *_: (0, 0, 0)),
                pl.BlockSpec((OUT, 1), lambda i, *_: (0, 0)),
            ],
        ),
        out_shape=[
            jax.ShapeDtypeStruct((3, 9 * CH, OUT), jnp.float32),
            jax.ShapeDtypeStruct((OUT, 1), jnp.float32),
        ],
        compiler_params=pltpu.CompilerParams(vmem_limit_bytes=32 * 1024 * 1024),
        cost_estimate=pl.CostEstimate(flops=3_500_000_000, bytes_accessed=6_000_000, transcendentals=0),
        name="backward",
    )(lines, filled, rows, stacked, slope)


def per_device(
    features,
    counts,
    rebalance,
    neighbors,
    coarse_owner,
    conv_weight,
    convolution_bias_vector,
    merged_adjoint,
):
    block_count = lax.axis_size("block")
    region_count = lax.axis_size("region")
    me_block = lax.axis_index("block")
    group_rows = 2 * block_count
    occupied = rebalance >= 0
    line = jnp.where(occupied, rebalance % group_rows, 0)

    tags = jnp.where(occupied, line * region_count + coarse_owner, -1)
    all_tags = lax.all_gather(tags, "block", tiled=True)
    wanted = 2 * me_block + jnp.arange(2, dtype=jnp.int32)
    match = (all_tags[None, :] >= 0) & (all_tags[None, :] // region_count == wanted[:, None])
    owner = jnp.sum(jnp.where(match, all_tags[None, :] % region_count, 0), axis=1)

    adjoint = merged_adjoint.reshape(2, CH, 128)
    adjoint_region = lax.all_gather(adjoint, "region", tiled=True)
    work_cot = jnp.take(adjoint_region, owner * 2 + jnp.arange(2, dtype=jnp.int32), axis=0)
    group_cot = lax.all_gather(work_cot, "block", tiled=True)

    layers = make_layers(counts, features)
    up = [(i, i + 1) for i in range(block_count - 1)]
    down = [(i + 1, i) for i in range(block_count - 1)]
    before = lax.ppermute(layers, "block", up)
    after = lax.ppermute(layers, "block", down)

    weight = conv_weight.reshape(3, 9 * CH, OUT).transpose(0, 2, 1).reshape(3 * OUT, 9 * CH)
    pooled_rows, stacked, slope = forward(
        counts, neighbors, features, layers, before, after, weight, convolution_bias_vector[:, None]
    )

    placed = (line[None, :] == jnp.arange(group_rows, dtype=jnp.int32)[:, None]) & occupied[None, :]
    send = jnp.zeros((group_rows, CH, 128), jnp.bfloat16)
    for slot in range(SLOTS):
        send = jnp.where(placed[:, slot][:, None, None], pooled_rows[slot][None], send)
    work_pooled = lax.psum_scatter(send, "block", scatter_dimension=0, tiled=True)
    to_owner = owner[None, :] == jnp.arange(region_count, dtype=jnp.int32)[:, None]
    send = jnp.where(to_owner[:, :, None, None], work_pooled[None], jnp.zeros((), jnp.bfloat16))
    pooled = lax.psum_scatter(
        send.reshape(region_count * 2, CH, 128), "region", scatter_dimension=0, tiled=True
    )

    weight_grad, bias_grad = backward(line, occupied.astype(jnp.int32), group_cot, stacked, slope)
    weight_total, bias_total = lax.psum(
        (weight_grad.reshape(27, CH, OUT), bias_grad.reshape(OUT)), ("region", "block")
    )
    return pooled.reshape(2, CH * 128), weight_total, bias_total


def solution(mesh):
    in_specs = (
        P(("region", "block"), None, None),
        P(("region", "block")),
        P(("region", "block")),
        P(("region", "block"), None),
        P(("region", "block")),
        P(),
        P(),
        P(("region", "block"), None),
    )
    out_specs = (P(("region", "block"), None), P(), P())
    return jax.shard_map(
        per_device, mesh=mesh, in_specs=in_specs, out_specs=out_specs, check_vma=False
    )
```

time: 624 us -> 692 us (1.11)
  waiting for transfers between devices: 250 us -> 485 us
  local copies, waits for them, and re-layouts: 139 us -> 15.7 us
  starting transfers between devices: 58.4 us -> 5.48 us
  blocking collectives: 97.8 us -> 149 us
  other arithmetic: 52.3 us -> 5.53 us
  Pallas kernels: 0 us -> 16.1 us
  matrix products: 8.32 us -> 0 us
    reduce_scatter x0 -> x2, waiting for transfers between devices: none -> 172 us  [the longest x1 172 us: per_device(): lax.psum_scatter(send, 'block', scatter_dimension=0, tiled=True)]
    all_gather x0 -> x1, waiting for transfers between devices: none -> 82.8 us  [per_device(): group_cot = lax.all_gather(work_cot, 'block', tiled=True)]
    all_to_all x6 -> x0, waiting for transfers between devices: 78.1 us -> none  [the longest x1 37.6 us: per_device(): lax.all_to_all(send_blocks, 'block', split_axis=0, concat_axis=0, tiled=T...]
    psum x1, waiting for transfers between devices: 172 us -> 230 us  [per_device(): lax.psum((weight_grad.reshape(27, CH, OUT), bias_grad.reshape(OUT)), ('re...]
    all_to_all x6 -> x0, starting transfers between devices: 52.4 us -> none  [the longest x1 11.8 us: owners(): lax.all_to_all(slot_tags, 'region', split_axis=0, concat_axis=0, tiled=True)]
    reshape x48 -> x1, local copies, waits for them, and re-layouts: 43.1 us -> 1.26 us  [per_device(): conv_weight.reshape(3, 9 * CH, OUT).transpose(0, 2, 1)]
    all_gather x0 -> x1, blocking collectives: none -> 29.4 us  [per_device(): adjoint_region = lax.all_gather(adjoint, 'region', tiled=True)]
    gather x40 -> x1, local copies, waits for them, and re-layouts: 29 us -> 0.56 us  [per_device(): jnp.take(adjoint_region, owner * 2 + jnp.arange(2, dtype=jnp.int32), axis=0)]
  transfers between devices with their start and end apart: 9 -> 6, of which waited for: 4 -> 3; matrix products, arithmetic and copies ran while one was open for 19% -> 1% of each run, Pallas kernels for 0% -> 1%
where the time goes in v1:
time: 692 us; the launch traced here: 691 us
  waiting for transfers between devices  485 us (70%)
  blocking collectives  149 us (22%)
  Pallas kernels  16.1 us (2%)
  local copies, waits for them, and re-layouts  15.7 us (2%)
  between operations  14.6 us (2%)
    psum x1, waiting for transfers between devices, per_device(): lax.psum((weight_grad.reshape(27, CH, OUT), bias_grad.reshape(OUT)), ('re...  230 us
    reduce_scatter x1, waiting for transfers between devices, per_device(): lax.psum_scatter(send, 'block', scatter_dimension=0, tiled=True)  172 us
    psum x1, blocking collectives, per_device(): lax.psum((weight_grad.reshape(27, CH, OUT), bias_grad.reshape(OUT)), ('re...  101 us
    all_gather x1, waiting for transfers between devices, per_device(): group_cot = lax.all_gather(work_cot, 'block', tiled=True)  82.8 us
    all_gather x1, blocking collectives, per_device(): adjoint_region = lax.all_gather(adjoint, 'region', tiled=True)  29.4 us
    unnamed x1, blocking collectives  18.6 us
  transfers between devices with their start and end apart: 6, of which 3 were waited for; matrix products, arithmetic and copies ran while one was open for 1% of the time, Pallas kernels for 1%

profile of v1, /device:TPU:1, one launch (start us, length us, event | category | flops | bytes accessed | tf_op | source)
XLA Modules:
  0.0 691.3 jit_solution(4852549978399277904)
XLA Ops:
  7.2 1.6 layers.1.layers_ref
  8.8 4.0 collective-permute-start
  12.9 1.3 collective-permute-start.1
  14.2 0.7 fusion.5
  14.8 1.3 dynamic-slice
  16.8 0.8 select_dynamic-update-slice_fusion
  17.6 1.3 copy.17
  18.9 0.8 copy.18.bias_ref
  19.7 0.9 copy-done
  20.6 0.8 copy-done.1
  21.5 0.7 copy-done.2
  22.1 0.7 copy-done.4
  22.8 8.3 %forward.1 = (bf16[4,64,128]{2,1,0:T(8,128)(2,1)S(1)}, bf16[4,576,768]{2,1,0:T(8,128)(2,1)S(1)}, f32[4,128,512]{2,1,0:T(8,128)S(1)}) custom-call(s32[4]{0:T(128)S(1)} %copy-done.2, s32[4,26]{1,0:T(4,128)S(1)} %copy-done.4, bf16[4,64,512]{2,1,0:T(8,128)(2,1)S(1)} %copy-done, bf16[4,64,128]{2,1,0:T(8,128)(2,1)S(1)} %copy-done.1, ...), custom_call_target="tpu_custom_call" | custom-call | flops 3500000000 | bytes 6000000 | tf_op jit(solution)/shard_map/forward/pallas_call | solution.py:196
  31.2 1.7 copy-done.5
  32.9 1.3 select_select_fusion
  34.3 18.6 %all-reduce = s32[128]{0:T(128)S(1)} all-reduce(s32[128]{0:T(128)S(1)} %get-tuple-element.13), channel_id=1, replica_groups=mesh['region'=16,'block'=32] {'block'}, use_global_device_ids=true, to_apply=%add | all-reduce | flops 128 | bytes 1024
  52.9 0.2 fusion.1
  53.1 29.4 %all_gather.10 = bf16[32,64,128]{2,1,0:T(8,128)(2,1)S(1)} all-gather(bf16[2,64,128]{2,1,0:T(8,128)(2,1)S(1)} %bitcast.43), channel_id=1, replica_groups=mesh['region'=16,'block'=32] {'region'}, dimensions={0}, use_global_device_ids=true | all-gather | bytes 557056 | tf_op jit(solution)/shard_map/all_gather | solution.py:283
  82.5 0.6 gather_fusion
  83.1 0.7 broadcast_select_fusion
  84.0 0.1 eq.57
  84.1 172.1 %reduce-scatter.3.cloned.1.call-done = bf16[2,64,128]{2,1,0:T(8,128)(2,1)} async-done(((bf16[64,64,128]{2,1,0:T(8,128)(2,1)}), bf16[2,64,128]{2,1,0:T(8,128)(2,1)}) %reduce-scatter.3.cloned.1.call-update) | async-done | bytes 32784 | tf_op jit(solution)/shard_map/reduce_scatter | solution.py:302
  256.1 1.7 bitcast_select_fusion
  257.9 82.8 %all-gather.2.cloned.1.call-done.row_ref = bf16[64,64,128]{2,1,0:T(8,128)(2,1)} async-done(((bf16[2,64,128]{2,1,0:T(8,128)(2,1)}), bf16[64,64,128]{2,1,0:T(8,128)(2,1)}) %all-gather.2.cloned.1.call-update) | async-done | bytes 1048592 | tf_op jit(solution)/shard_map/all_gather | solution.py:285
  340.6 1.2 copy-done.3
  341.9 2.0 copy-done.6
  343.9 6.2 backward.1
  350.1 0.1 reduce
  350.2 101.1 %psum.15 = f32[128]{0:T(128)} all-reduce(f32[128]{0:T(128)S(1)} %reduce), channel_id=1, replica_groups=mesh['region'=16,'block'=32] {'region','block'}, use_global_device_ids=true, to_apply=%region_4.5 | all-reduce | flops 128 | bytes 1024 | tf_op jit(solution)/shard_map/psum | solution.py:310
  451.3 1.4 copy.24
  452.7 229.9 %all-reduce.3.cloned.1.call-done = f32[27,64,128]{2,1,0:T(8,128)} async-done(((f32[27,64,128]{2,1,0:T(8,128)}), f32[27,64,128]{2,1,0:T(8,128)}) %all-reduce.3.cloned.1.call-update) | async-done | bytes 884752 | tf_op jit(solution)/shard_map/psum | solution.py:310
  682.6 2.2 copy.27
  (35 shorter events, 0.5 us)
Async XLA Ops:
  7.2 249.0 %reduce-scatter.3.cloned.1.call-start = ((), (), s32[]{:S(2)}) async-start(), calls=%async_computation.2 | async-start | bytes 1081344 | tf_op jit(solution)/shard_map/reduce_scatter | solution.py:302
  8.8 10.8 %collective-permute-start = (bf16[4,64,128]{2,1,0:T(8,128)(2,1)}, bf16[4,64,128]{2,1,0:T(8,128)(2,1)S(1)}, u32[]{:S(2)}, u32[]{:S(2)}) collective-permute-start(bf16[4,64,128]{2,1,0:T(8,128)(2,1)} %layers.1.layers_ref), channel_id=1, source_target_pairs={{0,1},{1,2},{2,3},{3,4},{4,5},{5,6},{6,7},{7,8},{8,9},{9,10},{10,1... | collective-permute-start | bytes 196616 | tf_op jit(solution)/shard_map/ppermute | solution.py:290
  12.9 6.8 collective-permute-start.1
  19.7 1.0 copy-start
  20.6 0.8 copy-start.1
  21.5 0.7 copy-start.2
  22.1 0.7 copy-start.4
  22.8 11.5 %copy-start.7 = (bf16[2,8192]{1,0:T(2,128)(2,1)S(1)}, bf16[2,8192]{1,0:T(2,128)(2,1)}, u32[]{:S(2)}) copy-start(bf16[2,8192]{1,0:T(2,128)(2,1)} %param.15) | copy-start | bytes 98308
  31.1 1.8 copy-start.5
  34.2 306.4 %all-gather.2.cloned.1.call-start = ((), (), s32[]{:S(2)}) async-start(), calls=%async_computation.4 | async-start | bytes 1081344 | tf_op jit(solution)/shard_map/all_gather | solution.py:285
  83.8 367.5 %reduce-scatter.5.cloned.1.call-start = ((), (), s32[]{:S(2)}) async-start(), calls=%async_computation.3 | async-start | bytes 557056 | tf_op jit(solution)/shard_map/reduce_scatter | solution.py:305
  257.8 424.8 %all-reduce.3.cloned.1.call-start = ((), (), s32[]{:S(2)}) async-start(), calls=%async_computation.5 | async-start | bytes 1769472 | tf_op jit(solution)/shard_map/psum | solution.py:310
  340.6 1.2 copy-start.3
  341.9 2.0 copy-start.6
Sparse Core Ops, SparseCore 0:
  34.4 221.7 reduce-scatter.2
  259.9 80.7 all-gather.1
  343.4 59.8 reduce-scatter.4
  409.5 273.0 all-reduce.2

commit v2 on v1

v2 whole, which is shorter than its diff:
```python
import jax
import jax.numpy as jnp
from jax import lax
from jax.experimental import pallas as pl
from jax.experimental.pallas import tpu as pltpu
from jax.sharding import Mesh
from jax.sharding import PartitionSpec as P

SLOTS = 4
CH = 64
OUT = 128
VOX = 512
FRAME = 768
TAP_ROWS = 1728
BLOCK = 32
CHIPS = 256
HALF = TAP_ROWS // 2
EXTRA = HALF - 3 * CHIPS
EDGES = ((-1, -1), (-1, 0), (-1, 1), (0, -1), (0, 0), (0, 1), (1, -1), (1, 0), (1, 1))
VMEM = pltpu.VMEM
SMEM = pltpu.SMEM


def voxel_mask(count):
    lanes = lax.broadcasted_iota(jnp.int32, (1, VOX), 1)
    return ((lanes * 167) & 511) < count


def layer_pair(block):
    lanes = lax.broadcasted_iota(jnp.int32, (CH, 128), 1)
    return jnp.where(lanes < 64, block[:, :128], block[:, VOX - 128 :])


def column_of(ea, eb, ec):
    tap = 9 * (ea + 1) + 3 * (eb + 1) + (ec + 1)
    return tap if tap < 13 else tap - 1


def dot(a, b):
    return jnp.dot(a, b, preferred_element_type=jnp.float32)


def dot_lanes(a, b):
    return lax.dot_general(a, b, (((1,), (1,)), ((), ())), preferred_element_type=jnp.float32)


def grid_of(shape):
    return lax.broadcasted_iota(jnp.int32, shape, 0), lax.broadcasted_iota(jnp.int32, shape, 1)


def onehot(shape, chosen):
    return jnp.where(chosen(*grid_of(shape)), 1.0, 0.0).astype(jnp.bfloat16)


def bf16(array):
    return array.astype(jnp.bfloat16)


def cell_table(slot, voxels_first):
    shape = (VOX, 256) if voxels_first else (256, VOX)
    rows, columns = grid_of(shape)
    voxel, column = (rows, columns) if voxels_first else (columns, rows)
    index = ((voxel >> 7) << 4) | (((voxel >> 4) & 3) << 2) | ((voxel & 7) >> 1)
    wanted = jnp.where(((column >> 5) & 3) == slot, ((column >> 7) << 5) | (column & 31), -1)
    return bf16(jnp.where(index == wanted, 0.125, 0.0))


def layers_kernel(counts_ref, features_ref, layers_ref):
    for slot in range(SLOTS):
        block = features_ref[slot].astype(jnp.float32)
        block = jnp.where(voxel_mask(counts_ref[slot]), block, 0.0)
        layers_ref[slot] = bf16(layer_pair(block))


def offer_kernel(line_ref, owner_ref, adjoint_ref, message_ref):
    message = jnp.zeros((2 * CHIPS, 128), jnp.float32)
    rows, lanes = grid_of((2 * CHIPS, 128))
    keep = (lanes >> 5) == ((rows >> 1) & 3)
    for s in range(2):
        spread = dot(
            onehot((2 * CHIPS, 64), lambda r, c: ((r >> 3) == c) & ((r & 1) == s)),
            adjoint_ref[s * 64 : (s + 1) * 64, :],
        )
        message += jnp.where(keep, spread, 0.0)
    folded = dot(bf16(message), onehot((128, 128), lambda r, c: ((r & 31) == c) & (c < 32)))
    tags = jnp.zeros((1, 128), jnp.float32)
    lane = lax.broadcasted_iota(jnp.int32, (1, 128), 1)
    for slot in range(SLOTS):
        tags = jnp.where(lane == 64 + slot, line_ref[slot].astype(jnp.float32), tags)
        tags = jnp.where(lane == 68 + slot, owner_ref[slot].astype(jnp.float32), tags)
    message_ref[...] = bf16(folded + tags)


def forward_kernel(
    counts_ref,
    neighbors_ref,
    features_ref,
    layers_ref,
    before_ref,
    after_ref,
    weight_ref,
    bias_ref,
    pooled_ref,
    stacked_ref,
    slope_ref,
    blocks_ref,
    rims_ref,
    cells_ref,
):
    slot = pl.program_id(0)
    first = ((lax.axis_index("z") * 2 + lax.axis_index("c")) * BLOCK + lax.axis_index("b")) * SLOTS

    @pl.when(slot == 0)
    def _():
        for index in range(SLOTS):
            block = features_ref[index].astype(jnp.float32)
            blocks_ref[index] = jnp.where(voxel_mask(counts_ref[index]), block, 0.0)
            rims_ref[index] = before_ref[index].astype(jnp.float32)
            rims_ref[SLOTS + index] = layers_ref[index].astype(jnp.float32)
            rims_ref[2 * SLOTS + index] = after_ref[index].astype(jnp.float32)
        blocks_ref[SLOTS] = jnp.zeros((CH, VOX), jnp.float32)
        rims_ref[3 * SLOTS] = jnp.zeros((CH, 128), jnp.float32)
        cells_ref[...] = jnp.zeros_like(cells_ref)

    def rim(ea, eb, ec):
        target = neighbors_ref[slot, column_of(ea, eb, ec)]
        place = jnp.clip(target - (first - SLOTS), 0, 3 * SLOTS - 1)
        return rims_ref[jnp.where(target >= 0, place, 3 * SLOTS)]

    def inner(eb, ec):
        if eb == 0 and ec == 0:
            return blocks_ref[slot]
        target = neighbors_ref[slot, column_of(0, eb, ec)]
        place = jnp.clip(target - first, 0, SLOTS - 1)
        return blocks_ref[jnp.where(target >= 0, place, SLOTS)]

    def frame(eb, ec):
        return jnp.concatenate([rim(-1, eb, ec), inner(eb, ec), rim(1, eb, ec)], axis=1)

    lanes = lax.broadcasted_iota(jnp.int32, (CH, FRAME), 1)
    at_c = lanes & 7
    at_b = (lanes >> 3) & 7

    def moved(array, steps):
        return pltpu.roll(array, (-steps) % FRAME, 1)

    along_c = {}
    for eb in (-1, 0, 1):
        middle = frame(eb, 0)
        along_c[eb, 0] = middle
        along_c[eb, -1] = jnp.where(at_c == 0, moved(frame(eb, -1), 7), moved(middle, -1))
        along_c[eb, 1] = jnp.where(at_c == 7, moved(frame(eb, 1), -7), moved(middle, 1))
    for index, (eb, ec) in enumerate(EDGES):
        if eb == 0:
            value = along_c[0, ec]
        elif eb < 0:
            value = jnp.where(at_b == 0, moved(along_c[-1, ec], 56), moved(along_c[0, ec], -8))
        else:
            value = jnp.where(at_b == 7, moved(along_c[1, ec], -56), moved(along_c[0, ec], 8))
        stacked_ref[0, index * CH : (index + 1) * CH, :] = value.astype(jnp.bfloat16)

    product = dot(weight_ref[...], stacked_ref[0])
    sides = product[:OUT, : FRAME - 128] + product[2 * OUT :, 128:]
    sides = pltpu.roll(sides, FRAME - 128 - 64, 1)[:, :VOX]
    preact = product[OUT : 2 * OUT, 128 : 128 + VOX] + sides + bias_ref[...]
    mask = voxel_mask(counts_ref[slot])
    sigmoid = jax.nn.sigmoid(preact)
    slope = sigmoid * (1.0 + preact * (1.0 - sigmoid))
    slope_ref[0] = jnp.where(mask, slope, 0.0)
    activation = jnp.where(mask, preact * sigmoid, 0.0)
    high = activation.astype(jnp.bfloat16)
    low = (activation - high.astype(jnp.float32)).astype(jnp.bfloat16)
    table = cell_table(slot, True)
    cells_ref[...] += dot(high, table) + dot(low, table)

    @pl.when(slot == SLOTS - 1)
    def _():
        cells = cells_ref[...].astype(jnp.bfloat16)
        even = onehot((CHIPS, OUT), lambda r, c: r == 2 * c)
        odd = onehot((CHIPS, OUT), lambda r, c: r == 2 * c + 1)
        pooled = dot(even, cells[:, :128]) + dot(odd, cells[:, 128:])
        pooled_ref[...] = pooled.astype(jnp.bfloat16)


def choose_kernel(offers_ref, pooled_ref, message_ref, tags_ref):
    core = lax.axis_index("c")
    even = onehot((CHIPS, 2 * CHIPS), lambda r, c: c == 2 * r)
    for half in range(2):
        tags = dot(even, offers_ref[half * 2 * CHIPS : (half + 1) * 2 * CHIPS, :])
        tags_ref[half * CHIPS : (half + 1) * CHIPS, :] = bf16(tags)
    tags = dot(even, offers_ref[pl.ds(core * 2 * CHIPS, 2 * CHIPS), :]).astype(jnp.int32)
    lanes = lax.broadcasted_iota(jnp.int32, (CHIPS, 4 * CHIPS), 1)
    cotangent = jnp.zeros((CHIPS, 128), jnp.float32)
    for slot in range(SLOTS):
        line = tags[:, 64 + slot : 65 + slot]
        owner = tags[:, 68 + slot : 69 + slot]
        source = ((owner & 1) * CHIPS + (owner >> 1) * BLOCK + ((line - 1) >> 1)) * 2 + ((line - 1) & 1)
        source = jnp.where(line > 0, source, -1)
        picked = dot(bf16(jnp.where(lanes == source, 1.0, 0.0)), offers_ref[...])
        cotangent += dot(bf16(picked), onehot((128, 128), lambda r, c: (r + 32 * slot == c) & (r < 32)))
    message = dot(onehot((2 * CHIPS, CHIPS), lambda r, c: r == 2 * c), bf16(cotangent))
    message += dot(onehot((2 * CHIPS, CHIPS), lambda r, c: r == 2 * c + 1), pooled_ref[...])
    message_ref[...] = bf16(message)


def backward_kernel(
    pieces_ref,
    stacked_ref,
    slope_ref,
    mine_ref,
    other_ref,
    pooled_ref,
    cells_ref,
    total_ref,
    bias_ref,
):
    slot = pl.program_id(0)

    @pl.when(slot == 0)
    def _():
        low = dot(onehot((OUT, 2 * CHIPS), lambda r, c: c == 4 * r), pieces_ref[...])
        high = dot(onehot((OUT, 2 * CHIPS), lambda r, c: c == 4 * r + 2), pieces_ref[...])
        cells_ref[...] = bf16(jnp.concatenate([low, high], axis=1))
        pooled = dot(onehot((CHIPS, 2 * CHIPS), lambda r, c: c == 2 * r + 1), pieces_ref[...])
        pooled_ref[...] = bf16(pooled)
        total_ref[...] = jnp.zeros_like(total_ref)
        bias_ref[...] = jnp.zeros_like(bias_ref)

    grad = dot(cells_ref[...], cell_table(slot, False)) * slope_ref[0]
    rounded = bf16(grad)
    ones = jnp.ones((8, VOX), jnp.bfloat16)
    rest = bf16(grad - rounded.astype(jnp.float32))
    bias_ref[...] += dot_lanes(ones, rounded) + dot_lanes(ones, rest)
    wide = jnp.concatenate([rounded.astype(jnp.float32), jnp.zeros((OUT, 128), jnp.float32)], axis=1)
    shifted = bf16(pltpu.roll(wide, 64, 1))
    total_ref[0:576] += dot_lanes(stacked_ref[0, :, 0 : FRAME - 128], shifted)
    total_ref[576:1152] += dot_lanes(stacked_ref[0, :, 128 : 128 + VOX], rounded)
    total_ref[1152:1728] += dot_lanes(stacked_ref[0, :, 128:], shifted)

    @pl.when(slot == SLOTS - 1)
    def _():
        core = lax.axis_index("c")
        mine_ref[:HALF] = total_ref[pl.ds(pl.multiple_of(core * HALF, 8), HALF), :]
        mine_ref[HALF:] = bias_ref[...]
        other_ref[:HALF] = total_ref[pl.ds(pl.multiple_of((1 - core) * HALF, 8), HALF), :]
        other_ref[HALF:] = bias_ref[...]


def share_kernel(mine_ref, got_ref, pooled_ref, tags_ref, message_ref):
    core = lax.axis_index("c")
    total = mine_ref[...] + got_ref[...]
    rounded = bf16(total)
    rows, lanes = grid_of((CHIPS, 128))
    piece = ((lanes >> 4) - (rows & 7)) & 7
    last = jnp.zeros((CHIPS, 128), jnp.float32)
    repeat = onehot((CHIPS, EXTRA // 3), lambda r, c: (r >> 3) == c)
    for t in range(3):
        start = 3 * CHIPS + t * (EXTRA // 3)
        last = jnp.where(piece == t, dot(repeat, rounded[start : start + EXTRA // 3]), last)

    bias = total[HALF : HALF + 1]
    high = bf16(bias).astype(jnp.float32)
    low = bf16(bias - high).astype(jnp.float32)
    value = jnp.where(lanes == (rows & 127), jnp.where(rows < 128, high, low), 0.0)
    last = jnp.where(piece == 7, jnp.sum(value, axis=1, keepdims=True), last)

    tags = tags_ref[...]
    columns = tags.astype(jnp.float32).astype(jnp.int32)
    by_lane = dot_lanes(onehot((8, 128), lambda r, c: c == r + 64), tags).astype(jnp.int32)
    chips = lax.broadcasted_iota(jnp.int32, (CHIPS, 2 * CHIPS), 0)
    parity = (lax.broadcasted_iota(jnp.int32, (2 * CHIPS, 128), 1) >> 5) & 1
    pooled = jnp.zeros((CHIPS, 128), jnp.float32)
    for slot in range(SLOTS):
        line, owner = by_lane[slot : slot + 1], by_lane[4 + slot : 5 + slot]
        chip = (owner >> 1) * BLOCK + ((line - 1) >> 1)
        chip = jnp.where((line > 0) & ((owner & 1) == core), chip, -1)
        copies = dot(
            pooled_ref[...], onehot((128, 128), lambda r, c: ((r >> 5) == slot) & ((r & 31) == (c & 31)))
        )
        copies = jnp.where(parity == ((columns[:, 64 + slot : 65 + slot] - 1) & 1), copies, 0.0)
        pooled += dot(bf16(jnp.where(chips == chip, 1.0, 0.0)), bf16(copies))
    last = bf16(jnp.where((piece >= 3) & (piece < 7), pooled, last))

    order = onehot((256, 256), lambda r, c: c == (r & 3) * 64 + (r >> 2))
    for quarter in range(4):
        at = 64 * quarter
        block = jnp.concatenate(
            [rounded[t * CHIPS + at : t * CHIPS + at + 64] for t in range(3)] + [last[at : at + 64]], axis=0
        )
        message_ref[256 * quarter : 256 * (quarter + 1), :] = bf16(dot(order, block))


def reduce_kernel(pieces_ref, message_ref, pooled_ref):
    chip = lax.axis_index("z") * BLOCK + lax.axis_index("b")
    pieces = pieces_ref[...]
    sums = dot(onehot((8, 4 * CHIPS), lambda r, c: (c & 3) == r), pieces)
    rows, lanes = grid_of((8, 128))
    piece = ((lanes >> 4) - chip) & 7
    high = bf16(sums).astype(jnp.float32)
    low = pltpu.roll(sums - high, 64, 1)
    last = jnp.where((piece < 3) | (piece == 7), high, jnp.where(piece == 3, low, 0.0))
    tile = bf16(jnp.where(rows < 3, high, last))
    message_ref[...] = bf16(dot(onehot((4 * CHIPS, 8), lambda r, c: (r & 3) == c), tile))

    pooled = dot(onehot((CHIPS, 4 * CHIPS), lambda r, c: c == 4 * r + 3), pieces)
    piece = ((lax.broadcasted_iota(jnp.int32, (CHIPS, 128), 1) >> 4) - chip) & 7
    pooled = jnp.where((piece >= 3) & (piece < 7), pooled, 0.0)
    pooled_ref[...] = bf16(pooled + pltpu.roll(pooled, 64, 1))


def finish_kernel(pieces_ref, weight_ref, bias_ref):
    order = onehot((256, 256), lambda r, c: r == (c & 3) * 64 + (c >> 2))
    rows, lanes = grid_of((CHIPS, 128))
    piece = ((lanes >> 4) - (rows & 7)) & 7
    gather = onehot((EXTRA // 3, CHIPS), lambda r, c: (c >> 3) == r)
    for half in range(2):
        last = []
        for quarter in range(4):
            start = half * 4 * CHIPS + 256 * quarter
            block = dot(order, pieces_ref[start : start + 256, :])
            for t in range(3):
                at = half * HALF + t * CHIPS + 64 * quarter
                weight_ref[at : at + 64, :] = block[64 * t : 64 * (t + 1)]
            last.append(block[192:])
        last = jnp.concatenate(last, axis=0)
        for t in range(3):
            at = half * HALF + 3 * CHIPS + t * (EXTRA // 3)
            weight_ref[at : at + EXTRA // 3, :] = dot(gather, bf16(jnp.where(piece == t, last, 0.0)))
        if half == 0:
            parts = jnp.where(((piece == 7) | (piece == 3)) & ((lanes & 15) == 0), last, 0.0)
            value = jnp.sum(parts, axis=1, keepdims=True)
            spread = jnp.where(lanes == (rows & 127), value, 0.0)
            bias_ref[...] = jnp.sum(spread, axis=0, keepdims=True)


def call(kernel, name, outs, operands, smem=0):
    return pl.pallas_call(
        kernel,
        out_shape=[jax.ShapeDtypeStruct(shape, dtype) for shape, dtype in outs],
        in_specs=[pl.BlockSpec(memory_space=SMEM if i < smem else VMEM) for i in range(len(operands))],
        out_specs=[pl.BlockSpec(memory_space=VMEM) for _ in outs],
        compiler_params=pltpu.CompilerParams(vmem_limit_bytes=32 * 1024 * 1024),
        name=name,
    )(*operands)


def forward(counts, neighbors, features, layers, before, after, weight, bias):
    def whole(shape):
        return pl.BlockSpec(shape, lambda i, *_: (0,) * len(shape))

    def per_slot(shape):
        return pl.BlockSpec((1,) + shape, lambda i, *_: (i, 0, 0))

    return pl.pallas_call(
        forward_kernel,
        grid_spec=pltpu.PrefetchScalarGridSpec(
            num_scalar_prefetch=2,
            grid=(SLOTS,),
            in_specs=[
                whole((SLOTS, CH, VOX)),
                whole((SLOTS, CH, 128)),
                whole((SLOTS, CH, 128)),
                whole((SLOTS, CH, 128)),
                whole((3 * OUT, 9 * CH)),
                whole((OUT, 1)),
            ],
            out_specs=[
                whole((CHIPS, 128)),
                per_slot((9 * CH, FRAME)),
                per_slot((OUT, VOX)),
            ],
            scratch_shapes=[
                pltpu.VMEM((SLOTS + 1, CH, VOX), jnp.float32),
                pltpu.VMEM((3 * SLOTS + 1, CH, 128), jnp.float32),
                pltpu.VMEM((OUT, 256), jnp.float32),
            ],
        ),
        out_shape=[
            jax.ShapeDtypeStruct((CHIPS, 128), jnp.bfloat16),
            jax.ShapeDtypeStruct((SLOTS, 9 * CH, FRAME), jnp.bfloat16),
            jax.ShapeDtypeStruct((SLOTS, OUT, VOX), jnp.float32),
        ],
        compiler_params=pltpu.CompilerParams(vmem_limit_bytes=32 * 1024 * 1024),
        cost_estimate=pl.CostEstimate(flops=3_500_000_000, bytes_accessed=6_000_000, transcendentals=300_000),
        name="forward",
    )(counts, neighbors, features, layers, before, after, weight, bias)


def backward(pieces, stacked, slope):
    def whole(shape):
        return pl.BlockSpec(shape, lambda i: (0,) * len(shape))

    def per_slot(shape):
        return pl.BlockSpec((1,) + shape, lambda i: (i, 0, 0))

    return pl.pallas_call(
        backward_kernel,
        grid=(SLOTS,),
        in_specs=[whole((2 * CHIPS, 128)), per_slot((9 * CH, FRAME)), per_slot((OUT, VOX))],
        out_specs=[whole((HALF + 8, OUT)), whole((HALF + 8, OUT)), whole((CHIPS, 128))],
        scratch_shapes=[
            pltpu.VMEM((OUT, 256), jnp.bfloat16),
            pltpu.VMEM((TAP_ROWS, OUT), jnp.float32),
            pltpu.VMEM((8, OUT), jnp.float32),
        ],
        out_shape=[
            jax.ShapeDtypeStruct((HALF + 8, OUT), jnp.float32),
            jax.ShapeDtypeStruct((HALF + 8, OUT), jnp.float32),
            jax.ShapeDtypeStruct((CHIPS, 128), jnp.bfloat16),
        ],
        compiler_params=pltpu.CompilerParams(vmem_limit_bytes=32 * 1024 * 1024),
        cost_estimate=pl.CostEstimate(flops=3_500_000_000, bytes_accessed=6_000_000, transcendentals=0),
        name="backward",
    )(pieces, stacked, slope)


def to_chips(message, rows):
    message = message.reshape(CHIPS, rows, 128)
    return lax.all_to_all(message, ("z", "b"), 0, 0, tiled=True)


def per_device(
    features,
    counts,
    rebalance,
    neighbors,
    coarse_owner,
    conv_weight,
    convolution_bias_vector,
    merged_adjoint,
):
    narrow, wide = jnp.bfloat16, jnp.float32
    occupied = rebalance >= 0
    line = jnp.where(occupied, rebalance % (2 * BLOCK) + 1, 0)
    owner = jnp.where(occupied, coarse_owner, 0)
    adjoint = merged_adjoint.reshape(128, 128)
    (offer,) = call(offer_kernel, "offer", [((2 * CHIPS, 128), narrow)], (line, owner, adjoint), smem=2)
    offers = to_chips(offer, 2)

    (layers,) = call(layers_kernel, "layers", [((SLOTS, CH, 128), narrow)], (counts, features), smem=1)
    up = [(i, i + 1) for i in range(BLOCK - 1)]
    down = [(i + 1, i) for i in range(BLOCK - 1)]
    before = lax.ppermute(layers, "b", up)
    after = lax.ppermute(layers, "b", down)
    weight = conv_weight.reshape(3, 9 * CH, OUT).transpose(0, 2, 1).reshape(3 * OUT, 9 * CH)
    pooled_pieces, stacked, slope = forward(
        counts, neighbors, features, layers, before, after, weight, convolution_bias_vector[:, None]
    )

    offers = lax.all_gather(offers, "c", tiled=True).reshape(4 * CHIPS, 128)
    message, tags = call(
        choose_kernel,
        "choose",
        [((2 * CHIPS, 128), narrow), ((2 * CHIPS, 128), narrow)],
        (offers, pooled_pieces),
    )
    pieces = to_chips(message, 2).reshape(2 * CHIPS, 128)
    mine, other, pooled_pieces = backward(pieces, stacked, slope)
    got = lax.ppermute(other, "c", [(0, 1), (1, 0)])
    pooled_pieces = lax.all_gather(pooled_pieces, "c", tiled=True)
    (message,) = call(
        share_kernel, "share", [((4 * CHIPS, 128), narrow)], (mine, got, pooled_pieces, tags)
    )
    pieces = to_chips(message, 4).reshape(4 * CHIPS, 128)
    message, pooled = call(
        reduce_kernel, "reduce", [((4 * CHIPS, 128), narrow), ((CHIPS, 128), narrow)], (pieces,)
    )
    pieces = to_chips(message, 4)
    pieces = lax.all_gather(pieces, "c", tiled=True).reshape(8 * CHIPS, 128)
    weight_total, bias_total = call(
        finish_kernel, "finish", [((TAP_ROWS, OUT), wide), ((1, OUT), wide)], (pieces,)
    )
    pooled = pooled[:, :64].reshape(CHIPS, 2, 32).transpose(1, 0, 2).reshape(2, CHIPS * 32)
    return pooled, weight_total.reshape(27, CH, OUT), bias_total.reshape(OUT)


def solution(mesh):
    chips = Mesh(mesh.devices.reshape(-1, 2, BLOCK), ("z", "c", "b"))
    whole = ("z", "c", "b")
    in_specs = (
        P(whole, None, None),
        P(whole),
        P(whole),
        P(whole, None),
        P(whole),
        P(),
        P(),
        P(whole, None),
    )
    out_specs = (P(whole, None), P(), P())
    return jax.shard_map(
        per_device, mesh=chips, in_specs=in_specs, out_specs=out_specs, check_vma=False
    )
```

time: 692 us -> 151 us (0.22)
  waiting for transfers between devices: 485 us -> 12.1 us
  blocking collectives: 149 us -> 64 us
  starting transfers between devices: 5.48 us -> 41.4 us
  between operations: 14.6 us -> 0.77 us
    psum x1 -> x0, waiting for transfers between devices: 230 us -> none  [per_device(): lax.psum((weight_grad.reshape(27, CH, OUT), bias_grad.reshape(OUT)), ('re...]
    reduce_scatter x2 -> x0, waiting for transfers between devices: 172 us -> none  [the longest x1 172 us: per_device(): lax.psum_scatter(send, 'block', scatter_dimension=0, tiled=True)]
    psum x1 -> x0, blocking collectives: 101 us -> none  [per_device(): lax.psum((weight_grad.reshape(27, CH, OUT), bias_grad.reshape(OUT)), ('re...]
    all_gather x1 -> x0, waiting for transfers between devices: 82.8 us -> none  [per_device(): group_cot = lax.all_gather(work_cot, 'block', tiled=True)]
    all_to_all x0 -> x2, blocking collectives: none -> 53.7 us  [to_chips(): return lax.all_to_all(message, ('z', 'b'), 0, 0, tiled=True)]
    all_to_all x0 -> x2, starting transfers between devices: none -> 31.7 us  [to_chips(): return lax.all_to_all(message, ('z', 'b'), 0, 0, tiled=True)]
    all_gather x1 -> x3, blocking collectives: 29.4 us -> 10.3 us  [the longest x1 5.23 us: per_device(): pieces = lax.all_gather(pieces, 'c', tiled=True).reshape(8 * CHIPS, 128)]
    unnamed x1 -> x0, blocking collectives: 18.6 us -> none
  transfers between devices with their start and end apart: 6 -> 5, of which waited for: 3 -> 1; matrix products, arithmetic and copies ran while one was open for 1% -> 3% of each run, Pallas kernels for 1% -> 6%
where the time goes in v2:
time: 151 us; the launch traced here: 150 us
  blocking collectives  64 us (42%)
  starting transfers between devices  41.4 us (27%)
  Pallas kernels  19.6 us (13%)
  waiting for transfers between devices  12.1 us (8%)
  local copies, waits for them, and re-layouts  11.5 us (8%)
    all_to_all x2, blocking collectives, to_chips(): return lax.all_to_all(message, ('z', 'b'), 0, 0, tiled=True)  53.7 us
    all_to_all x2, starting transfers between devices, to_chips(): return lax.all_to_all(message, ('z', 'b'), 0, 0, tiled=True)  31.7 us
    all_to_all x2, waiting for transfers between devices, to_chips(): return lax.all_to_all(message, ('z', 'b'), 0, 0, tiled=True)  12.1 us
    pallas_call x6, Pallas kernels, call(): pl.pallas_call(kernel, out_shape=[jax.ShapeDtypeStruct(shape, dtype) for...  8.14 us
    unnamed x14, local copies, waits for them, and re-layouts  7.64 us
    pallas_call x1, Pallas kernels, forward(): pl.pallas_call(forward_kernel, grid_spec=pltpu.PrefetchScalarGridSpec(num...  7.19 us
    all_gather x1, blocking collectives, per_device(): pieces = lax.all_gather(pieces, 'c', tiled=True).reshape(8 * CHIPS, 128)  5.23 us
    ppermute x1, starting transfers between devices, per_device(): before = lax.ppermute(layers, 'b', up)  4.66 us
  transfers between devices with their start and end apart: 5, of which 1 were waited for; matrix products, arithmetic and copies ran while one was open for 3% of the time, Pallas kernels for 6%

profile of v2, /device:TPU:1, one launch (start us, length us, event | category | flops | bytes accessed | tf_op | source)
XLA Modules:
  0.0 150.0 jit_solution(2742635601986343340)
XLA Ops:
  0.6 0.9 copy-done
  1.6 0.7 copy-done.2
  2.2 0.6 layers.1.layers_ref
  2.8 1.3 collective-permute-start.1
  4.1 4.7 %collective-permute-start = (bf16[4,64,128]{2,1,0:T(8,128)(2,1)S(1)}, bf16[4,64,128]{2,1,0:T(8,128)(2,1)S(1)}, u32[]{:S(2)}, u32[]{:S(2)}) collective-permute-start(bf16[4,64,128]{2,1,0:T(8,128)(2,1)S(1)} %layers.1.layers_ref), channel_id=1, source_target_pairs={{0,1},{1,2},{2,3},{3,4},{4,5},{5,6},{6,7},{7,8},{8,9},{9,10},{10,1... | collective-permute-start | bytes 196616 | tf_op jit(solution)/shard_map/ppermute | solution.py:443
  8.8 0.7 compare_select_fusion.2
  9.5 0.8 reshape.51.adjoint_ref
  10.3 1.6 %offer.1 = bf16[512,128]{1,0:T(8,128)(2,1)} custom-call(s32[4]{0:T(128)S(1)} %get-tuple-element.28.line_ref, s32[4]{0:T(128)S(1)} %get-tuple-element.27.owner_ref, bf16[128,128]{1,0:T(8,128)(2,1)S(1)} %reshape.51.adjoint_ref), custom_call_target="tpu_custom_call" | custom-call | tf_op jit(solution)/shard_map/offer/pallas_call | solution.py:337
  11.8 22.5 %all-to-all-start = ((bf16[256,2,128]{2,1,0:T(2,128)(2,1)}), bf16[256,2,128]{2,1,0:T(2,128)(2,1)S(1)}, u32[]{:S(2)}, u32[]{:S(2)}) async-start(bf16[256,2,128]{2,1,0:T(2,128)(2,1)} %bitcast), calls=%async_computation | async-start | bytes 262144 | tf_op jit(solution)/shard_map/all_to_all | solution.py:419
  34.4 0.8 copy.19.bias_ref
  35.1 1.3 copy.18
  36.4 0.9 copy-done.1
  37.4 0.7 copy-done.3
  38.0 0.7 copy-done.4
  38.7 7.2 %forward.1 = (bf16[256,128]{1,0:T(8,128)(2,1)S(1)}, bf16[4,576,768]{2,1,0:T(8,128)(2,1)S(1)}, f32[4,128,512]{2,1,0:T(8,128)S(1)}) custom-call(s32[4]{0:T(128)S(1)} %copy-done.3, s32[4,26]{1,0:T(4,128)S(1)} %copy-done.4, bf16[4,64,512]{2,1,0:T(8,128)(2,1)S(1)} %copy-done.1, bf16[4,64,128]{2,1,0:T(8,128)(2,1)S(1)} %layers.1.layers_ref, ...), custom_call_target="tpu_custom_call" | custom-call | flops 3500000000 | bytes 6000000 | tf_op jit(solution)/shard_map/forward/pallas_call | solution.py:354
  45.9 1.8 %copy-done.5 = bf16[4,576,768]{2,1,0:T(8,128)(2,1)} copy-done((bf16[4,576,768]{2,1,0:T(8,128)(2,1)}, bf16[4,576,768]{2,1,0:T(8,128)(2,1)S(1)}, u32[]{:S(2)}) %copy-start.5) | copy-done | bytes 3538968
  47.7 3.1 %all_gather.9 = bf16[512,2,128]{2,1,0:T(2,128)(2,1)S(1)} all-gather(bf16[256,2,128]{2,1,0:T(2,128)(2,1)S(1)} %all-to-all-done), channel_id=1, replica_groups=mesh['z'=8,'c'=2,'b'=32] {'c'}, dimensions={0}, use_global_device_ids=true | all-gather | bytes 393216 | tf_op jit(solution)/shard_map/all_gather | solution.py:450
  50.8 1.9 %choose.1 = (bf16[512,128]{1,0:T(8,128)(2,1)S(1)}, bf16[512,128]{1,0:T(8,128)(2,1)S(1)}) custom-call(bf16[1024,128]{1,0:T(8,128)(2,1)S(1)} %bitcast.20, bf16[256,128]{1,0:T(8,128)(2,1)S(1)} %get-tuple-element.15.pooled_ref), custom_call_target="tpu_custom_call" | custom-call | tf_op jit(solution)/shard_map/choose/pallas_call | solution.py:337
  52.7 30.0 %all_to_all.20 = bf16[256,2,128]{2,1,0:T(2,128)(2,1)S(1)} all-to-all(bf16[256,2,128]{2,1,0:T(2,128)(2,1)S(1)} %bitcast.25), channel_id=1, replica_groups=mesh['z'=8,'c'=2,'b'=32] {'z','b'}, dimensions={0} | all-to-all | bytes 262144 | tf_op jit(solution)/shard_map/all_to_all | solution.py:419
  82.7 2.0 %copy-done.6 = bf16[4,576,768]{2,1,0:T(8,128)(2,1)S(1)} copy-done((bf16[4,576,768]{2,1,0:T(8,128)(2,1)S(1)}, bf16[4,576,768]{2,1,0:T(8,128)(2,1)}, u32[]{:S(2)}) %copy-start.6) | copy-done | bytes 3538968
  84.7 4.3 %backward.1 = (f32[872,128]{1,0:T(8,128)S(1)}, f32[872,128]{1,0:T(8,128)S(1)}, bf16[256,128]{1,0:T(8,128)(2,1)S(1)}) custom-call(bf16[512,128]{1,0:T(8,128)(2,1)S(1)} %bitcast.24, bf16[4,576,768]{2,1,0:T(8,128)(2,1)S(1)} %copy-done.6, f32[4,128,512]{2,1,0:T(8,128)S(1)} %get-tuple-element.18.slope_ref), custom_call_target="tpu_custom_call" | custom-call | flops 3500000000 | bytes 6000000 | tf_op jit(solution)/shard_map/backward/pallas_call | solution.py:396
  89.0 3.7 %collective-permute-start.2 = (f32[872,128]{1,0:T(8,128)S(1)}, f32[872,128]{1,0:T(8,128)S(1)}, u32[]{:S(2)}, u32[]{:S(2)}) collective-permute-start(f32[872,128]{1,0:T(8,128)S(1)} %get-tuple-element.20), channel_id=1, source_target_pairs={{0,32},{32,0},{1,33},{33,1},{2,34},{34,2},{3,35},{35,3},{4,36},{36... | collective-permute-start | bytes 1339400 | tf_op jit(solution)/shard_map/ppermute | solution.py:459
  92.7 1.9 %all_gather.10.pooled_ref = bf16[512,128]{1,0:T(8,128)(2,1)S(1)} all-gather(bf16[256,128]{1,0:T(8,128)(2,1)S(1)} %get-tuple-element.21), channel_id=1, replica_groups=mesh['z'=8,'c'=2,'b'=32] {'c'}, dimensions={0}, use_global_device_ids=true | all-gather | bytes 196608 | tf_op jit(solution)/shard_map/all_gather | solution.py:460
  94.6 1.3 share.1
  95.9 23.7 %all_to_all.21 = bf16[256,4,128]{2,1,0:T(4,128)(2,1)S(1)} all-to-all(bf16[256,4,128]{2,1,0:T(4,128)(2,1)S(1)} %bitcast.22), channel_id=1, replica_groups=mesh['z'=8,'c'=2,'b'=32] {'z','b'}, dimensions={0} | all-to-all | bytes 524288 | tf_op jit(solution)/shard_map/all_to_all | solution.py:419
  119.6 1.2 reduce.1
  120.8 9.2 %all-to-all-start.3 = ((bf16[256,4,128]{2,1,0:T(4,128)(2,1)}), bf16[256,4,128]{2,1,0:T(4,128)(2,1)S(1)}, u32[]{:S(2)}, u32[]{:S(2)}) async-start(bf16[256,4,128]{2,1,0:T(4,128)(2,1)} %bitcast.12), calls=%async_computation.3 | async-start | bytes 524288 | tf_op jit(solution)/shard_map/all_to_all | solution.py:419
  130.1 0.1 copy.21
  130.2 0.8 reshape.61
  131.0 12.0 %all-to-all-done.3 = bf16[256,4,128]{2,1,0:T(4,128)(2,1)S(1)} async-done(((bf16[256,4,128]{2,1,0:T(4,128)(2,1)}), bf16[256,4,128]{2,1,0:T(4,128)(2,1)S(1)}, u32[]{:S(2)}, u32[]{:S(2)}) %all-to-all-start.3) | async-done | bytes 262176 | tf_op jit(solution)/shard_map/all_to_all | solution.py:419
  143.0 5.2 %all_gather.11 = bf16[512,4,128]{2,1,0:T(4,128)(2,1)S(1)} all-gather(bf16[256,4,128]{2,1,0:T(4,128)(2,1)S(1)} %all-to-all-done.3), channel_id=1, replica_groups=mesh['z'=8,'c'=2,'b'=32] {'c'}, dimensions={0}, use_global_device_ids=true | all-gather | bytes 786432 | tf_op jit(solution)/shard_map/all_gather | solution.py:469
  148.3 1.7 %finish.1 = (f32[1728,128]{1,0:T(8,128)}, f32[1,128]{1,0:T(1,128)}) custom-call(bf16[2048,128]{1,0:T(8,128)(2,1)S(1)} %bitcast.19), custom_call_target="tpu_custom_call" | custom-call | tf_op jit(solution)/shard_map/finish/pallas_call | solution.py:337
  (12 shorter events, 0.1 us)
Async XLA Ops:
  0.6 1.0 copy-start
  1.6 0.7 copy-start.2
  2.8 33.6 %collective-permute-start.1 = (bf16[4,64,128]{2,1,0:T(8,128)(2,1)S(1)}, bf16[4,64,128]{2,1,0:T(8,128)(2,1)S(1)}, u32[]{:S(2)}, u32[]{:S(2)}) collective-permute-start(bf16[4,64,128]{2,1,0:T(8,128)(2,1)S(1)} %layers.1.layers_ref), channel_id=1, source_target_pairs={{1,0},{2,1},{3,2},{4,3},{5,4},{6,5},{7,6},{8,7},{9,8},{10,9},{11,1... | collective-permute-start | bytes 196616 | tf_op jit(solution)/shard_map/ppermute | solution.py:444
  4.1 32.3 %collective-permute-start = (bf16[4,64,128]{2,1,0:T(8,128)(2,1)S(1)}, bf16[4,64,128]{2,1,0:T(8,128)(2,1)S(1)}, u32[]{:S(2)}, u32[]{:S(2)}) collective-permute-start(bf16[4,64,128]{2,1,0:T(8,128)(2,1)S(1)} %layers.1.layers_ref), channel_id=1, source_target_pairs={{0,1},{1,2},{2,3},{3,4},{4,5},{5,6},{6,7},{7,8},{8,9},{9,10},{10,1... | collective-permute-start | bytes 196616 | tf_op jit(solution)/shard_map/ppermute | solution.py:443
  11.8 35.8 %all-to-all-start = ((bf16[256,2,128]{2,1,0:T(2,128)(2,1)}), bf16[256,2,128]{2,1,0:T(2,128)(2,1)S(1)}, u32[]{:S(2)}, u32[]{:S(2)}) async-start(bf16[256,2,128]{2,1,0:T(2,128)(2,1)} %bitcast), calls=%async_computation | async-start | bytes 262144 | tf_op jit(solution)/shard_map/all_to_all | solution.py:419
  36.4 1.0 copy-start.1
  37.4 0.7 copy-start.3
  38.0 0.7 copy-start.4
  45.9 1.8 %copy-start.5 = (bf16[4,576,768]{2,1,0:T(8,128)(2,1)}, bf16[4,576,768]{2,1,0:T(8,128)(2,1)S(1)}, u32[]{:S(2)}) copy-start(bf16[4,576,768]{2,1,0:T(8,128)(2,1)S(1)} %get-tuple-element.17.stacked_ref) | copy-start | bytes 10616836
  82.7 2.0 %copy-start.6 = (bf16[4,576,768]{2,1,0:T(8,128)(2,1)S(1)}, bf16[4,576,768]{2,1,0:T(8,128)(2,1)}, u32[]{:S(2)}) copy-start(bf16[4,576,768]{2,1,0:T(8,128)(2,1)} %copy-done.5) | copy-start | bytes 10616836
  89.0 5.7 %collective-permute-start.2 = (f32[872,128]{1,0:T(8,128)S(1)}, f32[872,128]{1,0:T(8,128)S(1)}, u32[]{:S(2)}, u32[]{:S(2)}) collective-permute-start(f32[872,128]{1,0:T(8,128)S(1)} %get-tuple-element.20), channel_id=1, source_target_pairs={{0,32},{32,0},{1,33},{33,1},{2,34},{34,2},{3,35},{35,3},{4,36},{36... | collective-permute-start | bytes 1339400 | tf_op jit(solution)/shard_map/ppermute | solution.py:459
  120.8 22.2 %all-to-all-start.3 = ((bf16[256,4,128]{2,1,0:T(4,128)(2,1)}), bf16[256,4,128]{2,1,0:T(4,128)(2,1)S(1)}, u32[]{:S(2)}, u32[]{:S(2)}) async-start(bf16[256,4,128]{2,1,0:T(4,128)(2,1)} %bitcast.12), calls=%async_computation.3 | async-start | bytes 524288 | tf_op jit(solution)/shard_map/all_to_all | solution.py:419

commit v3 on v1

v3 whole, which is shorter than its diff:
```python
import functools

import jax
import jax.numpy as jnp
from jax import lax
from jax.experimental import pallas as pl
from jax.experimental.pallas import tpu as pltpu
from jax.sharding import Mesh
from jax.sharding import PartitionSpec as P

SLOTS = 4
CH = 64
OUT = 128
VOX = 512
FRAME = 768
TAP_ROWS = 1728
BLOCK = 32
HALF = TAP_ROWS // 2
MAIN = 24
EXTRA = 3
SHARE = MAIN + EXTRA
HBM = pltpu.HBM
EDGES = ((-1, -1), (-1, 0), (-1, 1), (0, -1), (0, 0), (0, 1), (1, -1), (1, 0), (1, 1))
SMEM = pltpu.SMEM


def voxel_mask(count):
    lanes = lax.broadcasted_iota(jnp.int32, (1, VOX), 1)
    return ((lanes * 167) & 511) < count


def layer_pair(block):
    lanes = lax.broadcasted_iota(jnp.int32, (CH, 128), 1)
    return jnp.where(lanes < 64, block[:, :128], block[:, VOX - 128 :])


def column_of(ea, eb, ec):
    tap = 9 * (ea + 1) + 3 * (eb + 1) + (ec + 1)
    return tap if tap < 13 else tap - 1


def dot(a, b):
    return jnp.dot(a, b, preferred_element_type=jnp.float32)


def dot_lanes(a, b):
    return lax.dot_general(a, b, (((1,), (1,)), ((), ())), preferred_element_type=jnp.float32)


def grid_of(shape):
    return lax.broadcasted_iota(jnp.int32, shape, 0), lax.broadcasted_iota(jnp.int32, shape, 1)


def onehot(shape, chosen):
    return jnp.where(chosen(*grid_of(shape)), 1.0, 0.0).astype(jnp.bfloat16)


def bf16(array):
    return array.astype(jnp.bfloat16)


def pool_table(voxels_first):
    shape = (VOX, 64) if voxels_first else (64, VOX)
    rows, columns = grid_of(shape)
    voxel, cell = (rows, columns) if voxels_first else (columns, rows)
    index = ((voxel >> 7) << 4) | (((voxel >> 4) & 3) << 2) | ((voxel & 7) >> 1)
    return bf16(jnp.where(index == cell, 0.125, 0.0))


def fetch(pairs, sems):
    copies = [pltpu.make_async_copy(source, target, sems.at[i]) for i, (source, target) in enumerate(pairs)]
    for copy in copies:
        copy.start()
    for copy in copies:
        copy.wait()


def begin_kernel(
    counts_hbm, rebalance_hbm, owner_hbm, features_hbm, adjoint_hbm,
    layers_ref, offer_ref,
    counts_ref, rebalance_ref, owner_ref, features_ref, adjoint_ref, dense_ref, sems,
):
    fetch(
        [
            (counts_hbm, counts_ref),
            (rebalance_hbm, rebalance_ref),
            (owner_hbm, owner_ref),
            (features_hbm, features_ref),
            (adjoint_hbm, adjoint_ref),
        ],
        sems,
    )
    lanes = lax.broadcasted_iota(jnp.int32, (1, 128), 1)
    tags = jnp.zeros((1, 128), jnp.float32)
    for slot in range(SLOTS):
        block = jnp.where(voxel_mask(counts_ref[slot]), features_ref[slot].astype(jnp.float32), 0.0)
        layers_ref[slot] = bf16(layer_pair(block))
        row = rebalance_ref[slot]
        line = jnp.where(row >= 0, (row & (2 * BLOCK - 1)) + 1, 0).astype(jnp.float32)
        owner = jnp.maximum(owner_ref[slot], 0).astype(jnp.float32)
        tags = jnp.where(lanes == slot, line, tags)
        tags = jnp.where(lanes == SLOTS + slot, owner, tags)
    for part in range(64):
        dense_ref[2 * part : 2 * part + 2, :] = adjoint_ref[:, 128 * part : 128 * (part + 1)].astype(jnp.float32)
    order = onehot(
        (8 * BLOCK, 128),
        lambda r, c: ((r & 7) < 4) & (c == 2 * (2 * (r >> 3) + (r & 1)) + ((r >> 1) & 1)),
    )
    rows = lax.broadcasted_iota(jnp.int32, (8 * BLOCK, 128), 0)
    offer_ref[...] = bf16(jnp.where((rows & 7) == 4, tags, dot(order, bf16(dense_ref[...]))))


def spread_kernel(offers_ref, message_ref, tags_ref):
    offers = offers_ref[...]
    message = bf16(dot(onehot((4 * BLOCK, 8 * BLOCK), lambda r, c: c == 8 * (r >> 2) + (r & 3)), offers))
    message_ref[...] = jnp.broadcast_to(message[None], message_ref.shape)
    tags_ref[...] = dot(onehot((BLOCK, 8 * BLOCK), lambda r, c: c == 8 * r + 4), offers).astype(jnp.int32)


def place_of(tags_ref, row):
    tags = tags_ref[...]
    rows, lanes = grid_of((BLOCK, 128))
    hit = (tags == 2 * lax.axis_index("b") + row + 1) & (lanes < SLOTS)
    owner = jnp.where(hit, pltpu.roll(tags, 128 - SLOTS, 1), 0).astype(jnp.float32)
    home = jnp.where(hit, rows, 0).astype(jnp.float32)
    return [
        jnp.sum(jnp.sum(value, axis=1, keepdims=True), axis=0, keepdims=True).astype(jnp.int32)[0, 0]
        for value in (home, owner)
    ]


def forward_kernel(start, *refs):
    operands, refs = refs[: 7 + start // 2], refs[7 + start // 2 :]
    pooled_ref, stacked_hbm, slope_hbm, features_ref, blocks_ref, rims_ref, stacked_ref, slope_ref, dense_ref = refs[:9]
    counts_ref, neighbors_ref, bias_ref, weight_ref, sems, out_sems = refs[9:]
    targets = [
        counts_ref,
        neighbors_ref,
        bias_ref,
        features_ref,
        rims_ref.at[pl.ds(0, SLOTS)],
        rims_ref.at[pl.ds(2 * SLOTS, SLOTS)],
        weight_ref,
        dense_ref.at[pl.ds(0, 2)],
    ]
    fetch(list(zip(operands, targets)), sems)
    for index in range(SLOTS):
        block = jnp.where(voxel_mask(counts_ref[index]), features_ref[index].astype(jnp.float32), 0.0)
        blocks_ref[index] = block
        rims_ref[SLOTS + index] = bf16(layer_pair(block))
    blocks_ref[SLOTS] = jnp.zeros((CH, VOX), jnp.float32)
    rims_ref[3 * SLOTS] = jnp.zeros((CH, 128), jnp.bfloat16)
    first = ((lax.axis_index("z") * 2 + lax.axis_index("c")) * BLOCK + lax.axis_index("b")) * SLOTS
    rows, columns = grid_of((OUT, OUT))
    bias = jnp.sum(jnp.where(rows == columns, bias_ref[...], 0.0), axis=1, keepdims=True)
    lanes = lax.broadcasted_iota(jnp.int32, (CH, FRAME), 1)
    at_c = lanes & 7
    at_b = (lanes >> 3) & 7

    def moved(array, steps):
        return pltpu.roll(array, (-steps) % FRAME, 1)

    @pl.loop(0, 2)
    def _(place):
        slot = start + place

        def rim(ea, eb, ec):
            target = neighbors_ref[slot, column_of(ea, eb, ec)]
            at = jnp.clip(target - (first - SLOTS), 0, 3 * SLOTS - 1)
            return rims_ref[jnp.where(target >= 0, at, 3 * SLOTS)].astype(jnp.float32)

        def inner(eb, ec):
            if eb == 0 and ec == 0:
                return blocks_ref[slot]
            target = neighbors_ref[slot, column_of(0, eb, ec)]
            at = jnp.clip(target - first, 0, SLOTS - 1)
            return blocks_ref[jnp.where(target >= 0, at, SLOTS)]

        def frame(eb, ec):
            return jnp.concatenate([rim(-1, eb, ec), inner(eb, ec), rim(1, eb, ec)], axis=1)

        along_c = {}
        for eb in (-1, 0, 1):
            middle = frame(eb, 0)
            along_c[eb, 0] = middle
            along_c[eb, -1] = jnp.where(at_c == 0, moved(frame(eb, -1), 7), moved(middle, -1))
            along_c[eb, 1] = jnp.where(at_c == 7, moved(frame(eb, 1), -7), moved(middle, 1))
        for index, (eb, ec) in enumerate(EDGES):
            if eb == 0:
                value = along_c[0, ec]
            elif eb < 0:
                value = jnp.where(at_b == 0, moved(along_c[-1, ec], 56), moved(along_c[0, ec], -8))
            else:
                value = jnp.where(at_b == 7, moved(along_c[1, ec], -56), moved(along_c[0, ec], 8))
            stacked_ref[place, index * CH : (index + 1) * CH, :] = value.astype(jnp.bfloat16)

        pltpu.make_async_copy(stacked_ref.at[place], stacked_hbm.at[place], out_sems.at[place]).start()
        product = dot(weight_ref[...], stacked_ref[place])
        sides = product[:OUT, : FRAME - 128] + product[2 * OUT :, 128:]
        sides = pltpu.roll(sides, FRAME - 128 - 64, 1)[:, :VOX]
        preact = product[OUT : 2 * OUT, 128 : 128 + VOX] + sides + bias
        mask = voxel_mask(counts_ref[slot])
        sigmoid = jax.nn.sigmoid(preact)
        slope = sigmoid * (1.0 + preact * (1.0 - sigmoid))
        slope_ref[place] = jnp.where(mask, slope, 0.0)
        pltpu.make_async_copy(slope_ref.at[place], slope_hbm.at[place], out_sems.at[2 + place]).start()
        activation = jnp.where(mask, preact * sigmoid, 0.0)
        high = activation.astype(jnp.bfloat16)
        low = (activation - high.astype(jnp.float32)).astype(jnp.bfloat16)
        table = pool_table(True)
        cells = bf16(dot(high, table) + dot(low, table))
        even = dot(onehot((64, OUT), lambda r, c: c == 2 * r), cells)
        odd = dot(onehot((64, OUT), lambda r, c: c == 2 * r + 1), cells)
        dense_ref[start + place] = jnp.concatenate([even, odd], axis=1)

    if start == 0:
        pooled_ref[...] = dense_ref[:2]
    else:
        order = onehot((8 * BLOCK, 64 * SLOTS), lambda r, c: c == 64 * ((r & 7) >> 1) + 2 * (r >> 3) + (r & 1))
        pooled_ref[...] = bf16(dot(order, bf16(dense_ref[...].reshape(64 * SLOTS, 128))))
    for place in range(2):
        pltpu.make_async_copy(stacked_ref.at[place], stacked_hbm.at[place], out_sems.at[place]).wait()
        pltpu.make_async_copy(slope_ref.at[place], slope_hbm.at[place], out_sems.at[2 + place]).wait()


def choose_kernel(tags_ref, adjoint_ref, pooled_ref, message_ref):
    tags = bf16(tags_ref[...].astype(jnp.float32))
    tags = dot(onehot((8 * BLOCK, BLOCK), lambda r, c: (r >> 3) == c), tags)
    rows, lanes = grid_of((8 * BLOCK, 128))
    slot = (rows & 7) >> 1
    line = jnp.sum(jnp.where(lanes == slot, tags, 0.0), axis=1, keepdims=True).astype(jnp.int32)
    owner = jnp.sum(jnp.where(lanes == slot + SLOTS, tags, 0.0), axis=1, keepdims=True).astype(jnp.int32)
    source = ((owner & 1) * 8 + (owner >> 1)) * (4 * BLOCK) + 2 * (line - 1) + (rows[:, :1] & 1)
    source = jnp.where(line > 0, source, -1)
    lanes = lax.broadcasted_iota(jnp.int32, (8 * BLOCK, 64 * BLOCK), 1)
    cotangent = dot(bf16(jnp.where(lanes == source, 1.0, 0.0)), adjoint_ref[...])
    pooled = pooled_ref[...].astype(jnp.float32)
    message_ref[...] = bf16(
        jnp.concatenate([cotangent.reshape(BLOCK, 8, 128), pooled.reshape(BLOCK, 8, 128)], axis=1)
    )


def add_half(half, total_ref, grads_ref, stacked_ref, ready=lambda slot: None):
    middle = HALF - 9 * CH
    for slot in range(SLOTS):
        grad = grads_ref[slot]
        wide = jnp.concatenate([grad.astype(jnp.float32), jnp.zeros((OUT, 128), jnp.float32)], axis=1)
        shifted = bf16(pltpu.roll(wide, 64, 1))
        ready(slot)
        if half == 0:
            side = dot_lanes(stacked_ref[slot, :, 0 : FRAME - 128], shifted)
            inner = dot_lanes(stacked_ref[slot, :middle, 128 : 128 + VOX], grad)
            parts = ((0, 9 * CH, side), (9 * CH, HALF, inner))
        else:
            inner = dot_lanes(stacked_ref[slot, middle:, 128 : 128 + VOX], grad)
            side = dot_lanes(stacked_ref[slot, :, 128:], shifted)
            parts = ((0, middle, inner), (middle, HALF, side))
        for low, high, value in parts:
            if slot == 0:
                total_ref[low:high] = value
            else:
                total_ref[low:high] += value


def other_half_kernel(
    first_stacked, second_stacked, first_slope, second_slope, rows_ref,
    total_ref, grads_ref, bias_ref, stacked_ref, slope_ref, sems,
):
    slopes = [
        pltpu.make_async_copy(source, slope_ref.at[pl.ds(2 * i, 2)], sems.at[i])
        for i, source in enumerate((first_slope, second_slope))
    ]
    frames = [
        pltpu.make_async_copy((first_stacked, second_stacked)[i // 2].at[i % 2], stacked_ref.at[i], sems.at[2 + i])
        for i in range(SLOTS)
    ]
    for copy in slopes + frames:
        copy.start()
    order = onehot(
        (64 * SLOTS, 16 * BLOCK),
        lambda r, c: c == 16 * ((r & 63) >> 1) + 2 * (r >> 6) + (r & 1),
    )
    dense = bf16(dot(order, rows_ref[...]))
    table = pool_table(False)
    even = onehot((OUT, 64), lambda r, c: r == 2 * c)
    odd = onehot((OUT, 64), lambda r, c: r == 2 * c + 1)
    ones = jnp.ones((8, VOX), jnp.bfloat16)
    bias = jnp.zeros((8, OUT), jnp.float32)
    for slot in range(SLOTS):
        row = dense[64 * slot : 64 * (slot + 1)]
        cells = dot(even, row[:, :64]) + dot(odd, row[:, 64:])
        spread = dot(bf16(cells), table)
        if slot % 2 == 0:
            slopes[slot // 2].wait()
        grad = spread * slope_ref[slot]
        rounded = bf16(grad)
        rest = bf16(grad - rounded.astype(jnp.float32))
        bias += dot_lanes(ones, rounded) + dot_lanes(ones, rest)
        grads_ref[slot] = rounded
    bias_ref[...] = bias
    total_ref[HALF:] = bias
    core = lax.axis_index("c")
    for half in range(2):

        @pl.when(core == 1 - half)
        def _():
            add_half(half, total_ref, grads_ref, stacked_ref, lambda slot: frames[slot].wait())


def own_half_kernel(grads_ref, bias_ref, stacked_ref, total_ref):
    total_ref[HALF:] = bias_ref[...]
    core = lax.axis_index("c")
    for half in range(2):

        @pl.when(core == half)
        def _():
            add_half(half, total_ref, grads_ref, stacked_ref)


def share_kernel(tags_ref, mine_ref, got_ref, pooled_ref, message_ref):
    total = mine_ref[...] + got_ref[...]
    tags = tags_ref[...].astype(jnp.float32)
    lines = dot_lanes(onehot((8, 128), lambda r, c: c == r), bf16(tags))
    lines = dot(bf16(lines), onehot((BLOCK, 16 * BLOCK), lambda r, c: (c >> 4) == r)).astype(jnp.int32)
    rows, columns = grid_of((8, 16 * BLOCK))
    lines = jnp.where(rows == ((columns >> 1) & 7) - SLOTS, lines, 0).astype(jnp.float32)
    line = jnp.sum(lines, axis=0, keepdims=True).astype(jnp.int32)
    columns = lax.broadcasted_iota(jnp.int32, (1, 16 * BLOCK), 1)
    target = 8 * ((line - 1) >> 1) + EXTRA + 2 * ((line - 1) & 1) + (columns & 1)
    target = jnp.where(line > 0, target, -1)
    rows = lax.broadcasted_iota(jnp.int32, (8 * BLOCK, 16 * BLOCK), 0)
    tail = dot(bf16(jnp.where(rows == target, 1.0, 0.0)), pooled_ref[...])
    extra = onehot(
        (8 * BLOCK, EXTRA * BLOCK), lambda r, c: ((r & 7) < EXTRA) & (c == (r & 7) * BLOCK + (r >> 3))
    )
    tail += dot(extra, bf16(total[MAIN * BLOCK : HALF]))
    bias = total[HALF : HALF + 1]
    high = bf16(bias).astype(jnp.float32)
    rows = lax.broadcasted_iota(jnp.int32, (8 * BLOCK, 128), 0)
    tail = jnp.where((rows & 7) == 7, jnp.where((rows & 8) == 0, high, bias - high), tail)
    main = total[: MAIN * BLOCK].reshape(BLOCK, MAIN, 128)
    message_ref[...] = bf16(jnp.concatenate([main, tail.reshape(BLOCK, 8, 128)], axis=1))


def over_block_kernel(tags_ref, pieces_ref, message_ref):
    total = jnp.zeros((32, 128), jnp.float32)
    for device in range(BLOCK):
        total += pieces_ref[device].astype(jnp.float32)
    order = onehot(
        (128, 32 * BLOCK),
        lambda r, c: c == 32 * ((r & 63) >> 1) + SHARE + 2 * (r >> 6) + (r & 1),
    )
    pooled = bf16(dot(order, pieces_ref[...].reshape(32 * BLOCK, 128)))
    rows, lanes = grid_of((32, 128))
    total = jnp.where((rows < SHARE) | (rows == 31), total, 0.0)
    high = bf16(total).astype(jnp.float32)
    low = total - high
    owners = [place_of(tags_ref, row)[1] for row in range(2)]
    for z in range(8):
        tag = jnp.zeros((32, 128), jnp.float32)
        for core in range(2):
            for row in range(2):
                here = (rows == 28) & (lanes == core) & (owners[row] == 2 * z + core)
                tag = jnp.where(here, row + 1.0, tag)
        message_ref[3 * z] = bf16(jnp.concatenate([high + tag, low], axis=0))
        message_ref[3 * z + 1] = jnp.zeros((64, 128), jnp.bfloat16)
        message_ref[3 * z + 2] = jnp.zeros((64, 128), jnp.bfloat16)
    for row in range(2):
        message_ref[3 * (owners[row] >> 1) + 1 + (owners[row] & 1)] = pooled[64 * row : 64 * (row + 1)]


def over_z_kernel(pieces_ref, message_ref, mine_ref, other_ref):
    total = jnp.zeros((32, 128), jnp.float32)
    pooled = [[jnp.zeros((64, 128), jnp.float32) for _ in range(2)] for _ in range(2)]
    for z in range(8):
        parts = pieces_ref[3 * z].astype(jnp.float32)
        total += parts[:32] + parts[32:]
        for core in range(2):
            tag = parts[28:29, core : core + 1]
            value = pieces_ref[3 * z + 1 + core].astype(jnp.float32)
            for row in range(2):
                pooled[core][row] += jnp.where(tag == row + 1.0, value, 0.0)
    rows = lax.broadcasted_iota(jnp.int32, (32, 128), 0)
    bias = total[31:32]
    high = bf16(bias).astype(jnp.float32)
    tile = jnp.where(rows < SHARE, total, jnp.where(rows == 27, high, bias - high))
    message_ref[...] = jnp.broadcast_to(bf16(tile)[None], (BLOCK, 32, 128))
    core = lax.axis_index("c")
    for row in range(2):
        mine_ref[row] = bf16(jnp.where(core == 0, pooled[0][row], pooled[1][row]))
        other_ref[row] = bf16(jnp.where(core == 0, pooled[1][row], pooled[0][row]))


def finish_kernel(pieces_ref, weight_ref, bias_ref):
    order = onehot((EXTRA * BLOCK, 32 * BLOCK), lambda r, c: c == 32 * (r & 31) + MAIN + (r >> 5))
    for half in range(2):
        pieces = pieces_ref[half * BLOCK : (half + 1) * BLOCK]
        for device in range(BLOCK):
            start = half * HALF + device * MAIN
            part = pieces_ref[half * BLOCK + device].astype(jnp.float32)
            weight_ref[start : start + MAIN, :] = part[:MAIN]
        start = half * HALF + MAIN * BLOCK
        weight_ref[start : start + EXTRA * BLOCK, :] = dot(order, pieces.reshape(32 * BLOCK, 128))
    parts = [pieces_ref[device].astype(jnp.float32) for device in range(2)]
    bias_ref[...] = parts[0][27:28] + parts[0][28:29] + (parts[1][27:28] + parts[1][28:29])


def hbm(array):
    return pltpu.with_memory_space_constraint(array, HBM)


def vmem(array):
    return pltpu.with_memory_space_constraint(array, pltpu.VMEM)


def call(kernel, name, outs, operands, in_hbm=0, scratch=(), limit=12, flops=1_000_000):
    specs = [pl.BlockSpec(memory_space=HBM) for _ in range(in_hbm)]
    specs += [pl.BlockSpec(memory_space=pltpu.VMEM) for _ in operands[in_hbm:]]
    operands = [hbm(operand) for operand in operands[:in_hbm]] + list(operands[in_hbm:])
    return pl.pallas_call(
        kernel,
        out_shape=[
            pltpu.VMEM(shape, dtype) if kept else jax.ShapeDtypeStruct(shape, dtype) for shape, dtype, kept in outs
        ],
        in_specs=specs,
        out_specs=[pl.BlockSpec(memory_space=pltpu.VMEM) for _ in outs],
        scratch_shapes=list(scratch),
        compiler_params=pltpu.CompilerParams(vmem_limit_bytes=limit * 1024 * 1024),
        cost_estimate=pl.CostEstimate(flops=flops, bytes_accessed=1_000_000, transcendentals=0),
        name=name,
    )(*operands)


def begin(counts, rebalance, owner, features, adjoint):
    return call(
        begin_kernel,
        "begin",
        [
            ((SLOTS, CH, 128), jnp.bfloat16, False),
            ((8 * BLOCK, 128), jnp.bfloat16, False),
        ],
        (counts, rebalance, owner, features, adjoint),
        in_hbm=5,
        scratch=[
            pltpu.SMEM((SLOTS,), jnp.int32),
            pltpu.SMEM((SLOTS,), jnp.int32),
            pltpu.SMEM((SLOTS,), jnp.int32),
            pltpu.VMEM((SLOTS, CH, VOX), jnp.bfloat16),
            pltpu.VMEM((2, CH * 128), jnp.bfloat16),
            pltpu.VMEM((128, 128), jnp.float32),
            pltpu.SemaphoreType.DMA((5,)),
        ],
    )


def forward(start, *operands):
    pooled = ((2, 64, 128), jnp.float32) if start == 0 else ((8 * BLOCK, 128), jnp.bfloat16)
    kept = pl.BlockSpec(memory_space=HBM)
    return pl.pallas_call(
        functools.partial(forward_kernel, start),
        out_shape=[
            jax.ShapeDtypeStruct(*pooled),
            HBM((2, 9 * CH, FRAME), jnp.bfloat16),
            HBM((2, OUT, VOX), jnp.float32),
        ],
        in_specs=[kept for _ in operands],
        out_specs=[pl.BlockSpec(memory_space=pltpu.VMEM), kept, kept],
        scratch_shapes=[
            pltpu.VMEM((SLOTS, CH, VOX), jnp.bfloat16),
            pltpu.VMEM((SLOTS + 1, CH, VOX), jnp.float32),
            pltpu.VMEM((3 * SLOTS + 1, CH, 128), jnp.bfloat16),
            pltpu.VMEM((2, 9 * CH, FRAME), jnp.bfloat16),
            pltpu.VMEM((2, OUT, VOX), jnp.float32),
            pltpu.VMEM((SLOTS, 64, 128), jnp.float32),
            pltpu.SMEM((SLOTS,), jnp.int32),
            pltpu.SMEM((SLOTS, 26), jnp.int32),
            pltpu.VMEM((1, OUT), jnp.float32),
            pltpu.VMEM((3 * OUT, 9 * CH), jnp.bfloat16),
            pltpu.SemaphoreType.DMA((8,)),
            pltpu.SemaphoreType.DMA((4,)),
        ],
        compiler_params=pltpu.CompilerParams(vmem_limit_bytes=16 * 1024 * 1024),
        cost_estimate=pl.CostEstimate(flops=4_000_000_000, bytes_accessed=4_000_000, transcendentals=150_000),
        name="forward",
    )(*[hbm(operand) for operand in operands])


def exchange(message, axis):
    return lax.all_to_all(message, axis, 0, 0, tiled=True)


def per_device(
    features,
    counts,
    rebalance,
    neighbors,
    coarse_owner,
    conv_weight,
    convolution_bias_vector,
    merged_adjoint,
):
    narrow, wide = jnp.bfloat16, jnp.float32
    layers, offer = begin(counts, rebalance, coarse_owner, features, merged_adjoint)
    before = lax.ppermute(layers, "b", [(i, i + 1) for i in range(BLOCK - 1)])
    after = lax.ppermute(layers, "b", [(i + 1, i) for i in range(BLOCK - 1)])
    offers = exchange(offer.reshape(BLOCK, 8, 128), "b")
    weight = conv_weight.reshape(3, 9 * CH, OUT).transpose(0, 2, 1).reshape(3 * OUT, 9 * CH)
    bias = convolution_bias_vector.reshape(1, OUT)
    first = forward(0, counts, neighbors, bias, features, before, after, weight)
    offers, first_dense = lax.optimization_barrier((offers.reshape(8 * BLOCK, 128), first[0]))
    message, tags = call(
        spread_kernel,
        "spread",
        [((8, 4 * BLOCK, 128), narrow, False), ((BLOCK, 128), jnp.int32, False)],
        (offers,),
    )
    message, bias = lax.optimization_barrier((message, bias))
    adjoint = exchange(message, "z")
    adjoint = lax.all_gather(adjoint, "c", tiled=True).reshape(64 * BLOCK, 128)
    second = forward(2, counts, neighbors, bias, features, before, after, weight, first_dense)
    (message,) = call(
        choose_kernel,
        "choose",
        [((BLOCK, 16, 128), narrow, False)],
        (tags, adjoint, second[0]),
    )
    rows = exchange(message, "b").reshape(16 * BLOCK, 128)
    other, grads, bias_part, stacked = call(
        other_half_kernel,
        "other_half",
        [
            ((HALF + 8, OUT), wide, False),
            ((SLOTS, OUT, VOX), narrow, True),
            ((8, OUT), wide, True),
            ((SLOTS, 9 * CH, FRAME), narrow, True),
        ],
        (first[1], second[1], first[2], second[2], rows),
        in_hbm=4,
        scratch=[pltpu.VMEM((SLOTS, OUT, VOX), jnp.float32), pltpu.SemaphoreType.DMA((2 + SLOTS,))],
    )
    got = lax.ppermute(other, "c", [(0, 1), (1, 0)])
    (mine,) = call(
        own_half_kernel,
        "own_half",
        [((HALF + 8, OUT), wide, False)],
        (vmem(grads), vmem(bias_part), vmem(stacked)),
        flops=2_000_000_000,
    )
    (message,) = call(share_kernel, "share", [((BLOCK, 32, 128), narrow, False)], (tags, mine, got, rows))
    pieces = exchange(message, "b")
    (message,) = call(over_block_kernel, "over_block", [((24, 64, 128), narrow, False)], (tags, pieces))
    pieces = exchange(message.reshape(8, 192, 128), "z").reshape(24, 64, 128)
    message, pooled_mine, pooled_other = call(
        over_z_kernel,
        "over_z",
        [((BLOCK, 32, 128), narrow, False), ((2, CH, 128), narrow, False), ((2, CH, 128), narrow, False)],
        (pieces,),
    )
    pieces = exchange(message, "b")
    pooled = pooled_mine + lax.ppermute(pooled_other, "c", [(0, 1), (1, 0)])
    pieces = lax.all_gather(pieces, "c", tiled=True)
    weight_total, bias_total = call(
        finish_kernel, "finish", [((TAP_ROWS, OUT), wide, False), ((1, OUT), wide, False)], (pieces,)
    )
    return pooled.reshape(2, CH * 128), weight_total.reshape(27, CH, OUT), bias_total.reshape(OUT)


def solution(mesh):
    chips = Mesh(mesh.devices.reshape(-1, 2, BLOCK), ("z", "c", "b"))
    whole = ("z", "c", "b")
    in_specs = (
        P(whole, None, None),
        P(whole),
        P(whole),
        P(whole, None),
        P(whole),
        P(),
        P(),
        P(whole, None),
    )
    out_specs = (P(whole, None), P(), P())
    return jax.shard_map(
        per_device, mesh=chips, in_specs=in_specs, out_specs=out_specs, check_vma=False
    )
```

time: 692 us -> 137 us (0.20)
  waiting for transfers between devices: 485 us -> 8.74 us
  blocking collectives: 149 us -> 56.4 us
  starting transfers between devices: 5.48 us -> 43.1 us
  between operations: 14.6 us -> 0.77 us
  local copies, waits for them, and re-layouts: 15.7 us -> 3.92 us
  Pallas kernels: 16.1 us -> 23.1 us
    psum x1 -> x0, waiting for transfers between devices: 230 us -> none  [per_device(): lax.psum((weight_grad.reshape(27, CH, OUT), bias_grad.reshape(OUT)), ('re...]
    reduce_scatter x2 -> x0, waiting for transfers between devices: 172 us -> none  [the longest x1 172 us: per_device(): lax.psum_scatter(send, 'block', scatter_dimension=0, tiled=True)]
    psum x1 -> x0, blocking collectives: 101 us -> none  [per_device(): lax.psum((weight_grad.reshape(27, CH, OUT), bias_grad.reshape(OUT)), ('re...]
    all_gather x1 -> x0, waiting for transfers between devices: 82.8 us -> none  [per_device(): group_cot = lax.all_gather(work_cot, 'block', tiled=True)]
    all_to_all x0 -> x3, blocking collectives: none -> 44.4 us  [exchange(): return lax.all_to_all(message, axis, 0, 0, tiled=True)]
    all_to_all x0 -> x3, starting transfers between devices: none -> 28.7 us  [exchange(): return lax.all_to_all(message, axis, 0, 0, tiled=True)]
    unnamed x1 -> x0, blocking collectives: 18.6 us -> none
    all_gather x1 -> x2, blocking collectives: 29.4 us -> 11.9 us  [the longest x1 6.2 us: per_device(): pieces = lax.all_gather(pieces, 'c', tiled=True)]
  transfers between devices with their start and end apart: 6 -> 7, of which waited for: 3 -> 4; matrix products, arithmetic and copies ran while one was open for 1% -> 2% of each run, Pallas kernels for 1% -> 9%
where the time goes in v3:
time: 137 us; the launch traced here: 136 us
  blocking collectives  56.4 us (41%)
  starting transfers between devices  43.1 us (31%)
  Pallas kernels  23.1 us (17%)
  waiting for transfers between devices  8.74 us (6%)
  local copies, waits for them, and re-layouts  3.92 us (3%)
    all_to_all x3, blocking collectives, exchange(): return lax.all_to_all(message, axis, 0, 0, tiled=True)  44.4 us
    all_to_all x3, starting transfers between devices, exchange(): return lax.all_to_all(message, axis, 0, 0, tiled=True)  28.7 us
    pallas_call x9, Pallas kernels, call(): pl.pallas_call(kernel, out_shape=[pltpu.VMEM(shape, dtype) if kept else j...  12.1 us
    pallas_call x2, Pallas kernels, forward(): pl.pallas_call(functools.partial(forward_kernel, start), out_shape=[jax.S...  11 us
    all_to_all x3, waiting for transfers between devices, exchange(): return lax.all_to_all(message, axis, 0, 0, tiled=True)  7.9 us
    all_gather x1, blocking collectives, per_device(): pieces = lax.all_gather(pieces, 'c', tiled=True)  6.2 us
    all_gather x1, blocking collectives, per_device(): adjoint = lax.all_gather(adjoint, 'c', tiled=True).reshape(64 * BLOCK, 128)  5.74 us
    ppermute x1, starting transfers between devices, per_device(): before = lax.ppermute(layers, 'b', [(i, i + 1) for i in range(BLOCK - 1)])  4.66 us
  transfers between devices with their start and end apart: 7, of which 4 were waited for; matrix products, arithmetic and copies ran while one was open for 2% of the time, Pallas kernels for 9%

profile of v3, /device:TPU:1, one launch (start us, length us, event | category | flops | bytes accessed | tf_op | source)
XLA Modules:
  0.0 136.0 jit_solution(10058071102639974155)
XLA Ops:
  0.6 1.8 %begin.1 = (bf16[4,64,128]{2,1,0:T(8,128)(2,1)S(1)}, bf16[256,128]{1,0:T(8,128)(2,1)}) custom-call(s32[4]{0:T(128)} %refs_0_.3, s32[4]{0:T(128)} %rebalance_hbm.1, s32[4]{0:T(128)} %owner_hbm.1, bf16[4,64,512]{2,1,0:T(8,128)(2,1)} %refs_3_.3, bf16[2,8192]{1,0:T(2,128)(2,1)} %adjoint_hbm.1), custom_call_target="tpu_custom_call" | custom-call | flops 1000000 | bytes 1000000 | tf_op jit(solution)/shard_map/begin/pallas_call | solution.py:420
  2.5 1.3 collective-permute-start.1
  3.8 4.7 %collective-permute-start = (bf16[4,64,128]{2,1,0:T(8,128)(2,1)S(1)}, bf16[4,64,128]{2,1,0:T(8,128)(2,1)S(1)}, u32[]{:S(2)}, u32[]{:S(2)}) collective-permute-start(bf16[4,64,128]{2,1,0:T(8,128)(2,1)S(1)} %get-tuple-element.27), channel_id=1, source_target_pairs={{0,1},{1,2},{2,3},{3,4},{4,5},{5,6},{6,7},{7,8},{8,9},{9,10},{10,1... | collective-permute-start | bytes 196616 | tf_op jit(solution)/shard_map/ppermute | solution.py:504
  8.4 9.8 %all-to-all-start = ((bf16[32,8,128]{2,1,0:T(8,128)(2,1)}), bf16[32,8,128]{2,1,0:T(8,128)(2,1)S(1)}, u32[]{:S(2)}, u32[]{:S(2)}) async-start(bf16[32,8,128]{2,1,0:T(8,128)(2,1)} %bitcast), calls=%async_computation | async-start | bytes 131072 | tf_op jit(solution)/shard_map/all_to_all | solution.py:489
  18.3 2.0 %copy.12 = bf16[3,576,128]{1,2,0:T(8,128)(2,1)} copy(bf16[3,576,128]{2,1,0:T(8,128)(2,1)} %bitcast.26) | data formatting | bytes 884736 | tf_op jit(solution)/shard_map/reshape | solution.py:507
  20.3 0.6 copy-done.1
  20.9 0.0 copy-done.2
  21.0 5.5 %forward.2 = (f32[2,64,128]{2,1,0:T(8,128)S(1)}, bf16[2,576,768]{2,1,0:T(8,128)(2,1)}, f32[2,128,512]{2,1,0:T(8,128)}) custom-call(s32[4]{0:T(128)} %refs_0_.3, s32[4,26]{1,0:T(4,128)} %refs_1_.3, f32[1,128]{1,0:T(1,128)} %bitcast.29, bf16[4,64,512]{2,1,0:T(8,128)(2,1)} %refs_3_.3, bf16[4,64,128]{2,1,0:T(8,128)(2,1)} %copy-done.2, ...), custom_call_target="tpu_custom_call" | custom-call | flops 4000000000 | bytes 4000000 | tf_op jit(solution)/shard_map/forward/pallas_call | solution.py:459
  26.5 0.6 copy-done
  27.1 0.2 all-to-all-done
  27.3 0.9 spread.1
  28.1 10.0 %all-to-all-start.1 = ((bf16[8,128,128]{2,1,0:T(8,128)(2,1)}), bf16[8,128,128]{2,1,0:T(8,128)(2,1)S(1)}, u32[]{:S(2)}, u32[]{:S(2)}) async-start(bf16[8,128,128]{2,1,0:T(8,128)(2,1)} %get-tuple-element.38), calls=%async_computation.1 | async-start | bytes 524288 | tf_op jit(solution)/shard_map/all_to_all | solution.py:489
  38.2 5.5 %forward.3 = (bf16[256,128]{1,0:T(8,128)(2,1)S(1)}, bf16[2,576,768]{2,1,0:T(8,128)(2,1)}, f32[2,128,512]{2,1,0:T(8,128)}) custom-call(s32[4]{0:T(128)} %refs_0_.3, s32[4,26]{1,0:T(4,128)} %refs_1_.3, f32[1,128]{1,0:T(1,128)} %bitcast.30, bf16[4,64,512]{2,1,0:T(8,128)(2,1)} %refs_3_.3, bf16[4,64,128]{2,1,0:T(8,128)(2,1)} %copy-done.2, ...), custom_call_target="tpu_custom_call" | custom-call | flops 4000000000 | bytes 4000000 | tf_op jit(solution)/shard_map/forward/pallas_call | solution.py:459
  43.6 3.9 %all-to-all-done.1 = bf16[8,128,128]{2,1,0:T(8,128)(2,1)S(1)} async-done(((bf16[8,128,128]{2,1,0:T(8,128)(2,1)}), bf16[8,128,128]{2,1,0:T(8,128)(2,1)S(1)}, u32[]{:S(2)}, u32[]{:S(2)}) %all-to-all-start.1) | async-done | bytes 262176 | tf_op jit(solution)/shard_map/all_to_all | solution.py:489
  47.6 5.7 %all_gather.6 = bf16[16,128,128]{2,1,0:T(8,128)(2,1)S(1)} all-gather(bf16[8,128,128]{2,1,0:T(8,128)(2,1)S(1)} %all-to-all-done.1), channel_id=1, replica_groups=mesh['z'=8,'c'=2,'b'=32] {'c'}, dimensions={0}, use_global_device_ids=true | all-gather | bytes 786432 | tf_op jit(solution)/shard_map/all_gather | solution.py:519
  53.3 0.6 choose.1
  53.9 17.5 %all_to_all.30 = bf16[32,16,128]{2,1,0:T(8,128)(2,1)S(1)} all-to-all(bf16[32,16,128]{2,1,0:T(8,128)(2,1)S(1)} %choose.1), channel_id=1, replica_groups=mesh['z'=8,'c'=2,'b'=32] {'b'}, dimensions={0} | all-to-all | bytes 262144 | tf_op jit(solution)/shard_map/all_to_all | solution.py:489
  71.5 4.4 %other_half.1 = (f32[872,128]{1,0:T(8,128)S(1)}, bf16[4,128,512]{2,1,0:T(8,128)(2,1)S(1)}, f32[8,128]{1,0:T(8,128)S(1)}, bf16[4,576,768]{2,1,0:T(8,128)(2,1)S(1)}) custom-call(bf16[2,576,768]{2,1,0:T(8,128)(2,1)} %get-tuple-element.31.first_stacked, bf16[2,576,768]{2,1,0:T(8,128)(2,1)} %get-tuple-element.35.second_stacked, ...), custom_call_target="tpu_custom_call" | custom-call | flops 1000000 | bytes 1000000 | tf_op jit(solution)/shard_map/other_half/pallas_call | solution.py:420
  75.8 4.1 %collective-permute-start.2 = (f32[872,128]{1,0:T(8,128)S(1)}, f32[872,128]{1,0:T(8,128)S(1)}, u32[]{:S(2)}, u32[]{:S(2)}) collective-permute-start(f32[872,128]{1,0:T(8,128)S(1)} %get-tuple-element.43), channel_id=1, source_target_pairs={{0,32},{32,0},{1,33},{33,1},{2,34},{34,2},{3,35},{35,3},{4,36},{36... | collective-permute-start | bytes 1339400 | tf_op jit(solution)/shard_map/ppermute | solution.py:541
  80.0 1.5 %own_half.1.mine_ref = f32[872,128]{1,0:T(8,128)S(1)} custom-call(bf16[4,128,512]{2,1,0:T(8,128)(2,1)S(1)} %get-tuple-element.40.grads_ref, f32[8,128]{1,0:T(8,128)S(1)} %get-tuple-element.41.bias_ref, bf16[4,576,768]{2,1,0:T(8,128)(2,1)S(1)} %get-tuple-element.42.stacked_ref), custom_call_target="tpu_custom_call" | custom-call | flops 2000000000 | bytes 1000000 | tf_op jit(solution)/shard_map/own_half/pallas_call | solution.py:420
  81.5 0.5 share.1
  82.0 13.3 %all_to_all.31.pieces_ref = bf16[32,32,128]{2,1,0:T(8,128)(2,1)S(1)} all-to-all(bf16[32,32,128]{2,1,0:T(8,128)(2,1)S(1)} %share.1), channel_id=1, replica_groups=mesh['z'=8,'c'=2,'b'=32] {'b'}, dimensions={0} | all-to-all | bytes 524288 | tf_op jit(solution)/shard_map/all_to_all | solution.py:489
  95.3 0.3 over_block.1
  95.6 13.6 %all_to_all.32 = bf16[8,192,128]{2,1,0:T(8,128)(2,1)S(1)} all-to-all(bf16[8,192,128]{2,1,0:T(8,128)(2,1)S(1)} %bitcast.20), channel_id=1, replica_groups=mesh['z'=8,'c'=2,'b'=32] {'z'}, dimensions={0} | all-to-all | bytes 786432 | tf_op jit(solution)/shard_map/all_to_all | solution.py:489
  109.2 0.9 over_z.1
  110.2 8.8 %all-to-all-start.5 = ((bf16[32,32,128]{2,1,0:T(8,128)(2,1)}), bf16[32,32,128]{2,1,0:T(8,128)(2,1)S(1)}, u32[]{:S(2)}, u32[]{:S(2)}) async-start(bf16[32,32,128]{2,1,0:T(8,128)(2,1)} %get-tuple-element.46), calls=%async_computation.5 | async-start | bytes 524288 | tf_op jit(solution)/shard_map/all_to_all | solution.py:489
  118.9 4.3 %collective-permute-start.3 = (bf16[2,64,128]{2,1,0:T(8,128)(2,1)S(1)}, bf16[2,64,128]{2,1,0:T(8,128)(2,1)S(1)}, u32[]{:S(2)}, u32[]{:S(2)}) collective-permute-start(bf16[2,64,128]{2,1,0:T(8,128)(2,1)S(1)} %get-tuple-element.45), channel_id=1, source_target_pairs={{0,32},{32,0},{1,33},{33,1},{2,34},{34,2},{3,35},{35,3},{4,36},{36... | collective-permute-start | bytes 98312 | tf_op jit(solution)/shard_map/ppermute | solution.py:560
  123.3 0.8 collective-permute-done.3
  124.1 0.7 copy.15
  124.8 3.8 %all-to-all-done.5 = bf16[32,32,128]{2,1,0:T(8,128)(2,1)S(1)} async-done(((bf16[32,32,128]{2,1,0:T(8,128)(2,1)}), bf16[32,32,128]{2,1,0:T(8,128)(2,1)S(1)}, u32[]{:S(2)}, u32[]{:S(2)}) %all-to-all-start.5) | async-done | bytes 262176 | tf_op jit(solution)/shard_map/all_to_all | solution.py:489
  128.6 6.2 %all_gather.7.pieces_ref = bf16[64,32,128]{2,1,0:T(8,128)(2,1)S(1)} all-gather(bf16[32,32,128]{2,1,0:T(8,128)(2,1)S(1)} %all-to-all-done.5), channel_id=1, replica_groups=mesh['z'=8,'c'=2,'b'=32] {'c'}, dimensions={0}, use_global_device_ids=true | all-gather | bytes 786432 | tf_op jit(solution)/shard_map/all_gather | solution.py:561
  134.8 1.2 finish.1
  (7 shorter events, 0.0 us)
Async XLA Ops:
  2.5 17.8 %collective-permute-start.1 = (bf16[4,64,128]{2,1,0:T(8,128)(2,1)S(1)}, bf16[4,64,128]{2,1,0:T(8,128)(2,1)S(1)}, u32[]{:S(2)}, u32[]{:S(2)}) collective-permute-start(bf16[4,64,128]{2,1,0:T(8,128)(2,1)S(1)} %get-tuple-element.27), channel_id=1, source_target_pairs={{1,0},{2,1},{3,2},{4,3},{5,4},{6,5},{7,6},{8,7},{9,8},{10,9},{11,1... | collective-permute-start | bytes 196616 | tf_op jit(solution)/shard_map/ppermute | solution.py:505
  3.8 16.5 %collective-permute-start = (bf16[4,64,128]{2,1,0:T(8,128)(2,1)S(1)}, bf16[4,64,128]{2,1,0:T(8,128)(2,1)S(1)}, u32[]{:S(2)}, u32[]{:S(2)}) collective-permute-start(bf16[4,64,128]{2,1,0:T(8,128)(2,1)S(1)} %get-tuple-element.27), channel_id=1, source_target_pairs={{0,1},{1,2},{2,3},{3,4},{4,5},{5,6},{6,7},{7,8},{8,9},{9,10},{10,1... | collective-permute-start | bytes 196616 | tf_op jit(solution)/shard_map/ppermute | solution.py:504
  8.4 18.8 %all-to-all-start = ((bf16[32,8,128]{2,1,0:T(8,128)(2,1)}), bf16[32,8,128]{2,1,0:T(8,128)(2,1)S(1)}, u32[]{:S(2)}, u32[]{:S(2)}) async-start(bf16[32,8,128]{2,1,0:T(8,128)(2,1)} %bitcast), calls=%async_computation | async-start | bytes 131072 | tf_op jit(solution)/shard_map/all_to_all | solution.py:489
  20.3 0.6 copy-start.1
  20.3 0.6 copy-start.2
  26.5 0.6 copy-start
  28.1 19.4 %all-to-all-start.1 = ((bf16[8,128,128]{2,1,0:T(8,128)(2,1)}), bf16[8,128,128]{2,1,0:T(8,128)(2,1)S(1)}, u32[]{:S(2)}, u32[]{:S(2)}) async-start(bf16[8,128,128]{2,1,0:T(8,128)(2,1)} %get-tuple-element.38), calls=%async_computation.1 | async-start | bytes 524288 | tf_op jit(solution)/shard_map/all_to_all | solution.py:489
  75.8 5.7 %collective-permute-start.2 = (f32[872,128]{1,0:T(8,128)S(1)}, f32[872,128]{1,0:T(8,128)S(1)}, u32[]{:S(2)}, u32[]{:S(2)}) collective-permute-start(f32[872,128]{1,0:T(8,128)S(1)} %get-tuple-element.43), channel_id=1, source_target_pairs={{0,32},{32,0},{1,33},{33,1},{2,34},{34,2},{3,35},{35,3},{4,36},{36... | collective-permute-start | bytes 1339400 | tf_op jit(solution)/shard_map/ppermute | solution.py:541
  110.2 18.4 %all-to-all-start.5 = ((bf16[32,32,128]{2,1,0:T(8,128)(2,1)}), bf16[32,32,128]{2,1,0:T(8,128)(2,1)S(1)}, u32[]{:S(2)}, u32[]{:S(2)}) async-start(bf16[32,32,128]{2,1,0:T(8,128)(2,1)} %get-tuple-element.46), calls=%async_computation.5 | async-start | bytes 524288 | tf_op jit(solution)/shard_map/all_to_all | solution.py:489
  118.9 5.2 %collective-permute-start.3 = (bf16[2,64,128]{2,1,0:T(8,128)(2,1)S(1)}, bf16[2,64,128]{2,1,0:T(8,128)(2,1)S(1)}, u32[]{:S(2)}, u32[]{:S(2)}) collective-permute-start(bf16[2,64,128]{2,1,0:T(8,128)(2,1)S(1)} %get-tuple-element.45), channel_id=1, source_target_pairs={{0,32},{32,0},{1,33},{33,1},{2,34},{34,2},{3,35},{35,3},{4,36},{36... | collective-permute-start | bytes 98312 | tf_op jit(solution)/shard_map/ppermute | solution.py:560

commit v4 on v3

--- a/solution.py
+++ b/solution.py
@@ -12,7 +12,7 @@
 CH = 64
 OUT = 128
 VOX = 512
-FRAME = 768
+FRAME = 640
 TAP_ROWS = 1728
 BLOCK = 32
 HALF = TAP_ROWS // 2
@@ -31,7 +31,7 @@
 
 def layer_pair(block):
     lanes = lax.broadcasted_iota(jnp.int32, (CH, 128), 1)
-    return jnp.where(lanes < 64, block[:, :128], block[:, VOX - 128 :])
+    return pltpu.roll(jnp.where(lanes < 64, block[:, :128], block[:, VOX - 128 :]), 64, 1)
 
 
 def column_of(ea, eb, ec):
@@ -131,8 +131,8 @@
 
 def forward_kernel(start, *refs):
     operands, refs = refs[: 7 + start // 2], refs[7 + start // 2 :]
-    pooled_ref, stacked_hbm, slope_hbm, features_ref, blocks_ref, rims_ref, stacked_ref, slope_ref, dense_ref = refs[:9]
-    counts_ref, neighbors_ref, bias_ref, weight_ref, sems, out_sems = refs[9:]
+    pooled_out, stacked_ref, slope_hbm, features_ref, blocks_ref, rims_ref, slope_ref, dense_ref = refs[:8]
+    counts_ref, neighbors_ref, bias_ref, taps_ref, weight_ref, sems, out_sems = refs[8:]
     targets = [
         counts_ref,
         neighbors_ref,
@@ -140,16 +140,21 @@
         features_ref,
         rims_ref.at[pl.ds(0, SLOTS)],
         rims_ref.at[pl.ds(2 * SLOTS, SLOTS)],
-        weight_ref,
+        taps_ref,
         dense_ref.at[pl.ds(0, 2)],
     ]
     fetch(list(zip(operands, targets)), sems)
     for index in range(SLOTS):
         block = jnp.where(voxel_mask(counts_ref[index]), features_ref[index].astype(jnp.float32), 0.0)
+        block = pltpu.roll(block, 64, 1)
         blocks_ref[index] = block
-        rims_ref[SLOTS + index] = bf16(layer_pair(block))
+        rims_ref[SLOTS + index] = bf16(block[:, :128])
     blocks_ref[SLOTS] = jnp.zeros((CH, VOX), jnp.float32)
     rims_ref[3 * SLOTS] = jnp.zeros((CH, 128), jnp.bfloat16)
+    same = onehot((OUT, OUT), lambda r, c: r == c)
+    for part in range(3):
+        turned = dot_lanes(same, taps_ref[part * 9 * CH : (part + 1) * 9 * CH, :])
+        weight_ref[part * OUT : (part + 1) * OUT, :] = bf16(turned)
     first = ((lax.axis_index("z") * 2 + lax.axis_index("c")) * BLOCK + lax.axis_index("b")) * SLOTS
     rows, columns = grid_of((OUT, OUT))
     bias = jnp.sum(jnp.where(rows == columns, bias_ref[...], 0.0), axis=1, keepdims=True)
@@ -177,7 +182,12 @@
             return blocks_ref[jnp.where(target >= 0, at, SLOTS)]
 
         def frame(eb, ec):
-            return jnp.concatenate([rim(-1, eb, ec), inner(eb, ec), rim(1, eb, ec)], axis=1)
+            low = lax.broadcasted_iota(jnp.int32, (CH, 128), 1) < 64
+            block = inner(eb, ec)
+            ends = block[:, :128]
+            left = jnp.where(low, rim(-1, eb, ec), ends)
+            right = jnp.where(low, ends, rim(1, eb, ec))
+            return jnp.concatenate([left, block[:, 128:], right], axis=1)
 
         along_c = {}
         for eb in (-1, 0, 1):
@@ -194,16 +204,14 @@
                 value = jnp.where(at_b == 7, moved(along_c[1, ec], -56), moved(along_c[0, ec], 8))
             stacked_ref[place, index * CH : (index + 1) * CH, :] = value.astype(jnp.bfloat16)
 
-        pltpu.make_async_copy(stacked_ref.at[place], stacked_hbm.at[place], out_sems.at[place]).start()
         product = dot(weight_ref[...], stacked_ref[place])
-        sides = product[:OUT, : FRAME - 128] + product[2 * OUT :, 128:]
-        sides = pltpu.roll(sides, FRAME - 128 - 64, 1)[:, :VOX]
-        preact = product[OUT : 2 * OUT, 128 : 128 + VOX] + sides + bias
+        middle = pltpu.roll(product[OUT : 2 * OUT], FRAME - 64, 1)[:, :VOX]
+        preact = product[:OUT, :VOX] + middle + product[2 * OUT :, 128:] + bias
         mask = voxel_mask(counts_ref[slot])
         sigmoid = jax.nn.sigmoid(preact)
         slope = sigmoid * (1.0 + preact * (1.0 - sigmoid))
         slope_ref[place] = jnp.where(mask, slope, 0.0)
-        pltpu.make_async_copy(slope_ref.at[place], slope_hbm.at[place], out_sems.at[2 + place]).start()
+        pltpu.make_async_copy(slope_ref.at[place], slope_hbm.at[place], out_sems.at[place]).start()
         activation = jnp.where(mask, preact * sigmoid, 0.0)
         high = activation.astype(jnp.bfloat16)
         low = (activation - high.astype(jnp.float32)).astype(jnp.bfloat16)
@@ -213,14 +221,15 @@
         odd = dot(onehot((64, OUT), lambda r, c: c == 2 * r + 1), cells)
         dense_ref[start + place] = jnp.concatenate([even, odd], axis=1)
 
+    copies = [pltpu.make_async_copy(slope_ref.at[place], slope_hbm.at[place], out_sems.at[place]) for place in range(2)]
     if start == 0:
-        pooled_ref[...] = dense_ref[:2]
+        copies.append(pltpu.make_async_copy(dense_ref.at[pl.ds(0, 2)], pooled_out, out_sems.at[2]))
+        copies[2].start()
     else:
         order = onehot((8 * BLOCK, 64 * SLOTS), lambda r, c: c == 64 * ((r & 7) >> 1) + 2 * (r >> 3) + (r & 1))
-        pooled_ref[...] = bf16(dot(order, bf16(dense_ref[...].reshape(64 * SLOTS, 128))))
-    for place in range(2):
-        pltpu.make_async_copy(stacked_ref.at[place], stacked_hbm.at[place], out_sems.at[place]).wait()
-        pltpu.make_async_copy(slope_ref.at[place], slope_hbm.at[place], out_sems.at[2 + place]).wait()
+        pooled_out[...] = bf16(dot(order, bf16(dense_ref[...].reshape(64 * SLOTS, 128))))
+    for copy in copies:
+        copy.wait()
 
 
 def choose_kernel(tags_ref, adjoint_ref, pooled_ref, message_ref):
@@ -240,20 +249,20 @@
     )
 
 
-def add_half(half, total_ref, grads_ref, stacked_ref, ready=lambda slot: None):
+def add_half(half, total_ref, grads_ref, stacked_refs):
     middle = HALF - 9 * CH
     for slot in range(SLOTS):
+        stacked_ref, place = stacked_refs[slot // 2], slot % 2
         grad = grads_ref[slot]
         wide = jnp.concatenate([grad.astype(jnp.float32), jnp.zeros((OUT, 128), jnp.float32)], axis=1)
         shifted = bf16(pltpu.roll(wide, 64, 1))
-        ready(slot)
         if half == 0:
-            side = dot_lanes(stacked_ref[slot, :, 0 : FRAME - 128], shifted)
-            inner = dot_lanes(stacked_ref[slot, :middle, 128 : 128 + VOX], grad)
+            side = dot_lanes(stacked_ref[place, :, :VOX], grad)
+            inner = dot_lanes(stacked_ref[place, :middle, :], shifted)
             parts = ((0, 9 * CH, side), (9 * CH, HALF, inner))
         else:
-            inner = dot_lanes(stacked_ref[slot, middle:, 128 : 128 + VOX], grad)
-            side = dot_lanes(stacked_ref[slot, :, 128:], shifted)
+            inner = dot_lanes(stacked_ref[place, middle:, :], shifted)
+            side = dot_lanes(stacked_ref[place, :, 128:], grad)
             parts = ((0, middle, inner), (middle, HALF, side))
         for low, high, value in parts:
             if slot == 0:
@@ -263,18 +272,13 @@
 
 
 def other_half_kernel(
-    first_stacked, second_stacked, first_slope, second_slope, rows_ref,
-    total_ref, grads_ref, bias_ref, stacked_ref, slope_ref, sems,
+    first_slope, second_slope, first_stacked, second_stacked, rows_ref, total_ref, grads_ref, bias_ref, slope_ref, sems
 ):
     slopes = [
         pltpu.make_async_copy(source, slope_ref.at[pl.ds(2 * i, 2)], sems.at[i])
         for i, source in enumerate((first_slope, second_slope))
     ]
-    frames = [
-        pltpu.make_async_copy((first_stacked, second_stacked)[i // 2].at[i % 2], stacked_ref.at[i], sems.at[2 + i])
-        for i in range(SLOTS)
-    ]
-    for copy in slopes + frames:
+    for copy in slopes:
         copy.start()
     order = onehot(
         (64 * SLOTS, 16 * BLOCK),
@@ -304,17 +308,17 @@
 
         @pl.when(core == 1 - half)
         def _():
-            add_half(half, total_ref, grads_ref, stacked_ref, lambda slot: frames[slot].wait())
-
-
-def own_half_kernel(grads_ref, bias_ref, stacked_ref, total_ref):
+            add_half(half, total_ref, grads_ref, (first_stacked, second_stacked))
+
+
+def own_half_kernel(grads_ref, bias_ref, first_stacked, second_stacked, total_ref):
     total_ref[HALF:] = bias_ref[...]
     core = lax.axis_index("c")
     for half in range(2):
 
         @pl.when(core == half)
         def _():
-            add_half(half, total_ref, grads_ref, stacked_ref)
+            add_half(half, total_ref, grads_ref, (first_stacked, second_stacked))
 
 
 def share_kernel(tags_ref, mine_ref, got_ref, pooled_ref, message_ref):
@@ -454,35 +458,38 @@
 
 
 def forward(start, *operands):
-    pooled = ((2, 64, 128), jnp.float32) if start == 0 else ((8 * BLOCK, 128), jnp.bfloat16)
-    kept = pl.BlockSpec(memory_space=HBM)
+    in_hbm, in_vmem = pl.BlockSpec(memory_space=HBM), pl.BlockSpec(memory_space=pltpu.VMEM)
+    if start == 0:
+        pooled, pooled_spec = HBM((2, 64, 128), jnp.float32), in_hbm
+    else:
+        pooled, pooled_spec = jax.ShapeDtypeStruct((8 * BLOCK, 128), jnp.bfloat16), in_vmem
     return pl.pallas_call(
         functools.partial(forward_kernel, start),
         out_shape=[
-            jax.ShapeDtypeStruct(*pooled),
-            HBM((2, 9 * CH, FRAME), jnp.bfloat16),
+            pooled,
+            pltpu.VMEM((2, 9 * CH, FRAME), jnp.bfloat16),
             HBM((2, OUT, VOX), jnp.float32),
         ],
-        in_specs=[kept for _ in operands],
-        out_specs=[pl.BlockSpec(memory_space=pltpu.VMEM), kept, kept],
+        in_specs=[in_vmem if i in (4, 5) else in_hbm for i in range(len(operands))],
+        out_specs=[pooled_spec, in_vmem, in_hbm],
         scratch_shapes=[
             pltpu.VMEM((SLOTS, CH, VOX), jnp.bfloat16),
             pltpu.VMEM((SLOTS + 1, CH, VOX), jnp.float32),
             pltpu.VMEM((3 * SLOTS + 1, CH, 128), jnp.bfloat16),
-            pltpu.VMEM((2, 9 * CH, FRAME), jnp.bfloat16),
             pltpu.VMEM((2, OUT, VOX), jnp.float32),
             pltpu.VMEM((SLOTS, 64, 128), jnp.float32),
             pltpu.SMEM((SLOTS,), jnp.int32),
             pltpu.SMEM((SLOTS, 26), jnp.int32),
             pltpu.VMEM((1, OUT), jnp.float32),
+            pltpu.VMEM((TAP_ROWS, OUT), jnp.bfloat16),
             pltpu.VMEM((3 * OUT, 9 * CH), jnp.bfloat16),
             pltpu.SemaphoreType.DMA((8,)),
-            pltpu.SemaphoreType.DMA((4,)),
+            pltpu.SemaphoreType.DMA((3,)),
         ],
         compiler_params=pltpu.CompilerParams(vmem_limit_bytes=16 * 1024 * 1024),
         cost_estimate=pl.CostEstimate(flops=4_000_000_000, bytes_accessed=4_000_000, transcendentals=150_000),
         name="forward",
-    )(*[hbm(operand) for operand in operands])
+    )(*[operand if i in (4, 5) else hbm(operand) for i, operand in enumerate(operands)])
 
 
 def exchange(message, axis):
@@ -504,7 +511,7 @@
     before = lax.ppermute(layers, "b", [(i, i + 1) for i in range(BLOCK - 1)])
     after = lax.ppermute(layers, "b", [(i + 1, i) for i in range(BLOCK - 1)])
     offers = exchange(offer.reshape(BLOCK, 8, 128), "b")
-    weight = conv_weight.reshape(3, 9 * CH, OUT).transpose(0, 2, 1).reshape(3 * OUT, 9 * CH)
+    weight = conv_weight.reshape(TAP_ROWS, OUT)
     bias = convolution_bias_vector.reshape(1, OUT)
     first = forward(0, counts, neighbors, bias, features, before, after, weight)
     offers, first_dense = lax.optimization_barrier((offers.reshape(8 * BLOCK, 128), first[0]))
@@ -525,25 +532,21 @@
         (tags, adjoint, second[0]),
     )
     rows = exchange(message, "b").reshape(16 * BLOCK, 128)
-    other, grads, bias_part, stacked = call(
+    stacked = (vmem(first[1]), vmem(second[1]))
+    other, grads, bias_part = call(
         other_half_kernel,
         "other_half",
-        [
-            ((HALF + 8, OUT), wide, False),
-            ((SLOTS, OUT, VOX), narrow, True),
-            ((8, OUT), wide, True),
-            ((SLOTS, 9 * CH, FRAME), narrow, True),
-        ],
-        (first[1], second[1], first[2], second[2], rows),
-        in_hbm=4,
-        scratch=[pltpu.VMEM((SLOTS, OUT, VOX), jnp.float32), pltpu.SemaphoreType.DMA((2 + SLOTS,))],
+        [((HALF + 8, OUT), wide, False), ((SLOTS, OUT, VOX), narrow, True), ((8, OUT), wide, True)],
+        (first[2], second[2]) + stacked + (rows,),
+        in_hbm=2,
+        scratch=[pltpu.VMEM((SLOTS, OUT, VOX), jnp.float32), pltpu.SemaphoreType.DMA((2,))],
     )
     got = lax.ppermute(other, "c", [(0, 1), (1, 0)])
     (mine,) = call(
         own_half_kernel,
         "own_half",
         [((HALF + 8, OUT), wide, False)],
-        (vmem(grads), vmem(bias_part), vmem(stacked)),
+        (vmem(grads), vmem(bias_part)) + stacked,
         flops=2_000_000_000,
     )
     (message,) = call(share_kernel, "share", [((BLOCK, 32, 128), narrow, False)], (tags, mine, got, rows))

time: 137 us -> 132 us (0.964)
  blocking collectives: 56.4 us -> 51.7 us
  waiting for transfers between devices: 8.74 us -> 12.7 us
  local copies, waits for them, and re-layouts: 3.92 us -> 0.65 us
  Pallas kernels: 23.1 us -> 21.4 us
    all_to_all x3, blocking collectives: 44.4 us -> 40.1 us  [exchange(): return lax.all_to_all(message, axis, 0, 0, tiled=True)]
    all_to_all x3, waiting for transfers between devices: 7.9 us -> 11.7 us  [exchange(): return lax.all_to_all(message, axis, 0, 0, tiled=True)]
    reshape x1 -> x0, local copies, waits for them, and re-layouts: 2.02 us -> none  [per_device(): conv_weight.reshape(3, 9 * CH, OUT).transpose(0, 2, 1)]
  transfers between devices with their start and end apart: 7 -> 7, of which waited for: 4 -> 5; matrix products, arithmetic and copies ran while one was open for 2% -> 1% of each run, Pallas kernels for 9% -> 9%
where the time goes in v4:
time: 132 us; the launch traced here: 131 us
  blocking collectives  51.7 us (39%)
  starting transfers between devices  43.8 us (33%)
  Pallas kernels  21.4 us (16%)
  waiting for transfers between devices  12.7 us (10%)
    all_to_all x3, blocking collectives, exchange(): return lax.all_to_all(message, axis, 0, 0, tiled=True)  40.1 us
    all_to_all x3, starting transfers between devices, exchange(): return lax.all_to_all(message, axis, 0, 0, tiled=True)  29.5 us
    all_to_all x3, waiting for transfers between devices, exchange(): return lax.all_to_all(message, axis, 0, 0, tiled=True)  11.7 us
    pallas_call x9, Pallas kernels, call(): pl.pallas_call(kernel, out_shape=[pltpu.VMEM(shape, dtype) if kept else j...  10.9 us
    pallas_call x2, Pallas kernels, forward(): pl.pallas_call(functools.partial(forward_kernel, start), out_shape=[poole...  10.5 us
    all_gather x1, blocking collectives, per_device(): pieces = lax.all_gather(pieces, 'c', tiled=True)  5.86 us
    all_gather x1, blocking collectives, per_device(): adjoint = lax.all_gather(adjoint, 'c', tiled=True).reshape(64 * BLOCK, 128)  5.74 us
    ppermute x1, starting transfers between devices, per_device(): before = lax.ppermute(layers, 'b', [(i, i + 1) for i in range(BLOCK - 1)])  4.66 us
  transfers between devices with their start and end apart: 7, of which 5 were waited for; matrix products, arithmetic and copies ran while one was open for 1% of the time, Pallas kernels for 9%

profile of v4, /device:TPU:1, one launch (start us, length us, event | category | flops | bytes accessed | tf_op | source)
XLA Modules:
  0.0 131.0 jit_solution(2423759003570192403)
XLA Ops:
  0.6 1.8 %begin.1 = (bf16[4,64,128]{2,1,0:T(8,128)(2,1)S(1)}, bf16[256,128]{1,0:T(8,128)(2,1)}) custom-call(s32[4]{0:T(128)} %refs_0_.3, s32[4]{0:T(128)} %rebalance_hbm.1, s32[4]{0:T(128)} %owner_hbm.1, bf16[4,64,512]{2,1,0:T(8,128)(2,1)} %refs_3_.3, bf16[2,8192]{1,0:T(2,128)(2,1)} %adjoint_hbm.1), custom_call_target="tpu_custom_call" | custom-call | flops 1000000 | bytes 1000000 | tf_op jit(solution)/shard_map/begin/pallas_call | solution.py:424
  2.5 1.3 collective-permute-start.1
  3.8 4.7 %collective-permute-start = (bf16[4,64,128]{2,1,0:T(8,128)(2,1)S(1)}, bf16[4,64,128]{2,1,0:T(8,128)(2,1)S(1)}, u32[]{:S(2)}, u32[]{:S(2)}) collective-permute-start(bf16[4,64,128]{2,1,0:T(8,128)(2,1)S(1)} %get-tuple-element.26), channel_id=1, source_target_pairs={{0,1},{1,2},{2,3},{3,4},{4,5},{5,6},{6,7},{7,8},{8,9},{9,10},{10,1... | collective-permute-start | bytes 196616 | tf_op jit(solution)/shard_map/ppermute | solution.py:511
  8.4 9.8 %all-to-all-start = ((bf16[32,8,128]{2,1,0:T(8,128)(2,1)}), bf16[32,8,128]{2,1,0:T(8,128)(2,1)S(1)}, u32[]{:S(2)}, u32[]{:S(2)}) async-start(bf16[32,8,128]{2,1,0:T(8,128)(2,1)} %bitcast), calls=%async_computation | async-start | bytes 131072 | tf_op jit(solution)/shard_map/all_to_all | solution.py:496
  18.3 0.0 collective-permute-done.1.refs_5_
  18.3 0.0 collective-permute-done.refs_4_
  18.3 5.4 %forward.2 = (f32[2,64,128]{2,1,0:T(8,128)}, bf16[2,576,640]{2,1,0:T(8,128)(2,1)S(1)}, f32[2,128,512]{2,1,0:T(8,128)}) custom-call(s32[4]{0:T(128)} %refs_0_.3, s32[4,26]{1,0:T(4,128)} %refs_1_.3, f32[1,128]{1,0:T(1,128)} %bitcast.25, bf16[4,64,512]{2,1,0:T(8,128)(2,1)} %refs_3_.3, bf16[4,64,128]{2,1,0:T(8,128)(2,1)S(1)} %collective-permute-done.refs_4_, ...), custom_call_target="tpu_custom_call" | custom-call | flops 4000000000 | bytes 4000000 | tf_op jit(solution)/shard_map/forward/pallas_call | solution.py:466
  23.7 3.5 %all-to-all-done = bf16[32,8,128]{2,1,0:T(8,128)(2,1)S(1)} async-done(((bf16[32,8,128]{2,1,0:T(8,128)(2,1)}), bf16[32,8,128]{2,1,0:T(8,128)(2,1)S(1)}, u32[]{:S(2)}, u32[]{:S(2)}) %all-to-all-start) | async-done | bytes 65568 | tf_op jit(solution)/shard_map/all_to_all | solution.py:496
  27.2 0.9 spread.1
  28.1 10.0 %all-to-all-start.1 = ((bf16[8,128,128]{2,1,0:T(8,128)(2,1)}), bf16[8,128,128]{2,1,0:T(8,128)(2,1)S(1)}, u32[]{:S(2)}, u32[]{:S(2)}) async-start(bf16[8,128,128]{2,1,0:T(8,128)(2,1)} %get-tuple-element.37), calls=%async_computation.1 | async-start | bytes 524288 | tf_op jit(solution)/shard_map/all_to_all | solution.py:496
  38.2 5.1 %forward.3 = (bf16[256,128]{1,0:T(8,128)(2,1)S(1)}, bf16[2,576,640]{2,1,0:T(8,128)(2,1)S(1)}, f32[2,128,512]{2,1,0:T(8,128)}) custom-call(s32[4]{0:T(128)} %refs_0_.3, s32[4,26]{1,0:T(4,128)} %refs_1_.3, f32[1,128]{1,0:T(1,128)} %bitcast.26, bf16[4,64,512]{2,1,0:T(8,128)(2,1)} %refs_3_.3, bf16[4,64,128]{2,1,0:T(8,128)(2,1)S(1)} %collective-permute-done.refs_4_, ...), custom_call_target="tpu_custom_call" | custom-call | flops 4000000000 | bytes 4000000 | tf_op jit(solution)/shard_map/forward/pallas_call | solution.py:466
  43.2 4.3 %all-to-all-done.1 = bf16[8,128,128]{2,1,0:T(8,128)(2,1)S(1)} async-done(((bf16[8,128,128]{2,1,0:T(8,128)(2,1)}), bf16[8,128,128]{2,1,0:T(8,128)(2,1)S(1)}, u32[]{:S(2)}, u32[]{:S(2)}) %all-to-all-start.1) | async-done | bytes 262176 | tf_op jit(solution)/shard_map/all_to_all | solution.py:496
  47.5 5.7 %all_gather.6 = bf16[16,128,128]{2,1,0:T(8,128)(2,1)S(1)} all-gather(bf16[8,128,128]{2,1,0:T(8,128)(2,1)S(1)} %all-to-all-done.1), channel_id=1, replica_groups=mesh['z'=8,'c'=2,'b'=32] {'c'}, dimensions={0}, use_global_device_ids=true | all-gather | bytes 786432 | tf_op jit(solution)/shard_map/all_gather | solution.py:526
  53.3 0.6 choose.1
  53.9 14.2 %all_to_all.30 = bf16[32,16,128]{2,1,0:T(8,128)(2,1)S(1)} all-to-all(bf16[32,16,128]{2,1,0:T(8,128)(2,1)S(1)} %choose.1), channel_id=1, replica_groups=mesh['z'=8,'c'=2,'b'=32] {'b'}, dimensions={0} | all-to-all | bytes 262144 | tf_op jit(solution)/shard_map/all_to_all | solution.py:496
  68.1 3.4 %other_half.1 = (f32[872,128]{1,0:T(8,128)S(1)}, bf16[4,128,512]{2,1,0:T(8,128)(2,1)S(1)}, f32[8,128]{1,0:T(8,128)S(1)}) custom-call(f32[2,128,512]{2,1,0:T(8,128)} %get-tuple-element.30.first_slope, f32[2,128,512]{2,1,0:T(8,128)} %get-tuple-element.34.second_slope, bf16[2,576,640]{2,1,0:T(8,128)(2,1)S(1)} %get-tuple-element.35.first_stacked, ...), custom_call_target="tpu_custom_call" | custom-call | flops 1000000 | bytes 1000000 | tf_op jit(solution)/shard_map/other_half/pallas_call | solution.py:424
  71.5 4.1 %collective-permute-start.2 = (f32[872,128]{1,0:T(8,128)S(1)}, f32[872,128]{1,0:T(8,128)S(1)}, u32[]{:S(2)}, u32[]{:S(2)}) collective-permute-start(f32[872,128]{1,0:T(8,128)S(1)} %get-tuple-element.41), channel_id=1, source_target_pairs={{0,32},{32,0},{1,33},{33,1},{2,34},{34,2},{3,35},{35,3},{4,36},{36... | collective-permute-start | bytes 1339400 | tf_op jit(solution)/shard_map/ppermute | solution.py:544
  75.6 1.3 own_half.1.mine_ref
  76.9 0.1 collective-permute-done.2.got_ref
  77.0 0.5 share.1
  77.5 12.9 %all_to_all.31.pieces_ref = bf16[32,32,128]{2,1,0:T(8,128)(2,1)S(1)} all-to-all(bf16[32,32,128]{2,1,0:T(8,128)(2,1)S(1)} %share.1), channel_id=1, replica_groups=mesh['z'=8,'c'=2,'b'=32] {'b'}, dimensions={0} | all-to-all | bytes 524288 | tf_op jit(solution)/shard_map/all_to_all | solution.py:496
  90.4 0.3 over_block.1
  90.7 13.0 %all_to_all.32 = bf16[8,192,128]{2,1,0:T(8,128)(2,1)S(1)} all-to-all(bf16[8,192,128]{2,1,0:T(8,128)(2,1)S(1)} %bitcast.17), channel_id=1, replica_groups=mesh['z'=8,'c'=2,'b'=32] {'z'}, dimensions={0} | all-to-all | bytes 786432 | tf_op jit(solution)/shard_map/all_to_all | solution.py:496
  103.7 0.9 over_z.1
  104.6 9.6 %all-to-all-start.5 = ((bf16[32,32,128]{2,1,0:T(8,128)(2,1)}), bf16[32,32,128]{2,1,0:T(8,128)(2,1)S(1)}, u32[]{:S(2)}, u32[]{:S(2)}) async-start(bf16[32,32,128]{2,1,0:T(8,128)(2,1)} %get-tuple-element.44), calls=%async_computation.5 | async-start | bytes 524288 | tf_op jit(solution)/shard_map/all_to_all | solution.py:496
  114.3 4.3 %collective-permute-start.3 = (bf16[2,64,128]{2,1,0:T(8,128)(2,1)S(1)}, bf16[2,64,128]{2,1,0:T(8,128)(2,1)S(1)}, u32[]{:S(2)}, u32[]{:S(2)}) collective-permute-start(bf16[2,64,128]{2,1,0:T(8,128)(2,1)S(1)} %get-tuple-element.43), channel_id=1, source_target_pairs={{0,32},{32,0},{1,33},{33,1},{2,34},{34,2},{3,35},{35,3},{4,36},{36... | collective-permute-start | bytes 98312 | tf_op jit(solution)/shard_map/ppermute | solution.py:563
  118.6 0.8 collective-permute-done.3
  119.4 0.7 copy.13
  120.1 3.9 %all-to-all-done.5 = bf16[32,32,128]{2,1,0:T(8,128)(2,1)S(1)} async-done(((bf16[32,32,128]{2,1,0:T(8,128)(2,1)}), bf16[32,32,128]{2,1,0:T(8,128)(2,1)S(1)}, u32[]{:S(2)}, u32[]{:S(2)}) %all-to-all-start.5) | async-done | bytes 262176 | tf_op jit(solution)/shard_map/all_to_all | solution.py:496
  123.9 5.9 %all_gather.7.pieces_ref = bf16[64,32,128]{2,1,0:T(8,128)(2,1)S(1)} all-gather(bf16[32,32,128]{2,1,0:T(8,128)(2,1)S(1)} %all-to-all-done.5), channel_id=1, replica_groups=mesh['z'=8,'c'=2,'b'=32] {'c'}, dimensions={0}, use_global_device_ids=true | all-gather | bytes 786432 | tf_op jit(solution)/shard_map/all_gather | solution.py:564
  129.8 1.2 finish.1
  (1 shorter events, 0.0 us)
Async XLA Ops:
  2.5 15.8 %collective-permute-start.1 = (bf16[4,64,128]{2,1,0:T(8,128)(2,1)S(1)}, bf16[4,64,128]{2,1,0:T(8,128)(2,1)S(1)}, u32[]{:S(2)}, u32[]{:S(2)}) collective-permute-start(bf16[4,64,128]{2,1,0:T(8,128)(2,1)S(1)} %get-tuple-element.26), channel_id=1, source_target_pairs={{1,0},{2,1},{3,2},{4,3},{5,4},{6,5},{7,6},{8,7},{9,8},{10,9},{11,1... | collective-permute-start | bytes 196616 | tf_op jit(solution)/shard_map/ppermute | solution.py:512
  3.8 14.5 %collective-permute-start = (bf16[4,64,128]{2,1,0:T(8,128)(2,1)S(1)}, bf16[4,64,128]{2,1,0:T(8,128)(2,1)S(1)}, u32[]{:S(2)}, u32[]{:S(2)}) collective-permute-start(bf16[4,64,128]{2,1,0:T(8,128)(2,1)S(1)} %get-tuple-element.26), channel_id=1, source_target_pairs={{0,1},{1,2},{2,3},{3,4},{4,5},{5,6},{6,7},{7,8},{8,9},{9,10},{10,1... | collective-permute-start | bytes 196616 | tf_op jit(solution)/shard_map/ppermute | solution.py:511
  8.4 18.8 %all-to-all-start = ((bf16[32,8,128]{2,1,0:T(8,128)(2,1)}), bf16[32,8,128]{2,1,0:T(8,128)(2,1)S(1)}, u32[]{:S(2)}, u32[]{:S(2)}) async-start(bf16[32,8,128]{2,1,0:T(8,128)(2,1)} %bitcast), calls=%async_computation | async-start | bytes 131072 | tf_op jit(solution)/shard_map/all_to_all | solution.py:496
  28.1 19.4 %all-to-all-start.1 = ((bf16[8,128,128]{2,1,0:T(8,128)(2,1)}), bf16[8,128,128]{2,1,0:T(8,128)(2,1)S(1)}, u32[]{:S(2)}, u32[]{:S(2)}) async-start(bf16[8,128,128]{2,1,0:T(8,128)(2,1)} %get-tuple-element.37), calls=%async_computation.1 | async-start | bytes 524288 | tf_op jit(solution)/shard_map/all_to_all | solution.py:496
  71.5 5.5 %collective-permute-start.2 = (f32[872,128]{1,0:T(8,128)S(1)}, f32[872,128]{1,0:T(8,128)S(1)}, u32[]{:S(2)}, u32[]{:S(2)}) collective-permute-start(f32[872,128]{1,0:T(8,128)S(1)} %get-tuple-element.41), channel_id=1, source_target_pairs={{0,32},{32,0},{1,33},{33,1},{2,34},{34,2},{3,35},{35,3},{4,36},{36... | collective-permute-start | bytes 1339400 | tf_op jit(solution)/shard_map/ppermute | solution.py:544
  104.6 19.3 %all-to-all-start.5 = ((bf16[32,32,128]{2,1,0:T(8,128)(2,1)}), bf16[32,32,128]{2,1,0:T(8,128)(2,1)S(1)}, u32[]{:S(2)}, u32[]{:S(2)}) async-start(bf16[32,32,128]{2,1,0:T(8,128)(2,1)} %get-tuple-element.44), calls=%async_computation.5 | async-start | bytes 524288 | tf_op jit(solution)/shard_map/all_to_all | solution.py:496
  114.3 5.1 %collective-permute-start.3 = (bf16[2,64,128]{2,1,0:T(8,128)(2,1)S(1)}, bf16[2,64,128]{2,1,0:T(8,128)(2,1)S(1)}, u32[]{:S(2)}, u32[]{:S(2)}) collective-permute-start(bf16[2,64,128]{2,1,0:T(8,128)(2,1)S(1)} %get-tuple-element.43), channel_id=1, source_target_pairs={{0,32},{32,0},{1,33},{33,1},{2,34},{34,2},{3,35},{35,3},{4,36},{36... | collective-permute-start | bytes 98312 | tf_op jit(solution)/shard_map/ppermute | solution.py:563

commit v5 on v4

--- a/solution.py
+++ b/solution.py
@@ -9,6 +9,7 @@
 from jax.sharding import PartitionSpec as P
 
 SLOTS = 4
+FIRST = 1
 CH = 64
 OUT = 128
 VOX = 512
@@ -19,6 +20,7 @@
 MAIN = 24
 EXTRA = 3
 SHARE = MAIN + EXTRA
+ROWS = SHARE + 1
 HBM = pltpu.HBM
 EDGES = ((-1, -1), (-1, 0), (-1, 1), (0, -1), (0, 0), (0, 1), (1, -1), (1, 0), (1, 1))
 SMEM = pltpu.SMEM
@@ -110,11 +112,14 @@
     offer_ref[...] = bf16(jnp.where((rows & 7) == 4, tags, dot(order, bf16(dense_ref[...]))))
 
 
-def spread_kernel(offers_ref, message_ref, tags_ref):
-    offers = offers_ref[...]
-    message = bf16(dot(onehot((4 * BLOCK, 8 * BLOCK), lambda r, c: c == 8 * (r >> 2) + (r & 3)), offers))
-    message_ref[...] = jnp.broadcast_to(message[None], message_ref.shape)
-    tags_ref[...] = dot(onehot((BLOCK, 8 * BLOCK), lambda r, c: c == 8 * r + 4), offers).astype(jnp.int32)
+def spread_kernel(offers_ref, message_ref):
+    order = onehot((4 * BLOCK, 8 * BLOCK), lambda r, c: c == 8 * (r >> 2) + (r & 3))
+    message_ref[...] = jnp.broadcast_to(bf16(dot(order, offers_ref[...]))[None], message_ref.shape)
+
+
+def tags_kernel(offers_ref, tags_ref):
+    order = onehot((BLOCK, 8 * BLOCK), lambda r, c: c == 8 * r + 4)
+    tags_ref[...] = dot(order, offers_ref[...]).astype(jnp.int32)
 
 
 def place_of(tags_ref, row):
@@ -130,7 +135,8 @@
 
 
 def forward_kernel(start, *refs):
-    operands, refs = refs[: 7 + start // 2], refs[7 + start // 2 :]
+    given, count = (7, FIRST) if start == 0 else (8, SLOTS - FIRST)
+    operands, refs = refs[:given], refs[given:]
     pooled_out, stacked_ref, slope_hbm, features_ref, blocks_ref, rims_ref, slope_ref, dense_ref = refs[:8]
     counts_ref, neighbors_ref, bias_ref, taps_ref, weight_ref, sems, out_sems = refs[8:]
     targets = [
@@ -141,7 +147,7 @@
         rims_ref.at[pl.ds(0, SLOTS)],
         rims_ref.at[pl.ds(2 * SLOTS, SLOTS)],
         taps_ref,
-        dense_ref.at[pl.ds(0, 2)],
+        dense_ref.at[pl.ds(0, FIRST)],
     ]
     fetch(list(zip(operands, targets)), sems)
     for index in range(SLOTS):
@@ -165,7 +171,7 @@
     def moved(array, steps):
         return pltpu.roll(array, (-steps) % FRAME, 1)
 
-    @pl.loop(0, 2)
+    @pl.loop(0, count)
     def _(place):
         slot = start + place
 
@@ -221,10 +227,10 @@
         odd = dot(onehot((64, OUT), lambda r, c: c == 2 * r + 1), cells)
         dense_ref[start + place] = jnp.concatenate([even, odd], axis=1)
 
-    copies = [pltpu.make_async_copy(slope_ref.at[place], slope_hbm.at[place], out_sems.at[place]) for place in range(2)]
+    copies = [pltpu.make_async_copy(slope_ref.at[place], slope_hbm.at[place], out_sems.at[place]) for place in range(count)]
     if start == 0:
-        copies.append(pltpu.make_async_copy(dense_ref.at[pl.ds(0, 2)], pooled_out, out_sems.at[2]))
-        copies[2].start()
+        copies.append(pltpu.make_async_copy(dense_ref.at[pl.ds(0, FIRST)], pooled_out, out_sems.at[count]))
+        copies[count].start()
     else:
         order = onehot((8 * BLOCK, 64 * SLOTS), lambda r, c: c == 64 * ((r & 7) >> 1) + 2 * (r >> 3) + (r & 1))
         pooled_out[...] = bf16(dot(order, bf16(dense_ref[...].reshape(64 * SLOTS, 128))))
@@ -252,7 +258,7 @@
 def add_half(half, total_ref, grads_ref, stacked_refs):
     middle = HALF - 9 * CH
     for slot in range(SLOTS):
-        stacked_ref, place = stacked_refs[slot // 2], slot % 2
+        stacked_ref, place = (stacked_refs[0], slot) if slot < FIRST else (stacked_refs[1], slot - FIRST)
         grad = grads_ref[slot]
         wide = jnp.concatenate([grad.astype(jnp.float32), jnp.zeros((OUT, 128), jnp.float32)], axis=1)
         shifted = bf16(pltpu.roll(wide, 64, 1))
@@ -271,15 +277,7 @@
                 total_ref[low:high] += value
 
 
-def other_half_kernel(
-    first_slope, second_slope, first_stacked, second_stacked, rows_ref, total_ref, grads_ref, bias_ref, slope_ref, sems
-):
-    slopes = [
-        pltpu.make_async_copy(source, slope_ref.at[pl.ds(2 * i, 2)], sems.at[i])
-        for i, source in enumerate((first_slope, second_slope))
-    ]
-    for copy in slopes:
-        copy.start()
+def other_half_kernel(first_slope, second_slope, first_stacked, second_stacked, rows_ref, total_ref, grads_ref, bias_ref):
     order = onehot(
         (64 * SLOTS, 16 * BLOCK),
         lambda r, c: c == 16 * ((r & 63) >> 1) + 2 * (r >> 6) + (r & 1),
@@ -288,21 +286,16 @@
     table = pool_table(False)
     even = onehot((OUT, 64), lambda r, c: r == 2 * c)
     odd = onehot((OUT, 64), lambda r, c: r == 2 * c + 1)
-    ones = jnp.ones((8, VOX), jnp.bfloat16)
-    bias = jnp.zeros((8, OUT), jnp.float32)
+    bias = jnp.zeros((OUT, 1), jnp.float32)
     for slot in range(SLOTS):
         row = dense[64 * slot : 64 * (slot + 1)]
         cells = dot(even, row[:, :64]) + dot(odd, row[:, 64:])
-        spread = dot(bf16(cells), table)
-        if slot % 2 == 0:
-            slopes[slot // 2].wait()
-        grad = spread * slope_ref[slot]
-        rounded = bf16(grad)
-        rest = bf16(grad - rounded.astype(jnp.float32))
-        bias += dot_lanes(ones, rounded) + dot_lanes(ones, rest)
-        grads_ref[slot] = rounded
-    bias_ref[...] = bias
-    total_ref[HALF:] = bias
+        slope = first_slope[slot] if slot < FIRST else second_slope[slot - FIRST]
+        grad = dot(bf16(cells), table) * slope
+        bias += jnp.sum(grad, axis=1, keepdims=True)
+        grads_ref[slot] = bf16(grad)
+    rows, columns = grid_of((OUT, OUT))
+    bias_ref[...] = jnp.sum(jnp.where(rows == columns, bias, 0.0), axis=0, keepdims=True)
     core = lax.axis_index("c")
     for half in range(2):
 
@@ -311,8 +304,7 @@
             add_half(half, total_ref, grads_ref, (first_stacked, second_stacked))
 
 
-def own_half_kernel(grads_ref, bias_ref, first_stacked, second_stacked, total_ref):
-    total_ref[HALF:] = bias_ref[...]
+def own_half_kernel(grads_ref, first_stacked, second_stacked, total_ref):
     core = lax.axis_index("c")
     for half in range(2):
 
@@ -321,7 +313,7 @@
             add_half(half, total_ref, grads_ref, (first_stacked, second_stacked))
 
 
-def share_kernel(tags_ref, mine_ref, got_ref, pooled_ref, message_ref):
+def share_kernel(tags_ref, mine_ref, got_ref, bias_ref, pooled_ref, message_ref):
     total = mine_ref[...] + got_ref[...]
     tags = tags_ref[...].astype(jnp.float32)
     lines = dot_lanes(onehot((8, 128), lambda r, c: c == r), bf16(tags))
@@ -338,7 +330,7 @@
         (8 * BLOCK, EXTRA * BLOCK), lambda r, c: ((r & 7) < EXTRA) & (c == (r & 7) * BLOCK + (r >> 3))
     )
     tail += dot(extra, bf16(total[MAIN * BLOCK : HALF]))
-    bias = total[HALF : HALF + 1]
+    bias = bias_ref[...]
     high = bf16(bias).astype(jnp.float32)
     rows = lax.broadcasted_iota(jnp.int32, (8 * BLOCK, 128), 0)
     tail = jnp.where((rows & 7) == 7, jnp.where((rows & 8) == 0, high, bias - high), tail)
@@ -373,22 +365,30 @@
         message_ref[3 * (owners[row] >> 1) + 1 + (owners[row] & 1)] = pooled[64 * row : 64 * (row + 1)]
 
 
-def over_z_kernel(pieces_ref, message_ref, mine_ref, other_ref):
+def over_z_kernel(pieces_ref, message_ref):
     total = jnp.zeros((32, 128), jnp.float32)
-    pooled = [[jnp.zeros((64, 128), jnp.float32) for _ in range(2)] for _ in range(2)]
     for z in range(8):
         parts = pieces_ref[3 * z].astype(jnp.float32)
         total += parts[:32] + parts[32:]
+    rows = lax.broadcasted_iota(jnp.int32, (32, 128), 0)
+    bias = total[31:32]
+    high = bf16(bias).astype(jnp.float32)
+    part = jnp.where((lax.axis_index("b") & 2) == 0, high, bias - high)
+    tile = jnp.where(rows < SHARE, total, part)[:ROWS]
+    four = bf16(jnp.concatenate([tile] * 4, axis=0))
+    for index in range(BLOCK // 4):
+        message_ref[4 * ROWS * index : 4 * ROWS * (index + 1), :] = four
+
+
+def pick_kernel(pieces_ref, mine_ref, other_ref):
+    pooled = [[jnp.zeros((64, 128), jnp.float32) for _ in range(2)] for _ in range(2)]
+    for z in range(8):
+        tags = pieces_ref[3 * z, 16:32, :].astype(jnp.float32)
         for core in range(2):
-            tag = parts[28:29, core : core + 1]
+            tag = tags[12:13, core : core + 1]
             value = pieces_ref[3 * z + 1 + core].astype(jnp.float32)
             for row in range(2):
                 pooled[core][row] += jnp.where(tag == row + 1.0, value, 0.0)
-    rows = lax.broadcasted_iota(jnp.int32, (32, 128), 0)
-    bias = total[31:32]
-    high = bf16(bias).astype(jnp.float32)
-    tile = jnp.where(rows < SHARE, total, jnp.where(rows == 27, high, bias - high))
-    message_ref[...] = jnp.broadcast_to(bf16(tile)[None], (BLOCK, 32, 128))
     core = lax.axis_index("c")
     for row in range(2):
         mine_ref[row] = bf16(jnp.where(core == 0, pooled[0][row], pooled[1][row]))
@@ -396,17 +396,19 @@
 
 
 def finish_kernel(pieces_ref, weight_ref, bias_ref):
-    order = onehot((EXTRA * BLOCK, 32 * BLOCK), lambda r, c: c == 32 * (r & 31) + MAIN + (r >> 5))
+    order = onehot((EXTRA * BLOCK, ROWS * BLOCK), lambda r, c: c == ROWS * (r & 31) + MAIN + (r >> 5))
+    bias = []
     for half in range(2):
-        pieces = pieces_ref[half * BLOCK : (half + 1) * BLOCK]
+        pieces = pieces_ref[half * ROWS * BLOCK : (half + 1) * ROWS * BLOCK, :]
+        values = pieces.astype(jnp.float32)
         for device in range(BLOCK):
             start = half * HALF + device * MAIN
-            part = pieces_ref[half * BLOCK + device].astype(jnp.float32)
-            weight_ref[start : start + MAIN, :] = part[:MAIN]
+            weight_ref[start : start + MAIN, :] = values[ROWS * device : ROWS * device + MAIN]
         start = half * HALF + MAIN * BLOCK
-        weight_ref[start : start + EXTRA * BLOCK, :] = dot(order, pieces.reshape(32 * BLOCK, 128))
-    parts = [pieces_ref[device].astype(jnp.float32) for device in range(2)]
-    bias_ref[...] = parts[0][27:28] + parts[0][28:29] + (parts[1][27:28] + parts[1][28:29])
+        weight_ref[start : start + EXTRA * BLOCK, :] = dot(order, pieces)
+        parts = [values[ROWS * device + SHARE : ROWS * device + SHARE + 1] for device in range(4)]
+        bias.append(parts[0] + parts[2] + (parts[1] + parts[3]))
+    bias_ref[...] = bias[0] + bias[1]
 
 
 def hbm(array):
@@ -459,16 +461,17 @@
 
 def forward(start, *operands):
     in_hbm, in_vmem = pl.BlockSpec(memory_space=HBM), pl.BlockSpec(memory_space=pltpu.VMEM)
+    count = FIRST if start == 0 else SLOTS - FIRST
     if start == 0:
-        pooled, pooled_spec = HBM((2, 64, 128), jnp.float32), in_hbm
+        pooled, pooled_spec = HBM((FIRST, 64, 128), jnp.float32), in_hbm
     else:
         pooled, pooled_spec = jax.ShapeDtypeStruct((8 * BLOCK, 128), jnp.bfloat16), in_vmem
     return pl.pallas_call(
         functools.partial(forward_kernel, start),
         out_shape=[
             pooled,
-            pltpu.VMEM((2, 9 * CH, FRAME), jnp.bfloat16),
-            HBM((2, OUT, VOX), jnp.float32),
+            pltpu.VMEM((count, 9 * CH, FRAME), jnp.bfloat16),
+            HBM((count, OUT, VOX), jnp.float32),
         ],
         in_specs=[in_vmem if i in (4, 5) else in_hbm for i in range(len(operands))],
         out_specs=[pooled_spec, in_vmem, in_hbm],
@@ -476,7 +479,7 @@
             pltpu.VMEM((SLOTS, CH, VOX), jnp.bfloat16),
             pltpu.VMEM((SLOTS + 1, CH, VOX), jnp.float32),
             pltpu.VMEM((3 * SLOTS + 1, CH, 128), jnp.bfloat16),
-            pltpu.VMEM((2, OUT, VOX), jnp.float32),
+            pltpu.VMEM((count, OUT, VOX), jnp.float32),
             pltpu.VMEM((SLOTS, 64, 128), jnp.float32),
             pltpu.SMEM((SLOTS,), jnp.int32),
             pltpu.SMEM((SLOTS, 26), jnp.int32),
@@ -484,7 +487,7 @@
             pltpu.VMEM((TAP_ROWS, OUT), jnp.bfloat16),
             pltpu.VMEM((3 * OUT, 9 * CH), jnp.bfloat16),
             pltpu.SemaphoreType.DMA((8,)),
-            pltpu.SemaphoreType.DMA((3,)),
+            pltpu.SemaphoreType.DMA((count + 1,)),
         ],
         compiler_params=pltpu.CompilerParams(vmem_limit_bytes=16 * 1024 * 1024),
         cost_estimate=pl.CostEstimate(flops=4_000_000_000, bytes_accessed=4_000_000, transcendentals=150_000),
@@ -515,16 +518,12 @@
     bias = convolution_bias_vector.reshape(1, OUT)
     first = forward(0, counts, neighbors, bias, features, before, after, weight)
     offers, first_dense = lax.optimization_barrier((offers.reshape(8 * BLOCK, 128), first[0]))
-    message, tags = call(
-        spread_kernel,
-        "spread",
-        [((8, 4 * BLOCK, 128), narrow, False), ((BLOCK, 128), jnp.int32, False)],
-        (offers,),
-    )
+    (message,) = call(spread_kernel, "spread", [((8, 4 * BLOCK, 128), narrow, False)], (offers,))
     message, bias = lax.optimization_barrier((message, bias))
     adjoint = exchange(message, "z")
     adjoint = lax.all_gather(adjoint, "c", tiled=True).reshape(64 * BLOCK, 128)
-    second = forward(2, counts, neighbors, bias, features, before, after, weight, first_dense)
+    (tags,) = call(tags_kernel, "tags", [((BLOCK, 128), jnp.int32, False)], (offers,))
+    second = forward(FIRST, counts, neighbors, bias, features, before, after, weight, first_dense)
     (message,) = call(
         choose_kernel,
         "choose",
@@ -536,32 +535,30 @@
     other, grads, bias_part = call(
         other_half_kernel,
         "other_half",
-        [((HALF + 8, OUT), wide, False), ((SLOTS, OUT, VOX), narrow, True), ((8, OUT), wide, True)],
-        (first[2], second[2]) + stacked + (rows,),
-        in_hbm=2,
-        scratch=[pltpu.VMEM((SLOTS, OUT, VOX), jnp.float32), pltpu.SemaphoreType.DMA((2,))],
+        [((HALF, OUT), wide, False), ((SLOTS, OUT, VOX), narrow, True), ((1, OUT), wide, True)],
+        (vmem(first[2]), vmem(second[2])) + stacked + (rows,),
     )
     got = lax.ppermute(other, "c", [(0, 1), (1, 0)])
     (mine,) = call(
         own_half_kernel,
         "own_half",
-        [((HALF + 8, OUT), wide, False)],
-        (vmem(grads), vmem(bias_part)) + stacked,
+        [((HALF, OUT), wide, False)],
+        (vmem(grads),) + stacked,
         flops=2_000_000_000,
     )
-    (message,) = call(share_kernel, "share", [((BLOCK, 32, 128), narrow, False)], (tags, mine, got, rows))
+    (message,) = call(
+        share_kernel, "share", [((BLOCK, 32, 128), narrow, False)], (tags, mine, got, vmem(bias_part), rows)
+    )
     pieces = exchange(message, "b")
     (message,) = call(over_block_kernel, "over_block", [((24, 64, 128), narrow, False)], (tags, pieces))
     pieces = exchange(message.reshape(8, 192, 128), "z").reshape(24, 64, 128)
-    message, pooled_mine, pooled_other = call(
-        over_z_kernel,
-        "over_z",
-        [((BLOCK, 32, 128), narrow, False), ((2, CH, 128), narrow, False), ((2, CH, 128), narrow, False)],
-        (pieces,),
-    )
-    pieces = exchange(message, "b")
+    (message,) = call(over_z_kernel, "over_z", [((ROWS * BLOCK, 128), narrow, False)], (pieces,))
+    totals = exchange(message.reshape(BLOCK, ROWS // 2, 2, 128), "b")
+    pooled_mine, pooled_other = call(
+        pick_kernel, "pick", [((2, CH, 128), narrow, False), ((2, CH, 128), narrow, False)], (pieces,)
+    )
     pooled = pooled_mine + lax.ppermute(pooled_other, "c", [(0, 1), (1, 0)])
-    pieces = lax.all_gather(pieces, "c", tiled=True)
+    pieces = lax.all_gather(totals, "c", tiled=True).reshape(2 * ROWS * BLOCK, 128)
     weight_total, bias_total = call(
         finish_kernel, "finish", [((TAP_ROWS, OUT), wide, False), ((1, OUT), wide, False)], (pieces,)
     )

time: 132 us -> 130 us (0.985)
  waiting for transfers between devices: 12.7 us -> 11.3 us
    all_to_all x3, waiting for transfers between devices: 11.7 us -> 10.3 us  [exchange(): return lax.all_to_all(message, axis, 0, 0, tiled=True)]
    pallas_call x9 -> x11, Pallas kernels: 10.9 us -> 9.91 us  [call(): pl.pallas_call(kernel, out_shape=[pltpu.VMEM(shape, dtype) if kept else j...]
where the time goes in v5:
time: 130 us; the launch traced here: 129 us
  blocking collectives  51.6 us (40%)
  starting transfers between devices  43.7 us (34%)
  Pallas kernels  20.3 us (16%)
  waiting for transfers between devices  11.3 us (9%)
  local copies, waits for them, and re-layouts  1.54 us (1%)
    all_to_all x3, blocking collectives, exchange(): return lax.all_to_all(message, axis, 0, 0, tiled=True)  39.8 us
    all_to_all x3, starting transfers between devices, exchange(): return lax.all_to_all(message, axis, 0, 0, tiled=True)  29.1 us
    pallas_call x2, Pallas kernels, forward(): pl.pallas_call(functools.partial(forward_kernel, start), out_shape=[poole...  10.4 us
    all_to_all x3, waiting for transfers between devices, exchange(): return lax.all_to_all(message, axis, 0, 0, tiled=True)  10.3 us
    pallas_call x11, Pallas kernels, call(): pl.pallas_call(kernel, out_shape=[pltpu.VMEM(shape, dtype) if kept else j...  9.91 us
    all_gather x1, blocking collectives, per_device(): adjoint = lax.all_gather(adjoint, 'c', tiled=True).reshape(64 * BLOCK, 128)  6.08 us
    all_gather x1, blocking collectives, per_device(): lax.all_gather(totals, 'c', tiled=True).reshape(2 * ROWS * BLOCK, 128)  5.72 us
    ppermute x1, starting transfers between devices, per_device(): before = lax.ppermute(layers, 'b', [(i, i + 1) for i in range(BLOCK - 1)])  4.66 us
  transfers between devices with their start and end apart: 7, of which 5 were waited for; matrix products, arithmetic and copies ran while one was open for 1% of the time, Pallas kernels for 9%

profile of v5, /device:TPU:1, one launch (start us, length us, event | category | flops | bytes accessed | tf_op | source)
XLA Modules:
  0.0 129.2 jit_solution(2551266206828326130)
XLA Ops:
  0.6 1.8 %begin.1 = (bf16[4,64,128]{2,1,0:T(8,128)(2,1)S(1)}, bf16[256,128]{1,0:T(8,128)(2,1)}) custom-call(s32[4]{0:T(128)} %refs_0_.3, s32[4]{0:T(128)} %rebalance_hbm.1, s32[4]{0:T(128)} %owner_hbm.1, bf16[4,64,512]{2,1,0:T(8,128)(2,1)} %refs_3_.3, bf16[2,8192]{1,0:T(2,128)(2,1)} %adjoint_hbm.1), custom_call_target="tpu_custom_call" | custom-call | flops 1000000 | bytes 1000000 | tf_op jit(solution)/shard_map/begin/pallas_call | solution.py:426
  2.5 1.3 %collective-permute-start.1 = (bf16[4,64,128]{2,1,0:T(8,128)(2,1)S(1)}, bf16[4,64,128]{2,1,0:T(8,128)(2,1)S(1)}, u32[]{:S(2)}, u32[]{:S(2)}) collective-permute-start(bf16[4,64,128]{2,1,0:T(8,128)(2,1)S(1)} %get-tuple-element.23), channel_id=1, source_target_pairs={{1,0},{2,1},{3,2},{4,3},{5,4},{6,5},{7,6},{8,7},{9,8},{10,9},{11,1... | collective-permute-start | bytes 196616 | tf_op jit(solution)/shard_map/ppermute | solution.py:515
  3.8 4.7 %collective-permute-start = (bf16[4,64,128]{2,1,0:T(8,128)(2,1)S(1)}, bf16[4,64,128]{2,1,0:T(8,128)(2,1)S(1)}, u32[]{:S(2)}, u32[]{:S(2)}) collective-permute-start(bf16[4,64,128]{2,1,0:T(8,128)(2,1)S(1)} %get-tuple-element.23), channel_id=1, source_target_pairs={{0,1},{1,2},{2,3},{3,4},{4,5},{5,6},{6,7},{7,8},{8,9},{9,10},{10,1... | collective-permute-start | bytes 196616 | tf_op jit(solution)/shard_map/ppermute | solution.py:514
  8.4 9.8 %all-to-all-start = ((bf16[32,8,128]{2,1,0:T(8,128)(2,1)}), bf16[32,8,128]{2,1,0:T(8,128)(2,1)S(1)}, u32[]{:S(2)}, u32[]{:S(2)}) async-start(bf16[32,8,128]{2,1,0:T(8,128)(2,1)} %bitcast), calls=%async_computation | async-start | bytes 131072 | tf_op jit(solution)/shard_map/all_to_all | solution.py:499
  18.3 3.7 %forward.2 = (f32[1,64,128]{2,1,0:T(8,128)}, bf16[1,576,640]{2,1,0:T(8,128)(2,1)S(1)}, f32[1,128,512]{2,1,0:T(8,128)}) custom-call(s32[4]{0:T(128)} %refs_0_.3, s32[4,26]{1,0:T(4,128)} %refs_1_.3, f32[1,128]{1,0:T(1,128)} %bitcast.30, bf16[4,64,512]{2,1,0:T(8,128)(2,1)} %refs_3_.3, bf16[4,64,128]{2,1,0:T(8,128)(2,1)S(1)} %collective-permute-done.refs_4_, ...), custom_call_target="tpu_custom_call" | custom-call | flops 4000000000 | bytes 4000000 | tf_op jit(solution)/shard_map/forward/pallas_call | solution.py:469
  22.0 0.9 copy-done.1
  22.9 4.3 %all-to-all-done = bf16[32,8,128]{2,1,0:T(8,128)(2,1)S(1)} async-done(((bf16[32,8,128]{2,1,0:T(8,128)(2,1)}), bf16[32,8,128]{2,1,0:T(8,128)(2,1)S(1)}, u32[]{:S(2)}, u32[]{:S(2)}) %all-to-all-start) | async-done | bytes 65568 | tf_op jit(solution)/shard_map/all_to_all | solution.py:499
  27.2 0.9 spread.1
  28.1 10.0 %all-to-all-start.1 = ((bf16[8,128,128]{2,1,0:T(8,128)(2,1)}), bf16[8,128,128]{2,1,0:T(8,128)(2,1)}, u32[]{:S(2)}, u32[]{:S(2)}) async-start(bf16[8,128,128]{2,1,0:T(8,128)(2,1)} %spread.1), calls=%async_computation.1 | async-start | bytes 524288 | tf_op jit(solution)/shard_map/all_to_all | solution.py:499
  38.1 0.1 tags.1.tags_ref
  38.3 6.7 %forward.3 = (bf16[256,128]{1,0:T(8,128)(2,1)S(1)}, bf16[3,576,640]{2,1,0:T(8,128)(2,1)S(1)}, f32[3,128,512]{2,1,0:T(8,128)}) custom-call(s32[4]{0:T(128)} %refs_0_.3, s32[4,26]{1,0:T(4,128)} %refs_1_.3, f32[1,128]{1,0:T(1,128)} %bitcast.31, bf16[4,64,512]{2,1,0:T(8,128)(2,1)} %refs_3_.3, bf16[4,64,128]{2,1,0:T(8,128)(2,1)S(1)} %collective-permute-done.refs_4_, ...), custom_call_target="tpu_custom_call" | custom-call | flops 4000000000 | bytes 4000000 | tf_op jit(solution)/shard_map/forward/pallas_call | solution.py:469
  45.0 2.7 %all-to-all-done.1 = bf16[8,128,128]{2,1,0:T(8,128)(2,1)} async-done(((bf16[8,128,128]{2,1,0:T(8,128)(2,1)}), bf16[8,128,128]{2,1,0:T(8,128)(2,1)}, u32[]{:S(2)}, u32[]{:S(2)}) %all-to-all-start.1) | async-done | bytes 262176 | tf_op jit(solution)/shard_map/all_to_all | solution.py:499
  47.6 6.1 %all_gather.6 = bf16[16,128,128]{2,1,0:T(8,128)(2,1)S(1)} all-gather(bf16[8,128,128]{2,1,0:T(8,128)(2,1)} %all-to-all-done.1), channel_id=1, replica_groups=mesh['z'=8,'c'=2,'b'=32] {'c'}, dimensions={0}, use_global_device_ids=true | all-gather | bytes 786432 | tf_op jit(solution)/shard_map/all_gather | solution.py:524
  53.7 0.6 choose.1
  54.4 13.3 %all_to_all.30 = bf16[32,16,128]{2,1,0:T(8,128)(2,1)S(1)} all-to-all(bf16[32,16,128]{2,1,0:T(8,128)(2,1)S(1)} %choose.1), channel_id=1, replica_groups=mesh['z'=8,'c'=2,'b'=32] {'b'}, dimensions={0} | all-to-all | bytes 262144 | tf_op jit(solution)/shard_map/all_to_all | solution.py:499
  67.7 2.3 %other_half.1 = (f32[864,128]{1,0:T(8,128)S(1)}, bf16[4,128,512]{2,1,0:T(8,128)(2,1)S(1)}, f32[1,128]{1,0:T(1,128)S(1)}) custom-call(f32[1,128,512]{2,1,0:T(8,128)S(1)} %copy-done.3, f32[3,128,512]{2,1,0:T(8,128)S(1)} %copy-done, bf16[1,576,640]{2,1,0:T(8,128)(2,1)S(1)} %copy-done.2, bf16[3,576,640]{2,1,0:T(8,128)(2,1)S(1)} %get-tuple-element.31.second_stacked, ...), custom_call_target="tpu_custom_call" | custom-call | flops 1000000 | bytes 1000000 | tf_op jit(solution)/shard_map/other_half/pallas_call | solution.py:426
  70.1 4.1 %collective-permute-start.2 = (f32[864,128]{1,0:T(8,128)S(1)}, f32[864,128]{1,0:T(8,128)S(1)}, u32[]{:S(2)}, u32[]{:S(2)}) collective-permute-start(f32[864,128]{1,0:T(8,128)S(1)} %get-tuple-element.35), channel_id=1, source_target_pairs={{0,32},{32,0},{1,33},{33,1},{2,34},{34,2},{3,35},{35,3},{4,36},{36... | collective-permute-start | bytes 1327112 | tf_op jit(solution)/shard_map/ppermute | solution.py:541
  74.2 1.3 own_half.1.mine_ref
  75.4 0.1 collective-permute-done.2.got_ref
  75.6 0.5 share.1
  76.0 12.9 %all_to_all.31.pieces_ref = bf16[32,32,128]{2,1,0:T(8,128)(2,1)S(1)} all-to-all(bf16[32,32,128]{2,1,0:T(8,128)(2,1)S(1)} %share.1), channel_id=1, replica_groups=mesh['z'=8,'c'=2,'b'=32] {'b'}, dimensions={0} | all-to-all | bytes 524288 | tf_op jit(solution)/shard_map/all_to_all | solution.py:499
  89.0 0.3 over_block.1
  89.2 13.5 %all_to_all.32 = bf16[8,192,128]{2,1,0:T(8,128)(2,1)S(1)} all-to-all(bf16[8,192,128]{2,1,0:T(8,128)(2,1)S(1)} %bitcast.21), channel_id=1, replica_groups=mesh['z'=8,'c'=2,'b'=32] {'z'}, dimensions={0} | all-to-all | bytes 786432 | tf_op jit(solution)/shard_map/all_to_all | solution.py:499
  102.7 0.7 over_z.1
  103.5 9.3 %all-to-all-start.5 = ((bf16[32,14,2,128]{3,2,1,0:T(2,128)(2,1)}), bf16[32,14,2,128]{3,2,1,0:T(2,128)(2,1)S(1)}, u32[]{:S(2)}, u32[]{:S(2)}) async-start(bf16[32,14,2,128]{3,2,1,0:T(2,128)(2,1)} %bitcast.8), calls=%async_computation.5 | async-start | bytes 458752 | tf_op jit(solution)/shard_map/all_to_all | solution.py:499
  112.7 0.2 pick.1
  113.0 4.5 %collective-permute-start.3 = (bf16[2,64,128]{2,1,0:T(8,128)(2,1)S(1)}, bf16[2,64,128]{2,1,0:T(8,128)(2,1)S(1)}, u32[]{:S(2)}, u32[]{:S(2)}) collective-permute-start(bf16[2,64,128]{2,1,0:T(8,128)(2,1)S(1)} %get-tuple-element.38), channel_id=1, source_target_pairs={{0,32},{32,0},{1,33},{33,1},{2,34},{34,2},{3,35},{35,3},{4,36},{36... | collective-permute-start | bytes 98312 | tf_op jit(solution)/shard_map/ppermute | solution.py:560
  117.5 0.8 collective-permute-done.3
  118.3 0.7 copy.13
  119.0 3.3 %all-to-all-done.5 = bf16[32,14,2,128]{3,2,1,0:T(2,128)(2,1)S(1)} async-done(((bf16[32,14,2,128]{3,2,1,0:T(2,128)(2,1)}), bf16[32,14,2,128]{3,2,1,0:T(2,128)(2,1)S(1)}, u32[]{:S(2)}, u32[]{:S(2)}) %all-to-all-start.5) | async-done | bytes 229408 | tf_op jit(solution)/shard_map/all_to_all | solution.py:499
  122.3 5.7 %all_gather.7 = bf16[64,14,2,128]{3,2,1,0:T(2,128)(2,1)S(1)} all-gather(bf16[32,14,2,128]{3,2,1,0:T(2,128)(2,1)S(1)} %all-to-all-done.5), channel_id=1, replica_groups=mesh['z'=8,'c'=2,'b'=32] {'c'}, dimensions={0}, use_global_device_ids=true | all-gather | bytes 688128 | tf_op jit(solution)/shard_map/all_gather | solution.py:561
  128.0 1.2 finish.1
  (10 shorter events, 0.0 us)
Async XLA Ops:
  2.5 15.8 %collective-permute-start.1 = (bf16[4,64,128]{2,1,0:T(8,128)(2,1)S(1)}, bf16[4,64,128]{2,1,0:T(8,128)(2,1)S(1)}, u32[]{:S(2)}, u32[]{:S(2)}) collective-permute-start(bf16[4,64,128]{2,1,0:T(8,128)(2,1)S(1)} %get-tuple-element.23), channel_id=1, source_target_pairs={{1,0},{2,1},{3,2},{4,3},{5,4},{6,5},{7,6},{8,7},{9,8},{10,9},{11,1... | collective-permute-start | bytes 196616 | tf_op jit(solution)/shard_map/ppermute | solution.py:515
  3.8 14.5 %collective-permute-start = (bf16[4,64,128]{2,1,0:T(8,128)(2,1)S(1)}, bf16[4,64,128]{2,1,0:T(8,128)(2,1)S(1)}, u32[]{:S(2)}, u32[]{:S(2)}) collective-permute-start(bf16[4,64,128]{2,1,0:T(8,128)(2,1)S(1)} %get-tuple-element.23), channel_id=1, source_target_pairs={{0,1},{1,2},{2,3},{3,4},{4,5},{5,6},{6,7},{7,8},{8,9},{9,10},{10,1... | collective-permute-start | bytes 196616 | tf_op jit(solution)/shard_map/ppermute | solution.py:514
  8.4 18.8 %all-to-all-start = ((bf16[32,8,128]{2,1,0:T(8,128)(2,1)}), bf16[32,8,128]{2,1,0:T(8,128)(2,1)S(1)}, u32[]{:S(2)}, u32[]{:S(2)}) async-start(bf16[32,8,128]{2,1,0:T(8,128)(2,1)} %bitcast), calls=%async_computation | async-start | bytes 131072 | tf_op jit(solution)/shard_map/all_to_all | solution.py:499
  22.0 0.9 copy-start.1
  28.1 19.5 %all-to-all-start.1 = ((bf16[8,128,128]{2,1,0:T(8,128)(2,1)}), bf16[8,128,128]{2,1,0:T(8,128)(2,1)}, u32[]{:S(2)}, u32[]{:S(2)}) async-start(bf16[8,128,128]{2,1,0:T(8,128)(2,1)} %spread.1), calls=%async_computation.1 | async-start | bytes 524288 | tf_op jit(solution)/shard_map/all_to_all | solution.py:499
  38.3 29.4 %copy-start.3 = (f32[1,128,512]{2,1,0:T(8,128)S(1)}, f32[1,128,512]{2,1,0:T(8,128)}, u32[]{:S(2)}) copy-start(f32[1,128,512]{2,1,0:T(8,128)} %get-tuple-element.26.first_slope) | copy-start | bytes 786436
  45.0 22.8 %copy-start = (f32[3,128,512]{2,1,0:T(8,128)S(1)}, f32[3,128,512]{2,1,0:T(8,128)}, u32[]{:S(2)}) copy-start(f32[3,128,512]{2,1,0:T(8,128)} %get-tuple-element.29.second_slope) | copy-start | bytes 2359300
  47.6 20.1 %copy-start.2 = (bf16[1,576,640]{2,1,0:T(8,128)(2,1)S(1)}, bf16[1,576,640]{2,1,0:T(8,128)(2,1)}, u32[]{:S(2)}) copy-start(bf16[1,576,640]{2,1,0:T(8,128)(2,1)} %copy-done.1) | copy-start | bytes 2211844
  70.1 5.5 %collective-permute-start.2 = (f32[864,128]{1,0:T(8,128)S(1)}, f32[864,128]{1,0:T(8,128)S(1)}, u32[]{:S(2)}, u32[]{:S(2)}) collective-permute-start(f32[864,128]{1,0:T(8,128)S(1)} %get-tuple-element.35), channel_id=1, source_target_pairs={{0,32},{32,0},{1,33},{33,1},{2,34},{34,2},{3,35},{35,3},{4,36},{36... | collective-permute-start | bytes 1327112 | tf_op jit(solution)/shard_map/ppermute | solution.py:541
  103.5 18.8 %all-to-all-start.5 = ((bf16[32,14,2,128]{3,2,1,0:T(2,128)(2,1)}), bf16[32,14,2,128]{3,2,1,0:T(2,128)(2,1)S(1)}, u32[]{:S(2)}, u32[]{:S(2)}) async-start(bf16[32,14,2,128]{3,2,1,0:T(2,128)(2,1)} %bitcast.8), calls=%async_computation.5 | async-start | bytes 458752 | tf_op jit(solution)/shard_map/all_to_all | solution.py:499
  113.0 5.3 %collective-permute-start.3 = (bf16[2,64,128]{2,1,0:T(8,128)(2,1)S(1)}, bf16[2,64,128]{2,1,0:T(8,128)(2,1)S(1)}, u32[]{:S(2)}, u32[]{:S(2)}) collective-permute-start(bf16[2,64,128]{2,1,0:T(8,128)(2,1)S(1)} %get-tuple-element.38), channel_id=1, source_target_pairs={{0,32},{32,0},{1,33},{33,1},{2,34},{34,2},{3,35},{35,3},{4,36},{36... | collective-permute-start | bytes 98312 | tf_op jit(solution)/shard_map/ppermute | solution.py:560

commit v6 on v5

--- a/solution.py
+++ b/solution.py
@@ -137,8 +137,9 @@
 def forward_kernel(start, *refs):
     given, count = (7, FIRST) if start == 0 else (8, SLOTS - FIRST)
     operands, refs = refs[:given], refs[given:]
-    pooled_out, stacked_ref, slope_hbm, features_ref, blocks_ref, rims_ref, slope_ref, dense_ref = refs[:8]
-    counts_ref, neighbors_ref, bias_ref, taps_ref, weight_ref, sems, out_sems = refs[8:]
+    pooled_out, stacked_out, slope_hbm, features_ref, blocks_ref, rims_ref, slope_ref, dense_ref = refs[:8]
+    counts_ref, neighbors_ref, bias_ref, taps_ref, weight_ref, sems, out_sems = refs[8:15]
+    stacked_ref = refs[15] if start == 0 else stacked_out
     targets = [
         counts_ref,
         neighbors_ref,
@@ -210,6 +211,8 @@
                 value = jnp.where(at_b == 7, moved(along_c[1, ec], -56), moved(along_c[0, ec], 8))
             stacked_ref[place, index * CH : (index + 1) * CH, :] = value.astype(jnp.bfloat16)
 
+        if start == 0:
+            pltpu.make_async_copy(stacked_ref.at[place], stacked_out.at[place], out_sems.at[count + 1 + place]).start()
         product = dot(weight_ref[...], stacked_ref[place])
         middle = pltpu.roll(product[OUT : 2 * OUT], FRAME - 64, 1)[:, :VOX]
         preact = product[:OUT, :VOX] + middle + product[2 * OUT :, 128:] + bias
@@ -231,6 +234,10 @@
     if start == 0:
         copies.append(pltpu.make_async_copy(dense_ref.at[pl.ds(0, FIRST)], pooled_out, out_sems.at[count]))
         copies[count].start()
+        copies += [
+            pltpu.make_async_copy(stacked_ref.at[place], stacked_out.at[place], out_sems.at[count + 1 + place])
+            for place in range(count)
+        ]
     else:
         order = onehot((8 * BLOCK, 64 * SLOTS), lambda r, c: c == 64 * ((r & 7) >> 1) + 2 * (r >> 3) + (r & 1))
         pooled_out[...] = bf16(dot(order, bf16(dense_ref[...].reshape(64 * SLOTS, 128))))
@@ -470,11 +477,11 @@
         functools.partial(forward_kernel, start),
         out_shape=[
             pooled,
-            pltpu.VMEM((count, 9 * CH, FRAME), jnp.bfloat16),
+            (HBM if start == 0 else pltpu.VMEM)((count, 9 * CH, FRAME), jnp.bfloat16),
             HBM((count, OUT, VOX), jnp.float32),
         ],
         in_specs=[in_vmem if i in (4, 5) else in_hbm for i in range(len(operands))],
-        out_specs=[pooled_spec, in_vmem, in_hbm],
+        out_specs=[pooled_spec, in_hbm if start == 0 else in_vmem, in_hbm],
         scratch_shapes=[
             pltpu.VMEM((SLOTS, CH, VOX), jnp.bfloat16),
             pltpu.VMEM((SLOTS + 1, CH, VOX), jnp.float32),
@@ -487,8 +494,9 @@
             pltpu.VMEM((TAP_ROWS, OUT), jnp.bfloat16),
             pltpu.VMEM((3 * OUT, 9 * CH), jnp.bfloat16),
             pltpu.SemaphoreType.DMA((8,)),
-            pltpu.SemaphoreType.DMA((count + 1,)),
-        ],
+            pltpu.SemaphoreType.DMA((2 * count + 1,)),
+        ]
+        + [pltpu.VMEM((count, 9 * CH, FRAME), jnp.bfloat16) for _ in range(start == 0)],
         compiler_params=pltpu.CompilerParams(vmem_limit_bytes=16 * 1024 * 1024),
         cost_estimate=pl.CostEstimate(flops=4_000_000_000, bytes_accessed=4_000_000, transcendentals=150_000),
         name="forward",

time: 130 us -> 129 us (level)
  no operation moved by 1% of the time
where the time goes in v6:
time: 129 us; the launch traced here: 128 us
  blocking collectives  50.7 us (39%)
  starting transfers between devices  43.7 us (34%)
  Pallas kernels  20.3 us (16%)
  waiting for transfers between devices  12.1 us (9%)
    all_to_all x3, blocking collectives, exchange(): return lax.all_to_all(message, axis, 0, 0, tiled=True)  38.9 us
    all_to_all x3, starting transfers between devices, exchange(): return lax.all_to_all(message, axis, 0, 0, tiled=True)  29.1 us
    all_to_all x3, waiting for transfers between devices, exchange(): return lax.all_to_all(message, axis, 0, 0, tiled=True)  11.2 us
    pallas_call x2, Pallas kernels, forward(): pl.pallas_call(functools.partial(forward_kernel, start), out_shape=[poole...  10.4 us
    pallas_call x11, Pallas kernels, call(): pl.pallas_call(kernel, out_shape=[pltpu.VMEM(shape, dtype) if kept else j...  9.91 us
    all_gather x1, blocking collectives, per_device(): adjoint = lax.all_gather(adjoint, 'c', tiled=True).reshape(64 * BLOCK, 128)  6.08 us
    all_gather x1, blocking collectives, per_device(): lax.all_gather(totals, 'c', tiled=True).reshape(2 * ROWS * BLOCK, 128)  5.72 us
    ppermute x1, starting transfers between devices, per_device(): before = lax.ppermute(layers, 'b', [(i, i + 1) for i in range(BLOCK - 1)])  4.66 us
  transfers between devices with their start and end apart: 7, of which 5 were waited for; matrix products, arithmetic and copies ran while one was open for 1% of the time, Pallas kernels for 9%

profile of v6, /device:TPU:1, one launch (start us, length us, event | category | flops | bytes accessed | tf_op | source)
XLA Modules:
  0.0 128.3 jit_solution(15444543736855886475)
XLA Ops:
  0.6 1.8 %begin.1 = (bf16[4,64,128]{2,1,0:T(8,128)(2,1)S(1)}, bf16[256,128]{1,0:T(8,128)(2,1)}) custom-call(s32[4]{0:T(128)} %refs_0_.3, s32[4]{0:T(128)} %rebalance_hbm.1, s32[4]{0:T(128)} %owner_hbm.1, bf16[4,64,512]{2,1,0:T(8,128)(2,1)} %refs_3_.3, bf16[2,8192]{1,0:T(2,128)(2,1)} %adjoint_hbm.1), custom_call_target="tpu_custom_call" | custom-call | flops 1000000 | bytes 1000000 | tf_op jit(solution)/shard_map/begin/pallas_call | solution.py:433
  2.5 1.3 %collective-permute-start.1 = (bf16[4,64,128]{2,1,0:T(8,128)(2,1)S(1)}, bf16[4,64,128]{2,1,0:T(8,128)(2,1)S(1)}, u32[]{:S(2)}, u32[]{:S(2)}) collective-permute-start(bf16[4,64,128]{2,1,0:T(8,128)(2,1)S(1)} %get-tuple-element.23), channel_id=1, source_target_pairs={{1,0},{2,1},{3,2},{4,3},{5,4},{6,5},{7,6},{8,7},{9,8},{10,9},{11,1... | collective-permute-start | bytes 196616 | tf_op jit(solution)/shard_map/ppermute | solution.py:523
  3.8 4.7 %collective-permute-start = (bf16[4,64,128]{2,1,0:T(8,128)(2,1)S(1)}, bf16[4,64,128]{2,1,0:T(8,128)(2,1)S(1)}, u32[]{:S(2)}, u32[]{:S(2)}) collective-permute-start(bf16[4,64,128]{2,1,0:T(8,128)(2,1)S(1)} %get-tuple-element.23), channel_id=1, source_target_pairs={{0,1},{1,2},{2,3},{3,4},{4,5},{5,6},{6,7},{7,8},{8,9},{9,10},{10,1... | collective-permute-start | bytes 196616 | tf_op jit(solution)/shard_map/ppermute | solution.py:522
  8.4 9.8 %all-to-all-start = ((bf16[32,8,128]{2,1,0:T(8,128)(2,1)}), bf16[32,8,128]{2,1,0:T(8,128)(2,1)S(1)}, u32[]{:S(2)}, u32[]{:S(2)}) async-start(bf16[32,8,128]{2,1,0:T(8,128)(2,1)} %bitcast), calls=%async_computation | async-start | bytes 131072 | tf_op jit(solution)/shard_map/all_to_all | solution.py:507
  18.3 3.7 %forward.2 = (f32[1,64,128]{2,1,0:T(8,128)}, bf16[1,576,640]{2,1,0:T(8,128)(2,1)}, f32[1,128,512]{2,1,0:T(8,128)}) custom-call(s32[4]{0:T(128)} %refs_0_.3, s32[4,26]{1,0:T(4,128)} %refs_1_.3, f32[1,128]{1,0:T(1,128)} %bitcast.30, bf16[4,64,512]{2,1,0:T(8,128)(2,1)} %refs_3_.3, bf16[4,64,128]{2,1,0:T(8,128)(2,1)S(1)} %collective-permute-done.refs_4_, ...), custom_call_target="tpu_custom_call" | custom-call | flops 4000000000 | bytes 4000000 | tf_op jit(solution)/shard_map/forward/pallas_call | solution.py:476
  22.0 5.2 %all-to-all-done = bf16[32,8,128]{2,1,0:T(8,128)(2,1)S(1)} async-done(((bf16[32,8,128]{2,1,0:T(8,128)(2,1)}), bf16[32,8,128]{2,1,0:T(8,128)(2,1)S(1)}, u32[]{:S(2)}, u32[]{:S(2)}) %all-to-all-start) | async-done | bytes 65568 | tf_op jit(solution)/shard_map/all_to_all | solution.py:507
  27.2 0.9 spread.1
  28.1 10.0 %all-to-all-start.1 = ((bf16[8,128,128]{2,1,0:T(8,128)(2,1)}), bf16[8,128,128]{2,1,0:T(8,128)(2,1)}, u32[]{:S(2)}, u32[]{:S(2)}) async-start(bf16[8,128,128]{2,1,0:T(8,128)(2,1)} %spread.1), calls=%async_computation.1 | async-start | bytes 524288 | tf_op jit(solution)/shard_map/all_to_all | solution.py:507
  38.1 0.1 tags.1.tags_ref
  38.3 6.7 %forward.3 = (bf16[256,128]{1,0:T(8,128)(2,1)S(1)}, bf16[3,576,640]{2,1,0:T(8,128)(2,1)S(1)}, f32[3,128,512]{2,1,0:T(8,128)}) custom-call(s32[4]{0:T(128)} %refs_0_.3, s32[4,26]{1,0:T(4,128)} %refs_1_.3, f32[1,128]{1,0:T(1,128)} %bitcast.31, bf16[4,64,512]{2,1,0:T(8,128)(2,1)} %refs_3_.3, bf16[4,64,128]{2,1,0:T(8,128)(2,1)S(1)} %collective-permute-done.refs_4_, ...), custom_call_target="tpu_custom_call" | custom-call | flops 4000000000 | bytes 4000000 | tf_op jit(solution)/shard_map/forward/pallas_call | solution.py:476
  45.0 0.0 copy-start
  45.0 2.6 %all-to-all-done.1 = bf16[8,128,128]{2,1,0:T(8,128)(2,1)} async-done(((bf16[8,128,128]{2,1,0:T(8,128)(2,1)}), bf16[8,128,128]{2,1,0:T(8,128)(2,1)}, u32[]{:S(2)}, u32[]{:S(2)}) %all-to-all-start.1) | async-done | bytes 262176 | tf_op jit(solution)/shard_map/all_to_all | solution.py:507
  47.6 6.1 %all_gather.6 = bf16[16,128,128]{2,1,0:T(8,128)(2,1)S(1)} all-gather(bf16[8,128,128]{2,1,0:T(8,128)(2,1)} %all-to-all-done.1), channel_id=1, replica_groups=mesh['z'=8,'c'=2,'b'=32] {'c'}, dimensions={0}, use_global_device_ids=true | all-gather | bytes 786432 | tf_op jit(solution)/shard_map/all_gather | solution.py:532
  53.7 0.6 choose.1
  54.4 12.5 %all_to_all.30 = bf16[32,16,128]{2,1,0:T(8,128)(2,1)S(1)} all-to-all(bf16[32,16,128]{2,1,0:T(8,128)(2,1)S(1)} %choose.1), channel_id=1, replica_groups=mesh['z'=8,'c'=2,'b'=32] {'b'}, dimensions={0} | all-to-all | bytes 262144 | tf_op jit(solution)/shard_map/all_to_all | solution.py:507
  66.9 2.3 %other_half.1 = (f32[864,128]{1,0:T(8,128)S(1)}, bf16[4,128,512]{2,1,0:T(8,128)(2,1)S(1)}, f32[1,128]{1,0:T(1,128)S(1)}) custom-call(f32[1,128,512]{2,1,0:T(8,128)S(1)} %copy-done.2, f32[3,128,512]{2,1,0:T(8,128)S(1)} %copy-done, bf16[1,576,640]{2,1,0:T(8,128)(2,1)S(1)} %copy-done.1, bf16[3,576,640]{2,1,0:T(8,128)(2,1)S(1)} %get-tuple-element.31.second_stacked, ...), custom_call_target="tpu_custom_call" | custom-call | flops 1000000 | bytes 1000000 | tf_op jit(solution)/shard_map/other_half/pallas_call | solution.py:433
  69.2 4.1 %collective-permute-start.2 = (f32[864,128]{1,0:T(8,128)S(1)}, f32[864,128]{1,0:T(8,128)S(1)}, u32[]{:S(2)}, u32[]{:S(2)}) collective-permute-start(f32[864,128]{1,0:T(8,128)S(1)} %get-tuple-element.35), channel_id=1, source_target_pairs={{0,32},{32,0},{1,33},{33,1},{2,34},{34,2},{3,35},{35,3},{4,36},{36... | collective-permute-start | bytes 1327112 | tf_op jit(solution)/shard_map/ppermute | solution.py:549
  73.3 1.3 own_half.1.mine_ref
  74.5 0.1 collective-permute-done.2.got_ref
  74.7 0.5 share.1
  75.1 12.9 %all_to_all.31.pieces_ref = bf16[32,32,128]{2,1,0:T(8,128)(2,1)S(1)} all-to-all(bf16[32,32,128]{2,1,0:T(8,128)(2,1)S(1)} %share.1), channel_id=1, replica_groups=mesh['z'=8,'c'=2,'b'=32] {'b'}, dimensions={0} | all-to-all | bytes 524288 | tf_op jit(solution)/shard_map/all_to_all | solution.py:507
  88.1 0.3 over_block.1
  88.4 13.5 %all_to_all.32 = bf16[8,192,128]{2,1,0:T(8,128)(2,1)S(1)} all-to-all(bf16[8,192,128]{2,1,0:T(8,128)(2,1)S(1)} %bitcast.21), channel_id=1, replica_groups=mesh['z'=8,'c'=2,'b'=32] {'z'}, dimensions={0} | all-to-all | bytes 786432 | tf_op jit(solution)/shard_map/all_to_all | solution.py:507
  101.9 0.7 over_z.1
  102.6 9.3 %all-to-all-start.5 = ((bf16[32,14,2,128]{3,2,1,0:T(2,128)(2,1)}), bf16[32,14,2,128]{3,2,1,0:T(2,128)(2,1)S(1)}, u32[]{:S(2)}, u32[]{:S(2)}) async-start(bf16[32,14,2,128]{3,2,1,0:T(2,128)(2,1)} %bitcast.8), calls=%async_computation.5 | async-start | bytes 458752 | tf_op jit(solution)/shard_map/all_to_all | solution.py:507
  111.9 0.2 pick.1
  112.1 4.5 %collective-permute-start.3 = (bf16[2,64,128]{2,1,0:T(8,128)(2,1)S(1)}, bf16[2,64,128]{2,1,0:T(8,128)(2,1)S(1)}, u32[]{:S(2)}, u32[]{:S(2)}) collective-permute-start(bf16[2,64,128]{2,1,0:T(8,128)(2,1)S(1)} %get-tuple-element.38), channel_id=1, source_target_pairs={{0,32},{32,0},{1,33},{33,1},{2,34},{34,2},{3,35},{35,3},{4,36},{36... | collective-permute-start | bytes 98312 | tf_op jit(solution)/shard_map/ppermute | solution.py:568
  116.6 0.8 collective-permute-done.3
  117.5 0.7 copy.13
  118.1 3.3 %all-to-all-done.5 = bf16[32,14,2,128]{3,2,1,0:T(2,128)(2,1)S(1)} async-done(((bf16[32,14,2,128]{3,2,1,0:T(2,128)(2,1)}), bf16[32,14,2,128]{3,2,1,0:T(2,128)(2,1)S(1)}, u32[]{:S(2)}, u32[]{:S(2)}) %all-to-all-start.5) | async-done | bytes 229408 | tf_op jit(solution)/shard_map/all_to_all | solution.py:507
  121.4 5.7 %all_gather.7 = bf16[64,14,2,128]{3,2,1,0:T(2,128)(2,1)S(1)} all-gather(bf16[32,14,2,128]{3,2,1,0:T(2,128)(2,1)S(1)} %all-to-all-done.5), channel_id=1, replica_groups=mesh['z'=8,'c'=2,'b'=32] {'c'}, dimensions={0}, use_global_device_ids=true | all-gather | bytes 688128 | tf_op jit(solution)/shard_map/all_gather | solution.py:569
  127.1 1.2 finish.1
  (8 shorter events, 0.0 us)
Async XLA Ops:
  2.5 15.8 %collective-permute-start.1 = (bf16[4,64,128]{2,1,0:T(8,128)(2,1)S(1)}, bf16[4,64,128]{2,1,0:T(8,128)(2,1)S(1)}, u32[]{:S(2)}, u32[]{:S(2)}) collective-permute-start(bf16[4,64,128]{2,1,0:T(8,128)(2,1)S(1)} %get-tuple-element.23), channel_id=1, source_target_pairs={{1,0},{2,1},{3,2},{4,3},{5,4},{6,5},{7,6},{8,7},{9,8},{10,9},{11,1... | collective-permute-start | bytes 196616 | tf_op jit(solution)/shard_map/ppermute | solution.py:523
  3.8 14.5 %collective-permute-start = (bf16[4,64,128]{2,1,0:T(8,128)(2,1)S(1)}, bf16[4,64,128]{2,1,0:T(8,128)(2,1)S(1)}, u32[]{:S(2)}, u32[]{:S(2)}) collective-permute-start(bf16[4,64,128]{2,1,0:T(8,128)(2,1)S(1)} %get-tuple-element.23), channel_id=1, source_target_pairs={{0,1},{1,2},{2,3},{3,4},{4,5},{5,6},{6,7},{7,8},{8,9},{9,10},{10,1... | collective-permute-start | bytes 196616 | tf_op jit(solution)/shard_map/ppermute | solution.py:522
  8.4 18.8 %all-to-all-start = ((bf16[32,8,128]{2,1,0:T(8,128)(2,1)}), bf16[32,8,128]{2,1,0:T(8,128)(2,1)S(1)}, u32[]{:S(2)}, u32[]{:S(2)}) async-start(bf16[32,8,128]{2,1,0:T(8,128)(2,1)} %bitcast), calls=%async_computation | async-start | bytes 131072 | tf_op jit(solution)/shard_map/all_to_all | solution.py:507
  28.1 19.5 %all-to-all-start.1 = ((bf16[8,128,128]{2,1,0:T(8,128)(2,1)}), bf16[8,128,128]{2,1,0:T(8,128)(2,1)}, u32[]{:S(2)}, u32[]{:S(2)}) async-start(bf16[8,128,128]{2,1,0:T(8,128)(2,1)} %spread.1), calls=%async_computation.1 | async-start | bytes 524288 | tf_op jit(solution)/shard_map/all_to_all | solution.py:507
  38.3 28.6 %copy-start.2 = (f32[1,128,512]{2,1,0:T(8,128)S(1)}, f32[1,128,512]{2,1,0:T(8,128)}, u32[]{:S(2)}) copy-start(f32[1,128,512]{2,1,0:T(8,128)} %get-tuple-element.26.first_slope) | copy-start | bytes 786436
  45.0 21.9 %copy-start = (f32[3,128,512]{2,1,0:T(8,128)S(1)}, f32[3,128,512]{2,1,0:T(8,128)}, u32[]{:S(2)}) copy-start(f32[3,128,512]{2,1,0:T(8,128)} %get-tuple-element.29.second_slope) | copy-start | bytes 2359300
  47.6 19.2 %copy-start.1 = (bf16[1,576,640]{2,1,0:T(8,128)(2,1)S(1)}, bf16[1,576,640]{2,1,0:T(8,128)(2,1)}, u32[]{:S(2)}) copy-start(bf16[1,576,640]{2,1,0:T(8,128)(2,1)} %get-tuple-element.30.first_stacked) | copy-start | bytes 2211844
  69.2 5.5 %collective-permute-start.2 = (f32[864,128]{1,0:T(8,128)S(1)}, f32[864,128]{1,0:T(8,128)S(1)}, u32[]{:S(2)}, u32[]{:S(2)}) collective-permute-start(f32[864,128]{1,0:T(8,128)S(1)} %get-tuple-element.35), channel_id=1, source_target_pairs={{0,32},{32,0},{1,33},{33,1},{2,34},{34,2},{3,35},{35,3},{4,36},{36... | collective-permute-start | bytes 1327112 | tf_op jit(solution)/shard_map/ppermute | solution.py:549
  102.6 18.8 %all-to-all-start.5 = ((bf16[32,14,2,128]{3,2,1,0:T(2,128)(2,1)}), bf16[32,14,2,128]{3,2,1,0:T(2,128)(2,1)S(1)}, u32[]{:S(2)}, u32[]{:S(2)}) async-start(bf16[32,14,2,128]{3,2,1,0:T(2,128)(2,1)} %bitcast.8), calls=%async_computation.5 | async-start | bytes 458752 | tf_op jit(solution)/shard_map/all_to_all | solution.py:507
  112.1 5.3 %collective-permute-start.3 = (bf16[2,64,128]{2,1,0:T(8,128)(2,1)S(1)}, bf16[2,64,128]{2,1,0:T(8,128)(2,1)S(1)}, u32[]{:S(2)}, u32[]{:S(2)}) collective-permute-start(bf16[2,64,128]{2,1,0:T(8,128)(2,1)S(1)} %get-tuple-element.38), channel_id=1, source_target_pairs={{0,32},{32,0},{1,33},{33,1},{2,34},{34,2},{3,35},{35,3},{4,36},{36... | collective-permute-start | bytes 98312 | tf_op jit(solution)/shard_map/ppermute | solution.py:568

commit v7 on v5

--- a/solution.py
+++ b/solution.py
@@ -1,5 +1,3 @@
-import functools
-
 import jax
 import jax.numpy as jnp
 from jax import lax
@@ -9,7 +7,6 @@
 from jax.sharding import PartitionSpec as P
 
 SLOTS = 4
-FIRST = 1
 CH = 64
 OUT = 128
 VOX = 512
@@ -134,11 +131,10 @@
     ]
 
 
-def forward_kernel(start, *refs):
-    given, count = (7, FIRST) if start == 0 else (8, SLOTS - FIRST)
-    operands, refs = refs[:given], refs[given:]
-    pooled_out, stacked_ref, slope_hbm, features_ref, blocks_ref, rims_ref, slope_ref, dense_ref = refs[:8]
-    counts_ref, neighbors_ref, bias_ref, taps_ref, weight_ref, sems, out_sems = refs[8:]
+def forward_kernel(*refs):
+    operands, refs = refs[:7], refs[7:]
+    pooled_ref, stacked_ref, first_slope, second_slope, features_ref, blocks_ref, rims_ref, slope_ref, dense_ref = refs[:9]
+    counts_ref, neighbors_ref, bias_ref, taps_ref, weight_ref, sems, out_sems = refs[9:]
     targets = [
         counts_ref,
         neighbors_ref,
@@ -147,7 +143,6 @@
         rims_ref.at[pl.ds(0, SLOTS)],
         rims_ref.at[pl.ds(2 * SLOTS, SLOTS)],
         taps_ref,
-        dense_ref.at[pl.ds(0, FIRST)],
     ]
     fetch(list(zip(operands, targets)), sems)
     for index in range(SLOTS):
@@ -171,10 +166,8 @@
     def moved(array, steps):
         return pltpu.roll(array, (-steps) % FRAME, 1)
 
-    @pl.loop(0, count)
-    def _(place):
-        slot = start + place
-
+    @pl.loop(0, SLOTS)
+    def _(slot):
         def rim(ea, eb, ec):
             target = neighbors_ref[slot, column_of(ea, eb, ec)]
             at = jnp.clip(target - (first - SLOTS), 0, 3 * SLOTS - 1)
@@ -208,16 +201,24 @@
                 value = jnp.where(at_b == 0, moved(along_c[-1, ec], 56), moved(along_c[0, ec], -8))
             else:
                 value = jnp.where(at_b == 7, moved(along_c[1, ec], -56), moved(along_c[0, ec], 8))
-            stacked_ref[place, index * CH : (index + 1) * CH, :] = value.astype(jnp.bfloat16)
-
-        product = dot(weight_ref[...], stacked_ref[place])
+            stacked_ref[slot, index * CH : (index + 1) * CH, :] = value.astype(jnp.bfloat16)
+
+        product = dot(weight_ref[...], stacked_ref[slot])
         middle = pltpu.roll(product[OUT : 2 * OUT], FRAME - 64, 1)[:, :VOX]
         preact = product[:OUT, :VOX] + middle + product[2 * OUT :, 128:] + bias
         mask = voxel_mask(counts_ref[slot])
         sigmoid = jax.nn.sigmoid(preact)
         slope = sigmoid * (1.0 + preact * (1.0 - sigmoid))
-        slope_ref[place] = jnp.where(mask, slope, 0.0)
-        pltpu.make_async_copy(slope_ref.at[place], slope_hbm.at[place], out_sems.at[place]).start()
+        slope_ref[slot] = jnp.where(mask, slope, 0.0)
+
+        @pl.when(slot < 1)
+        def _():
+            pltpu.make_async_copy(slope_ref.at[slot], first_slope.at[slot], out_sems.at[slot]).start()
+
+        @pl.when(slot >= 1)
+        def _():
+            pltpu.make_async_copy(slope_ref.at[slot], second_slope.at[slot - 1], out_sems.at[slot]).start()
+
         activation = jnp.where(mask, preact * sigmoid, 0.0)
         high = activation.astype(jnp.bfloat16)
         low = (activation - high.astype(jnp.float32)).astype(jnp.bfloat16)
@@ -225,20 +226,24 @@
         cells = bf16(dot(high, table) + dot(low, table))
         even = dot(onehot((64, OUT), lambda r, c: c == 2 * r), cells)
         odd = dot(onehot((64, OUT), lambda r, c: c == 2 * r + 1), cells)
-        dense_ref[start + place] = jnp.concatenate([even, odd], axis=1)
-
-    copies = [pltpu.make_async_copy(slope_ref.at[place], slope_hbm.at[place], out_sems.at[place]) for place in range(count)]
-    if start == 0:
-        copies.append(pltpu.make_async_copy(dense_ref.at[pl.ds(0, FIRST)], pooled_out, out_sems.at[count]))
-        copies[count].start()
-    else:
-        order = onehot((8 * BLOCK, 64 * SLOTS), lambda r, c: c == 64 * ((r & 7) >> 1) + 2 * (r >> 3) + (r & 1))
-        pooled_out[...] = bf16(dot(order, bf16(dense_ref[...].reshape(64 * SLOTS, 128))))
+        dense_ref[slot] = jnp.concatenate([even, odd], axis=1)
+
+    order = onehot((8 * BLOCK, 64 * SLOTS), lambda r, c: c == 64 * ((r & 7) >> 1) + 2 * (r >> 3) + (r & 1))
+    pooled_ref[...] = bf16(dot(order, bf16(dense_ref[...].reshape(64 * SLOTS, 128))))
+    for slot in range(SLOTS):
+        target = first_slope.at[slot] if slot < 1 else second_slope.at[slot - 1]
+        pltpu.make_async_copy(slope_ref.at[slot], target, out_sems.at[slot]).wait()
+
+
+def choose_kernel(
+    first_hbm, second_hbm, tags_ref, adjoint_ref, pooled_ref, message_ref, slope_ref, sems
+):
+    copies = [
+        pltpu.make_async_copy(first_hbm, slope_ref.at[pl.ds(0, 1)], sems.at[0]),
+        pltpu.make_async_copy(second_hbm, slope_ref.at[pl.ds(1, SLOTS - 1)], sems.at[1]),
+    ]
     for copy in copies:
-        copy.wait()
-
-
-def choose_kernel(tags_ref, adjoint_ref, pooled_ref, message_ref):
+        copy.start()
     tags = bf16(tags_ref[...].astype(jnp.float32))
     tags = dot(onehot((8 * BLOCK, BLOCK), lambda r, c: (r >> 3) == c), tags)
     rows, lanes = grid_of((8 * BLOCK, 128))
@@ -253,22 +258,23 @@
     message_ref[...] = bf16(
         jnp.concatenate([cotangent.reshape(BLOCK, 8, 128), pooled.reshape(BLOCK, 8, 128)], axis=1)
     )
-
-
-def add_half(half, total_ref, grads_ref, stacked_refs):
+    for copy in copies:
+        copy.wait()
+
+
+def add_half(half, total_ref, grads_ref, stacked_ref):
     middle = HALF - 9 * CH
     for slot in range(SLOTS):
-        stacked_ref, place = (stacked_refs[0], slot) if slot < FIRST else (stacked_refs[1], slot - FIRST)
         grad = grads_ref[slot]
         wide = jnp.concatenate([grad.astype(jnp.float32), jnp.zeros((OUT, 128), jnp.float32)], axis=1)
         shifted = bf16(pltpu.roll(wide, 64, 1))
         if half == 0:
-            side = dot_lanes(stacked_ref[place, :, :VOX], grad)
-            inner = dot_lanes(stacked_ref[place, :middle, :], shifted)
+            side = dot_lanes(stacked_ref[slot, :, :VOX], grad)
+            inner = dot_lanes(stacked_ref[slot, :middle, :], shifted)
             parts = ((0, 9 * CH, side), (9 * CH, HALF, inner))
         else:
-            inner = dot_lanes(stacked_ref[place, middle:, :], shifted)
-            side = dot_lanes(stacked_ref[place, :, 128:], grad)
+            inner = dot_lanes(stacked_ref[slot, middle:, :], shifted)
+            side = dot_lanes(stacked_ref[slot, :, 128:], grad)
             parts = ((0, middle, inner), (middle, HALF, side))
         for low, high, value in parts:
             if slot == 0:
@@ -277,7 +283,7 @@
                 total_ref[low:high] += value
 
 
-def other_half_kernel(first_slope, second_slope, first_stacked, second_stacked, rows_ref, total_ref, grads_ref, bias_ref):
+def other_half_kernel(slope_ref, stacked_ref, rows_ref, total_ref, grads_ref, bias_ref):
     order = onehot(
         (64 * SLOTS, 16 * BLOCK),
         lambda r, c: c == 16 * ((r & 63) >> 1) + 2 * (r >> 6) + (r & 1),
@@ -290,8 +296,7 @@
     for slot in range(SLOTS):
         row = dense[64 * slot : 64 * (slot + 1)]
         cells = dot(even, row[:, :64]) + dot(odd, row[:, 64:])
-        slope = first_slope[slot] if slot < FIRST else second_slope[slot - FIRST]
-        grad = dot(bf16(cells), table) * slope
+        grad = dot(bf16(cells), table) * slope_ref[slot]
         bias += jnp.sum(grad, axis=1, keepdims=True)
         grads_ref[slot] = bf16(grad)
     rows, columns = grid_of((OUT, OUT))
@@ -301,16 +306,16 @@
 
         @pl.when(core == 1 - half)
         def _():
-            add_half(half, total_ref, grads_ref, (first_stacked, second_stacked))
-
-
-def own_half_kernel(grads_ref, first_stacked, second_stacked, total_ref):
+            add_half(half, total_ref, grads_ref, stacked_ref)
+
+
+def own_half_kernel(grads_ref, stacked_ref, total_ref):
     core = lax.axis_index("c")
     for half in range(2):
 
         @pl.when(core == half)
         def _():
-            add_half(half, total_ref, grads_ref, (first_stacked, second_stacked))
+            add_half(half, total_ref, grads_ref, stacked_ref)
 
 
 def share_kernel(tags_ref, mine_ref, got_ref, bias_ref, pooled_ref, message_ref):
@@ -459,38 +464,34 @@
     )
 
 
-def forward(start, *operands):
+def forward(*operands):
     in_hbm, in_vmem = pl.BlockSpec(memory_space=HBM), pl.BlockSpec(memory_space=pltpu.VMEM)
-    count = FIRST if start == 0 else SLOTS - FIRST
-    if start == 0:
-        pooled, pooled_spec = HBM((FIRST, 64, 128), jnp.float32), in_hbm
-    else:
-        pooled, pooled_spec = jax.ShapeDtypeStruct((8 * BLOCK, 128), jnp.bfloat16), in_vmem
     return pl.pallas_call(
-        functools.partial(forward_kernel, start),
+        forward_kernel,
         out_shape=[
-            pooled,
-            pltpu.VMEM((count, 9 * CH, FRAME), jnp.bfloat16),
-            HBM((count, OUT, VOX), jnp.float32),
+            jax.ShapeDtypeStruct((8 * BLOCK, 128), jnp.bfloat16),
+            pltpu.VMEM((SLOTS, 9 * CH, FRAME), jnp.bfloat16),
+            HBM((1, OUT, VOX), jnp.float32),
+            HBM((SLOTS - 1, OUT, VOX), jnp.float32),
         ],
         in_specs=[in_vmem if i in (4, 5) else in_hbm for i in range(len(operands))],
-        out_specs=[pooled_spec, in_vmem, in_hbm],
+        out_specs=[in_vmem, in_vmem, in_hbm, in_hbm],
         scratch_shapes=[
             pltpu.VMEM((SLOTS, CH, VOX), jnp.bfloat16),
             pltpu.VMEM((SLOTS + 1, CH, VOX), jnp.float32),
             pltpu.VMEM((3 * SLOTS + 1, CH, 128), jnp.bfloat16),
-            pltpu.VMEM((count, OUT, VOX), jnp.float32),
+            pltpu.VMEM((SLOTS, OUT, VOX), jnp.float32),
             pltpu.VMEM((SLOTS, 64, 128), jnp.float32),
             pltpu.SMEM((SLOTS,), jnp.int32),
             pltpu.SMEM((SLOTS, 26), jnp.int32),
             pltpu.VMEM((1, OUT), jnp.float32),
             pltpu.VMEM((TAP_ROWS, OUT), jnp.bfloat16),
             pltpu.VMEM((3 * OUT, 9 * CH), jnp.bfloat16),
-            pltpu.SemaphoreType.DMA((8,)),
-            pltpu.SemaphoreType.DMA((count + 1,)),
+            pltpu.SemaphoreType.DMA((7,)),
+            pltpu.SemaphoreType.DMA((SLOTS,)),
         ],
         compiler_params=pltpu.CompilerParams(vmem_limit_bytes=16 * 1024 * 1024),
-        cost_estimate=pl.CostEstimate(flops=4_000_000_000, bytes_accessed=4_000_000, transcendentals=150_000),
+        cost_estimate=pl.CostEstimate(flops=40_000_000_000, bytes_accessed=4_000_000, transcendentals=300_000),
         name="forward",
     )(*[operand if i in (4, 5) else hbm(operand) for i, operand in enumerate(operands)])
 
@@ -511,39 +512,39 @@
 ):
     narrow, wide = jnp.bfloat16, jnp.float32
     layers, offer = begin(counts, rebalance, coarse_owner, features, merged_adjoint)
+    offers = exchange(offer.reshape(BLOCK, 8, 128), "b")
     before = lax.ppermute(layers, "b", [(i, i + 1) for i in range(BLOCK - 1)])
     after = lax.ppermute(layers, "b", [(i + 1, i) for i in range(BLOCK - 1)])
-    offers = exchange(offer.reshape(BLOCK, 8, 128), "b")
-    weight = conv_weight.reshape(TAP_ROWS, OUT)
+    offers = offers.reshape(8 * BLOCK, 128)
+    (message,) = call(spread_kernel, "spread", [((8, 4 * BLOCK, 128), narrow, False)], (offers,))
     bias = convolution_bias_vector.reshape(1, OUT)
-    first = forward(0, counts, neighbors, bias, features, before, after, weight)
-    offers, first_dense = lax.optimization_barrier((offers.reshape(8 * BLOCK, 128), first[0]))
-    (message,) = call(spread_kernel, "spread", [((8, 4 * BLOCK, 128), narrow, False)], (offers,))
     message, bias = lax.optimization_barrier((message, bias))
     adjoint = exchange(message, "z")
     adjoint = lax.all_gather(adjoint, "c", tiled=True).reshape(64 * BLOCK, 128)
     (tags,) = call(tags_kernel, "tags", [((BLOCK, 128), jnp.int32, False)], (offers,))
-    second = forward(FIRST, counts, neighbors, bias, features, before, after, weight, first_dense)
-    (message,) = call(
+    weight = conv_weight.reshape(TAP_ROWS, OUT)
+    pooled, stacked, *slopes = forward(counts, neighbors, bias, features, before, after, weight)
+    message, slope = call(
         choose_kernel,
         "choose",
-        [((BLOCK, 16, 128), narrow, False)],
-        (tags, adjoint, second[0]),
+        [((BLOCK, 16, 128), narrow, False), ((SLOTS, OUT, VOX), wide, True)],
+        (slopes[0], slopes[1], tags, adjoint, pooled),
+        in_hbm=2,
+        scratch=[pltpu.SemaphoreType.DMA((2,))],
     )
     rows = exchange(message, "b").reshape(16 * BLOCK, 128)
-    stacked = (vmem(first[1]), vmem(second[1]))
     other, grads, bias_part = call(
         other_half_kernel,
         "other_half",
         [((HALF, OUT), wide, False), ((SLOTS, OUT, VOX), narrow, True), ((1, OUT), wide, True)],
-        (vmem(first[2]), vmem(second[2])) + stacked + (rows,),
+        (vmem(slope), vmem(stacked), rows),
     )
     got = lax.ppermute(other, "c", [(0, 1), (1, 0)])
     (mine,) = call(
         own_half_kernel,
         "own_half",
         [((HALF, OUT), wide, False)],
-        (vmem(grads),) + stacked,
+        (vmem(grads), vmem(stacked)),
         flops=2_000_000_000,
     )
     (message,) = call(

time: 130 us -> 127 us (0.977)
  waiting for transfers between devices: 11.3 us -> 8.86 us
  blocking collectives: 51.6 us -> 53.6 us
  Pallas kernels: 20.3 us -> 18.8 us
    all_to_all x3, blocking collectives: 39.8 us -> 42.7 us  [exchange(): return lax.all_to_all(message, axis, 0, 0, tiled=True)]
    all_to_all x3, waiting for transfers between devices: 10.3 us -> 7.88 us  [exchange(): return lax.all_to_all(message, axis, 0, 0, tiled=True)]
    pallas_call x2 -> x1, Pallas kernels: 10.4 us -> 8.25 us  [forward(): pl.pallas_call(forward_kernel, out_shape=[jax.ShapeDtypeStruct((8 * BLOCK...]
  transfers between devices with their start and end apart: 7 -> 7, of which waited for: 5 -> 5; matrix products, arithmetic and copies ran while one was open for 1% -> 1% of each run, Pallas kernels for 9% -> 8%
where the time goes in v7:
time: 127 us; the launch traced here: 126 us
  blocking collectives  53.6 us (42%)
  starting transfers between devices  43.7 us (34%)
  Pallas kernels  18.8 us (15%)
  waiting for transfers between devices  8.86 us (7%)
    all_to_all x3, blocking collectives, exchange(): return lax.all_to_all(message, axis, 0, 0, tiled=True)  42.7 us
    all_to_all x3, starting transfers between devices, exchange(): return lax.all_to_all(message, axis, 0, 0, tiled=True)  29.8 us
    pallas_call x11, Pallas kernels, call(): pl.pallas_call(kernel, out_shape=[pltpu.VMEM(shape, dtype) if kept else j...  10.5 us
    pallas_call x1, Pallas kernels, forward(): pl.pallas_call(forward_kernel, out_shape=[jax.ShapeDtypeStruct((8 * BLOCK...  8.25 us
    all_to_all x3, waiting for transfers between devices, exchange(): return lax.all_to_all(message, axis, 0, 0, tiled=True)  7.88 us
    all_gather x1, blocking collectives, per_device(): lax.all_gather(totals, 'c', tiled=True).reshape(2 * ROWS * BLOCK, 128)  5.72 us
    all_gather x1, blocking collectives, per_device(): adjoint = lax.all_gather(adjoint, 'c', tiled=True).reshape(64 * BLOCK, 128)  5.24 us
    ppermute x1, starting transfers between devices, per_device(): pooled = pooled_mine + lax.ppermute(pooled_other, 'c', [(0, 1), (1, 0)])  4.51 us
  transfers between devices with their start and end apart: 7, of which 5 were waited for; matrix products, arithmetic and copies ran while one was open for 1% of the time, Pallas kernels for 8%

profile of v7, /device:TPU:1, one launch (start us, length us, event | category | flops | bytes accessed | tf_op | source)
XLA Modules:
  0.0 126.3 jit_solution(3138270437521889996)
XLA Ops:
  0.6 1.8 %begin.1 = (bf16[4,64,128]{2,1,0:T(8,128)(2,1)S(1)}, bf16[256,128]{1,0:T(8,128)(2,1)}) custom-call(s32[4]{0:T(128)} %refs_0_.1, s32[4]{0:T(128)} %rebalance_hbm.1, s32[4]{0:T(128)} %owner_hbm.1, bf16[4,64,512]{2,1,0:T(8,128)(2,1)} %refs_3_.1, bf16[2,8192]{1,0:T(2,128)(2,1)} %adjoint_hbm.1), custom_call_target="tpu_custom_call" | custom-call | flops 1000000 | bytes 1000000 | tf_op jit(solution)/shard_map/begin/pallas_call | solution.py:431
  2.5 10.5 %all-to-all-start = ((bf16[32,8,128]{2,1,0:T(8,128)(2,1)}), bf16[32,8,128]{2,1,0:T(8,128)(2,1)S(1)}, u32[]{:S(2)}, u32[]{:S(2)}) async-start(bf16[32,8,128]{2,1,0:T(8,128)(2,1)} %bitcast), calls=%async_computation | async-start | bytes 131072 | tf_op jit(solution)/shard_map/all_to_all | solution.py:500
  13.0 1.3 %collective-permute-start.1 = (bf16[4,64,128]{2,1,0:T(8,128)(2,1)S(1)}, bf16[4,64,128]{2,1,0:T(8,128)(2,1)S(1)}, u32[]{:S(2)}, u32[]{:S(2)}) collective-permute-start(bf16[4,64,128]{2,1,0:T(8,128)(2,1)S(1)} %get-tuple-element.22), channel_id=1, source_target_pairs={{1,0},{2,1},{3,2},{4,3},{5,4},{6,5},{7,6},{8,7},{9,8},{10,9},{11,1... | collective-permute-start | bytes 196616 | tf_op jit(solution)/shard_map/ppermute | solution.py:517
  14.3 4.0 %collective-permute-start = (bf16[4,64,128]{2,1,0:T(8,128)(2,1)S(1)}, bf16[4,64,128]{2,1,0:T(8,128)(2,1)S(1)}, u32[]{:S(2)}, u32[]{:S(2)}) collective-permute-start(bf16[4,64,128]{2,1,0:T(8,128)(2,1)S(1)} %get-tuple-element.22), channel_id=1, source_target_pairs={{0,1},{1,2},{2,3},{3,4},{4,5},{5,6},{6,7},{7,8},{8,9},{9,10},{10,1... | collective-permute-start | bytes 196616 | tf_op jit(solution)/shard_map/ppermute | solution.py:516
  18.3 3.6 %all-to-all-done = bf16[32,8,128]{2,1,0:T(8,128)(2,1)S(1)} async-done(((bf16[32,8,128]{2,1,0:T(8,128)(2,1)}), bf16[32,8,128]{2,1,0:T(8,128)(2,1)S(1)}, u32[]{:S(2)}, u32[]{:S(2)}) %all-to-all-start) | async-done | bytes 65568 | tf_op jit(solution)/shard_map/all_to_all | solution.py:500
  21.8 0.9 spread.1
  22.7 10.0 %all-to-all-start.1 = ((bf16[8,128,128]{2,1,0:T(8,128)(2,1)}), bf16[8,128,128]{2,1,0:T(8,128)(2,1)S(1)}, u32[]{:S(2)}, u32[]{:S(2)}) async-start(bf16[8,128,128]{2,1,0:T(8,128)(2,1)} %spread.1), calls=%async_computation.1 | async-start | bytes 524288 | tf_op jit(solution)/shard_map/all_to_all | solution.py:500
  32.7 0.0 collective-permute-done.1.refs_5_
  32.8 0.0 collective-permute-done.refs_4_
  32.8 8.3 %forward.1 = (bf16[256,128]{1,0:T(8,128)(2,1)S(1)}, bf16[4,576,640]{2,1,0:T(8,128)(2,1)S(1)}, f32[1,128,512]{2,1,0:T(8,128)}, f32[3,128,512]{2,1,0:T(8,128)}) custom-call(s32[4]{0:T(128)} %refs_0_.1, s32[4,26]{1,0:T(4,128)} %refs_1_.1, f32[1,128]{1,0:T(1,128)} %bitcast.29, bf16[4,64,512]{2,1,0:T(8,128)(2,1)} %refs_3_.1, ...), custom_call_target="tpu_custom_call" | custom-call | flops 40000000000 | bytes 4000000 | tf_op jit(solution)/shard_map/forward/pallas_call | solution.py:469
  41.0 0.1 tags.1.tags_ref
  41.2 1.0 all-to-all-done.1
  42.2 5.2 %all_gather.6 = bf16[16,128,128]{2,1,0:T(8,128)(2,1)S(1)} all-gather(bf16[8,128,128]{2,1,0:T(8,128)(2,1)S(1)} %all-to-all-done.1), channel_id=1, replica_groups=mesh['z'=8,'c'=2,'b'=32] {'c'}, dimensions={0}, use_global_device_ids=true | all-gather | bytes 786432 | tf_op jit(solution)/shard_map/all_gather | solution.py:523
  47.4 1.2 choose.1
  48.7 14.6 %all_to_all.30 = bf16[32,16,128]{2,1,0:T(8,128)(2,1)S(1)} all-to-all(bf16[32,16,128]{2,1,0:T(8,128)(2,1)S(1)} %get-tuple-element.29), channel_id=1, replica_groups=mesh['z'=8,'c'=2,'b'=32] {'b'}, dimensions={0} | all-to-all | bytes 262144 | tf_op jit(solution)/shard_map/all_to_all | solution.py:500
  63.3 2.3 %other_half.1 = (f32[864,128]{1,0:T(8,128)S(1)}, bf16[4,128,512]{2,1,0:T(8,128)(2,1)S(1)}, f32[1,128]{1,0:T(1,128)S(1)}) custom-call(f32[4,128,512]{2,1,0:T(8,128)S(1)} %get-tuple-element.27.slope_ref, bf16[4,576,640]{2,1,0:T(8,128)(2,1)S(1)} %get-tuple-element.28.stacked_ref, bf16[512,128]{1,0:T(8,128)(2,1)S(1)} %bitcast.22), custom_call_target="tpu_custom_call" | custom-call | flops 1000000 | bytes 1000000 | tf_op jit(solution)/shard_map/other_half/pallas_call | solution.py:431
  65.6 4.1 %collective-permute-start.2 = (f32[864,128]{1,0:T(8,128)S(1)}, f32[864,128]{1,0:T(8,128)S(1)}, u32[]{:S(2)}, u32[]{:S(2)}) collective-permute-start(f32[864,128]{1,0:T(8,128)S(1)} %get-tuple-element.31), channel_id=1, source_target_pairs={{0,32},{32,0},{1,33},{33,1},{2,34},{34,2},{3,35},{35,3},{4,36},{36... | collective-permute-start | bytes 1327112 | tf_op jit(solution)/shard_map/ppermute | solution.py:542
  69.7 1.3 own_half.1.mine_ref
  70.9 0.1 collective-permute-done.2.got_ref
  71.1 0.5 share.1
  71.5 12.9 %all_to_all.31.pieces_ref = bf16[32,32,128]{2,1,0:T(8,128)(2,1)S(1)} all-to-all(bf16[32,32,128]{2,1,0:T(8,128)(2,1)S(1)} %share.1), channel_id=1, replica_groups=mesh['z'=8,'c'=2,'b'=32] {'b'}, dimensions={0} | all-to-all | bytes 524288 | tf_op jit(solution)/shard_map/all_to_all | solution.py:500
  84.5 0.3 over_block.1
  84.8 15.1 %all_to_all.32 = bf16[8,192,128]{2,1,0:T(8,128)(2,1)S(1)} all-to-all(bf16[8,192,128]{2,1,0:T(8,128)(2,1)S(1)} %bitcast.21), channel_id=1, replica_groups=mesh['z'=8,'c'=2,'b'=32] {'z'}, dimensions={0} | all-to-all | bytes 786432 | tf_op jit(solution)/shard_map/all_to_all | solution.py:500
  99.9 0.7 over_z.1
  100.6 9.3 %all-to-all-start.5 = ((bf16[32,14,2,128]{3,2,1,0:T(2,128)(2,1)}), bf16[32,14,2,128]{3,2,1,0:T(2,128)(2,1)S(1)}, u32[]{:S(2)}, u32[]{:S(2)}) async-start(bf16[32,14,2,128]{3,2,1,0:T(2,128)(2,1)} %bitcast.8), calls=%async_computation.5 | async-start | bytes 458752 | tf_op jit(solution)/shard_map/all_to_all | solution.py:500
  109.9 0.2 pick.1
  110.1 4.5 %collective-permute-start.3 = (bf16[2,64,128]{2,1,0:T(8,128)(2,1)S(1)}, bf16[2,64,128]{2,1,0:T(8,128)(2,1)S(1)}, u32[]{:S(2)}, u32[]{:S(2)}) collective-permute-start(bf16[2,64,128]{2,1,0:T(8,128)(2,1)S(1)} %get-tuple-element.34), channel_id=1, source_target_pairs={{0,32},{32,0},{1,33},{33,1},{2,34},{34,2},{3,35},{35,3},{4,36},{36... | collective-permute-start | bytes 98312 | tf_op jit(solution)/shard_map/ppermute | solution.py:561
  114.6 0.8 collective-permute-done.3
  115.5 0.7 copy.13
  116.1 3.3 %all-to-all-done.5 = bf16[32,14,2,128]{3,2,1,0:T(2,128)(2,1)S(1)} async-done(((bf16[32,14,2,128]{3,2,1,0:T(2,128)(2,1)}), bf16[32,14,2,128]{3,2,1,0:T(2,128)(2,1)S(1)}, u32[]{:S(2)}, u32[]{:S(2)}) %all-to-all-start.5) | async-done | bytes 229408 | tf_op jit(solution)/shard_map/all_to_all | solution.py:500
  119.4 5.7 %all_gather.7 = bf16[64,14,2,128]{3,2,1,0:T(2,128)(2,1)S(1)} all-gather(bf16[32,14,2,128]{3,2,1,0:T(2,128)(2,1)S(1)} %all-to-all-done.5), channel_id=1, replica_groups=mesh['z'=8,'c'=2,'b'=32] {'c'}, dimensions={0}, use_global_device_ids=true | all-gather | bytes 688128 | tf_op jit(solution)/shard_map/all_gather | solution.py:562
  125.2 1.2 finish.1
  (1 shorter events, 0.0 us)
Async XLA Ops:
  2.5 19.4 %all-to-all-start = ((bf16[32,8,128]{2,1,0:T(8,128)(2,1)}), bf16[32,8,128]{2,1,0:T(8,128)(2,1)S(1)}, u32[]{:S(2)}, u32[]{:S(2)}) async-start(bf16[32,8,128]{2,1,0:T(8,128)(2,1)} %bitcast), calls=%async_computation | async-start | bytes 131072 | tf_op jit(solution)/shard_map/all_to_all | solution.py:500
  13.0 19.8 %collective-permute-start.1 = (bf16[4,64,128]{2,1,0:T(8,128)(2,1)S(1)}, bf16[4,64,128]{2,1,0:T(8,128)(2,1)S(1)}, u32[]{:S(2)}, u32[]{:S(2)}) collective-permute-start(bf16[4,64,128]{2,1,0:T(8,128)(2,1)S(1)} %get-tuple-element.22), channel_id=1, source_target_pairs={{1,0},{2,1},{3,2},{4,3},{5,4},{6,5},{7,6},{8,7},{9,8},{10,9},{11,1... | collective-permute-start | bytes 196616 | tf_op jit(solution)/shard_map/ppermute | solution.py:517
  14.3 18.5 %collective-permute-start = (bf16[4,64,128]{2,1,0:T(8,128)(2,1)S(1)}, bf16[4,64,128]{2,1,0:T(8,128)(2,1)S(1)}, u32[]{:S(2)}, u32[]{:S(2)}) collective-permute-start(bf16[4,64,128]{2,1,0:T(8,128)(2,1)S(1)} %get-tuple-element.22), channel_id=1, source_target_pairs={{0,1},{1,2},{2,3},{3,4},{4,5},{5,6},{6,7},{7,8},{8,9},{9,10},{10,1... | collective-permute-start | bytes 196616 | tf_op jit(solution)/shard_map/ppermute | solution.py:516
  22.7 19.5 %all-to-all-start.1 = ((bf16[8,128,128]{2,1,0:T(8,128)(2,1)}), bf16[8,128,128]{2,1,0:T(8,128)(2,1)S(1)}, u32[]{:S(2)}, u32[]{:S(2)}) async-start(bf16[8,128,128]{2,1,0:T(8,128)(2,1)} %spread.1), calls=%async_computation.1 | async-start | bytes 524288 | tf_op jit(solution)/shard_map/all_to_all | solution.py:500
  65.6 5.5 %collective-permute-start.2 = (f32[864,128]{1,0:T(8,128)S(1)}, f32[864,128]{1,0:T(8,128)S(1)}, u32[]{:S(2)}, u32[]{:S(2)}) collective-permute-start(f32[864,128]{1,0:T(8,128)S(1)} %get-tuple-element.31), channel_id=1, source_target_pairs={{0,32},{32,0},{1,33},{33,1},{2,34},{34,2},{3,35},{35,3},{4,36},{36... | collective-permute-start | bytes 1327112 | tf_op jit(solution)/shard_map/ppermute | solution.py:542
  100.6 18.8 %all-to-all-start.5 = ((bf16[32,14,2,128]{3,2,1,0:T(2,128)(2,1)}), bf16[32,14,2,128]{3,2,1,0:T(2,128)(2,1)S(1)}, u32[]{:S(2)}, u32[]{:S(2)}) async-start(bf16[32,14,2,128]{3,2,1,0:T(2,128)(2,1)} %bitcast.8), calls=%async_computation.5 | async-start | bytes 458752 | tf_op jit(solution)/shard_map/all_to_all | solution.py:500
  110.1 5.4 %collective-permute-start.3 = (bf16[2,64,128]{2,1,0:T(8,128)(2,1)S(1)}, bf16[2,64,128]{2,1,0:T(8,128)(2,1)S(1)}, u32[]{:S(2)}, u32[]{:S(2)}) collective-permute-start(bf16[2,64,128]{2,1,0:T(8,128)(2,1)S(1)} %get-tuple-element.34), channel_id=1, source_target_pairs={{0,32},{32,0},{1,33},{33,1},{2,34},{34,2},{3,35},{35,3},{4,36},{36... | collective-permute-start | bytes 98312 | tf_op jit(solution)/shard_map/ppermute | solution.py:561

commit v8 on v7

--- a/solution.py
+++ b/solution.py
@@ -133,8 +133,8 @@
 
 def forward_kernel(*refs):
     operands, refs = refs[:7], refs[7:]
-    pooled_ref, stacked_ref, first_slope, second_slope, features_ref, blocks_ref, rims_ref, slope_ref, dense_ref = refs[:9]
-    counts_ref, neighbors_ref, bias_ref, taps_ref, weight_ref, sems, out_sems = refs[9:]
+    pooled_ref, first_stacked, second_stacked, slope_hbm, features_ref, blocks_ref, rims_ref, slope_ref = refs[:8]
+    dense_ref, first_ref, counts_ref, neighbors_ref, bias_ref, taps_ref, weight_ref, sems, out_sems = refs[8:]
     targets = [
         counts_ref,
         neighbors_ref,
@@ -166,8 +166,7 @@
     def moved(array, steps):
         return pltpu.roll(array, (-steps) % FRAME, 1)
 
-    @pl.loop(0, SLOTS)
-    def _(slot):
+    def one(slot, stacked_ref, place):
         def rim(ea, eb, ec):
             target = neighbors_ref[slot, column_of(ea, eb, ec)]
             at = jnp.clip(target - (first - SLOTS), 0, 3 * SLOTS - 1)
@@ -201,9 +200,9 @@
                 value = jnp.where(at_b == 0, moved(along_c[-1, ec], 56), moved(along_c[0, ec], -8))
             else:
                 value = jnp.where(at_b == 7, moved(along_c[1, ec], -56), moved(along_c[0, ec], 8))
-            stacked_ref[slot, index * CH : (index + 1) * CH, :] = value.astype(jnp.bfloat16)
-
-        product = dot(weight_ref[...], stacked_ref[slot])
+            stacked_ref[place, index * CH : (index + 1) * CH, :] = value.astype(jnp.bfloat16)
+
+        product = dot(weight_ref[...], stacked_ref[place])
         middle = pltpu.roll(product[OUT : 2 * OUT], FRAME - 64, 1)[:, :VOX]
         preact = product[:OUT, :VOX] + middle + product[2 * OUT :, 128:] + bias
         mask = voxel_mask(counts_ref[slot])
@@ -211,14 +210,7 @@
         slope = sigmoid * (1.0 + preact * (1.0 - sigmoid))
         slope_ref[slot] = jnp.where(mask, slope, 0.0)
 
-        @pl.when(slot < 1)
-        def _():
-            pltpu.make_async_copy(slope_ref.at[slot], first_slope.at[slot], out_sems.at[slot]).start()
-
-        @pl.when(slot >= 1)
-        def _():
-            pltpu.make_async_copy(slope_ref.at[slot], second_slope.at[slot - 1], out_sems.at[slot]).start()
-
+        pltpu.make_async_copy(slope_ref.at[slot], slope_hbm.at[slot], out_sems.at[slot]).start()
         activation = jnp.where(mask, preact * sigmoid, 0.0)
         high = activation.astype(jnp.bfloat16)
         low = (activation - high.astype(jnp.float32)).astype(jnp.bfloat16)
@@ -228,22 +220,22 @@
         odd = dot(onehot((64, OUT), lambda r, c: c == 2 * r + 1), cells)
         dense_ref[slot] = jnp.concatenate([even, odd], axis=1)
 
+    one(0, first_ref, 0)
+    frames = pltpu.make_async_copy(first_ref, first_stacked, out_sems.at[SLOTS])
+    frames.start()
+
+    @pl.loop(1, SLOTS)
+    def _(slot):
+        one(slot, second_stacked, slot - 1)
+
     order = onehot((8 * BLOCK, 64 * SLOTS), lambda r, c: c == 64 * ((r & 7) >> 1) + 2 * (r >> 3) + (r & 1))
     pooled_ref[...] = bf16(dot(order, bf16(dense_ref[...].reshape(64 * SLOTS, 128))))
     for slot in range(SLOTS):
-        target = first_slope.at[slot] if slot < 1 else second_slope.at[slot - 1]
-        pltpu.make_async_copy(slope_ref.at[slot], target, out_sems.at[slot]).wait()
-
-
-def choose_kernel(
-    first_hbm, second_hbm, tags_ref, adjoint_ref, pooled_ref, message_ref, slope_ref, sems
-):
-    copies = [
-        pltpu.make_async_copy(first_hbm, slope_ref.at[pl.ds(0, 1)], sems.at[0]),
-        pltpu.make_async_copy(second_hbm, slope_ref.at[pl.ds(1, SLOTS - 1)], sems.at[1]),
-    ]
-    for copy in copies:
-        copy.start()
+        pltpu.make_async_copy(slope_ref.at[slot], slope_hbm.at[slot], out_sems.at[slot]).wait()
+    frames.wait()
+
+
+def choose_kernel(tags_ref, adjoint_ref, pooled_ref, message_ref):
     tags = bf16(tags_ref[...].astype(jnp.float32))
     tags = dot(onehot((8 * BLOCK, BLOCK), lambda r, c: (r >> 3) == c), tags)
     rows, lanes = grid_of((8 * BLOCK, 128))
@@ -258,23 +250,22 @@
     message_ref[...] = bf16(
         jnp.concatenate([cotangent.reshape(BLOCK, 8, 128), pooled.reshape(BLOCK, 8, 128)], axis=1)
     )
-    for copy in copies:
-        copy.wait()
-
-
-def add_half(half, total_ref, grads_ref, stacked_ref):
+
+
+def add_half(half, total_ref, grads_ref, stacked_refs):
     middle = HALF - 9 * CH
     for slot in range(SLOTS):
+        stacked_ref, place = (stacked_refs[0], 0) if slot == 0 else (stacked_refs[1], slot - 1)
         grad = grads_ref[slot]
         wide = jnp.concatenate([grad.astype(jnp.float32), jnp.zeros((OUT, 128), jnp.float32)], axis=1)
         shifted = bf16(pltpu.roll(wide, 64, 1))
         if half == 0:
-            side = dot_lanes(stacked_ref[slot, :, :VOX], grad)
-            inner = dot_lanes(stacked_ref[slot, :middle, :], shifted)
+            side = dot_lanes(stacked_ref[place, :, :VOX], grad)
+            inner = dot_lanes(stacked_ref[place, :middle, :], shifted)
             parts = ((0, 9 * CH, side), (9 * CH, HALF, inner))
         else:
-            inner = dot_lanes(stacked_ref[slot, middle:, :], shifted)
-            side = dot_lanes(stacked_ref[slot, :, 128:], grad)
+            inner = dot_lanes(stacked_ref[place, middle:, :], shifted)
+            side = dot_lanes(stacked_ref[place, :, 128:], grad)
             parts = ((0, middle, inner), (middle, HALF, side))
         for low, high, value in parts:
             if slot == 0:
@@ -283,7 +274,7 @@
                 total_ref[low:high] += value
 
 
-def other_half_kernel(slope_ref, stacked_ref, rows_ref, total_ref, grads_ref, bias_ref):
+def other_half_kernel(slope_ref, first_stacked, second_stacked, rows_ref, total_ref, grads_ref, bias_ref):
     order = onehot(
         (64 * SLOTS, 16 * BLOCK),
         lambda r, c: c == 16 * ((r & 63) >> 1) + 2 * (r >> 6) + (r & 1),
@@ -306,16 +297,16 @@
 
         @pl.when(core == 1 - half)
         def _():
-            add_half(half, total_ref, grads_ref, stacked_ref)
-
-
-def own_half_kernel(grads_ref, stacked_ref, total_ref):
+            add_half(half, total_ref, grads_ref, (first_stacked, second_stacked))
+
+
+def own_half_kernel(grads_ref, first_stacked, second_stacked, total_ref):
     core = lax.axis_index("c")
     for half in range(2):
 
         @pl.when(core == half)
         def _():
-            add_half(half, total_ref, grads_ref, stacked_ref)
+            add_half(half, total_ref, grads_ref, (first_stacked, second_stacked))
 
 
 def share_kernel(tags_ref, mine_ref, got_ref, bias_ref, pooled_ref, message_ref):
@@ -470,25 +461,26 @@
         forward_kernel,
         out_shape=[
             jax.ShapeDtypeStruct((8 * BLOCK, 128), jnp.bfloat16),
-            pltpu.VMEM((SLOTS, 9 * CH, FRAME), jnp.bfloat16),
-            HBM((1, OUT, VOX), jnp.float32),
-            HBM((SLOTS - 1, OUT, VOX), jnp.float32),
+            HBM((1, 9 * CH, FRAME), jnp.bfloat16),
+            pltpu.VMEM((SLOTS - 1, 9 * CH, FRAME), jnp.bfloat16),
+            HBM((SLOTS, OUT, VOX), jnp.float32),
         ],
         in_specs=[in_vmem if i in (4, 5) else in_hbm for i in range(len(operands))],
-        out_specs=[in_vmem, in_vmem, in_hbm, in_hbm],
+        out_specs=[in_vmem, in_hbm, in_vmem, in_hbm],
         scratch_shapes=[
             pltpu.VMEM((SLOTS, CH, VOX), jnp.bfloat16),
             pltpu.VMEM((SLOTS + 1, CH, VOX), jnp.float32),
             pltpu.VMEM((3 * SLOTS + 1, CH, 128), jnp.bfloat16),
             pltpu.VMEM((SLOTS, OUT, VOX), jnp.float32),
             pltpu.VMEM((SLOTS, 64, 128), jnp.float32),
+            pltpu.VMEM((1, 9 * CH, FRAME), jnp.bfloat16),
             pltpu.SMEM((SLOTS,), jnp.int32),
             pltpu.SMEM((SLOTS, 26), jnp.int32),
             pltpu.VMEM((1, OUT), jnp.float32),
             pltpu.VMEM((TAP_ROWS, OUT), jnp.bfloat16),
             pltpu.VMEM((3 * OUT, 9 * CH), jnp.bfloat16),
             pltpu.SemaphoreType.DMA((7,)),
-            pltpu.SemaphoreType.DMA((SLOTS,)),
+            pltpu.SemaphoreType.DMA((SLOTS + 1,)),
         ],
         compiler_params=pltpu.CompilerParams(vmem_limit_bytes=16 * 1024 * 1024),
         cost_estimate=pl.CostEstimate(flops=40_000_000_000, bytes_accessed=4_000_000, transcendentals=300_000),
@@ -523,28 +515,22 @@
     adjoint = lax.all_gather(adjoint, "c", tiled=True).reshape(64 * BLOCK, 128)
     (tags,) = call(tags_kernel, "tags", [((BLOCK, 128), jnp.int32, False)], (offers,))
     weight = conv_weight.reshape(TAP_ROWS, OUT)
-    pooled, stacked, *slopes = forward(counts, neighbors, bias, features, before, after, weight)
-    message, slope = call(
-        choose_kernel,
-        "choose",
-        [((BLOCK, 16, 128), narrow, False), ((SLOTS, OUT, VOX), wide, True)],
-        (slopes[0], slopes[1], tags, adjoint, pooled),
-        in_hbm=2,
-        scratch=[pltpu.SemaphoreType.DMA((2,))],
-    )
+    pooled, *kept = forward(counts, neighbors, bias, features, before, after, weight)
+    (message,) = call(choose_kernel, "choose", [((BLOCK, 16, 128), narrow, False)], (tags, adjoint, pooled))
     rows = exchange(message, "b").reshape(16 * BLOCK, 128)
+    stacked = (vmem(kept[0]), vmem(kept[1]))
     other, grads, bias_part = call(
         other_half_kernel,
         "other_half",
         [((HALF, OUT), wide, False), ((SLOTS, OUT, VOX), narrow, True), ((1, OUT), wide, True)],
-        (vmem(slope), vmem(stacked), rows),
+        (vmem(kept[2]),) + stacked + (rows,),
     )
     got = lax.ppermute(other, "c", [(0, 1), (1, 0)])
     (mine,) = call(
         own_half_kernel,
         "own_half",
         [((HALF, OUT), wide, False)],
-        (vmem(grads), vmem(stacked)),
+        (vmem(grads),) + stacked,
         flops=2_000_000_000,
     )
     (message,) = call(

time: 127 us -> 127 us (level)
  no operation moved by 1% of the time
where the time goes in v8:
time: 127 us; the launch traced here: 126 us
  blocking collectives  53.8 us (42%)
  starting transfers between devices  43.7 us (34%)
  Pallas kernels  18.1 us (14%)
  waiting for transfers between devices  9.05 us (7%)
    all_to_all x3, blocking collectives, exchange(): return lax.all_to_all(message, axis, 0, 0, tiled=True)  42.5 us
    all_to_all x3, starting transfers between devices, exchange(): return lax.all_to_all(message, axis, 0, 0, tiled=True)  29.8 us
    pallas_call x11, Pallas kernels, call(): pl.pallas_call(kernel, out_shape=[pltpu.VMEM(shape, dtype) if kept else j...  9.91 us
    pallas_call x1, Pallas kernels, forward(): pl.pallas_call(forward_kernel, out_shape=[jax.ShapeDtypeStruct((8 * BLOCK...  8.17 us
    all_to_all x3, waiting for transfers between devices, exchange(): return lax.all_to_all(message, axis, 0, 0, tiled=True)  8.07 us
    all_gather x1, blocking collectives, per_device(): lax.all_gather(totals, 'c', tiled=True).reshape(2 * ROWS * BLOCK, 128)  5.72 us
    all_gather x1, blocking collectives, per_device(): adjoint = lax.all_gather(adjoint, 'c', tiled=True).reshape(64 * BLOCK, 128)  5.58 us
    ppermute x1, starting transfers between devices, per_device(): pooled = pooled_mine + lax.ppermute(pooled_other, 'c', [(0, 1), (1, 0)])  4.5 us
  transfers between devices with their start and end apart: 7, of which 5 were waited for; matrix products, arithmetic and copies ran while one was open for 1% of the time, Pallas kernels for 8%

profile of v8, /device:TPU:1, one launch (start us, length us, event | category | flops | bytes accessed | tf_op | source)
XLA Modules:
  0.0 126.0 jit_solution(10207081793144432218)
XLA Ops:
  0.6 1.8 %begin.1 = (bf16[4,64,128]{2,1,0:T(8,128)(2,1)S(1)}, bf16[256,128]{1,0:T(8,128)(2,1)}) custom-call(s32[4]{0:T(128)} %refs_0_.1, s32[4]{0:T(128)} %rebalance_hbm.1, s32[4]{0:T(128)} %owner_hbm.1, bf16[4,64,512]{2,1,0:T(8,128)(2,1)} %refs_3_.1, bf16[2,8192]{1,0:T(2,128)(2,1)} %adjoint_hbm.1), custom_call_target="tpu_custom_call" | custom-call | flops 1000000 | bytes 1000000 | tf_op jit(solution)/shard_map/begin/pallas_call | solution.py:422
  2.5 10.5 %all-to-all-start = ((bf16[32,8,128]{2,1,0:T(8,128)(2,1)}), bf16[32,8,128]{2,1,0:T(8,128)(2,1)S(1)}, u32[]{:S(2)}, u32[]{:S(2)}) async-start(bf16[32,8,128]{2,1,0:T(8,128)(2,1)} %bitcast), calls=%async_computation | async-start | bytes 131072 | tf_op jit(solution)/shard_map/all_to_all | solution.py:492
  13.0 1.3 %collective-permute-start.1 = (bf16[4,64,128]{2,1,0:T(8,128)(2,1)S(1)}, bf16[4,64,128]{2,1,0:T(8,128)(2,1)S(1)}, u32[]{:S(2)}, u32[]{:S(2)}) collective-permute-start(bf16[4,64,128]{2,1,0:T(8,128)(2,1)S(1)} %get-tuple-element.20), channel_id=1, source_target_pairs={{1,0},{2,1},{3,2},{4,3},{5,4},{6,5},{7,6},{8,7},{9,8},{10,9},{11,1... | collective-permute-start | bytes 196616 | tf_op jit(solution)/shard_map/ppermute | solution.py:509
  14.3 4.0 %collective-permute-start = (bf16[4,64,128]{2,1,0:T(8,128)(2,1)S(1)}, bf16[4,64,128]{2,1,0:T(8,128)(2,1)S(1)}, u32[]{:S(2)}, u32[]{:S(2)}) collective-permute-start(bf16[4,64,128]{2,1,0:T(8,128)(2,1)S(1)} %get-tuple-element.20), channel_id=1, source_target_pairs={{0,1},{1,2},{2,3},{3,4},{4,5},{5,6},{6,7},{7,8},{8,9},{9,10},{10,1... | collective-permute-start | bytes 196616 | tf_op jit(solution)/shard_map/ppermute | solution.py:508
  18.3 3.6 %all-to-all-done = bf16[32,8,128]{2,1,0:T(8,128)(2,1)S(1)} async-done(((bf16[32,8,128]{2,1,0:T(8,128)(2,1)}), bf16[32,8,128]{2,1,0:T(8,128)(2,1)S(1)}, u32[]{:S(2)}, u32[]{:S(2)}) %all-to-all-start) | async-done | bytes 65568 | tf_op jit(solution)/shard_map/all_to_all | solution.py:492
  21.8 0.9 spread.1
  22.7 10.0 %all-to-all-start.1 = ((bf16[8,128,128]{2,1,0:T(8,128)(2,1)}), bf16[8,128,128]{2,1,0:T(8,128)(2,1)}, u32[]{:S(2)}, u32[]{:S(2)}) async-start(bf16[8,128,128]{2,1,0:T(8,128)(2,1)} %spread.1), calls=%async_computation.1 | async-start | bytes 524288 | tf_op jit(solution)/shard_map/all_to_all | solution.py:492
  32.7 0.0 collective-permute-done.1.refs_5_
  32.8 0.0 collective-permute-done.refs_4_
  32.8 8.2 %forward.1 = (bf16[256,128]{1,0:T(8,128)(2,1)S(1)}, bf16[1,576,640]{2,1,0:T(8,128)(2,1)}, bf16[3,576,640]{2,1,0:T(8,128)(2,1)S(1)}, f32[4,128,512]{2,1,0:T(8,128)}) custom-call(s32[4]{0:T(128)} %refs_0_.1, s32[4,26]{1,0:T(4,128)} %refs_1_.1, f32[1,128]{1,0:T(1,128)} %bitcast.29, bf16[4,64,512]{2,1,0:T(8,128)(2,1)} %refs_3_.1, ...), custom_call_target="tpu_custom_call" | custom-call | flops 40000000000 | bytes 4000000 | tf_op jit(solution)/shard_map/forward/pallas_call | solution.py:460
  41.0 0.1 tags.1.tags_ref
  41.1 1.2 all-to-all-done.1
  42.3 5.6 %all_gather.6 = bf16[16,128,128]{2,1,0:T(8,128)(2,1)S(1)} all-gather(bf16[8,128,128]{2,1,0:T(8,128)(2,1)} %all-to-all-done.1), channel_id=1, replica_groups=mesh['z'=8,'c'=2,'b'=32] {'c'}, dimensions={0}, use_global_device_ids=true | all-gather | bytes 786432 | tf_op jit(solution)/shard_map/all_gather | solution.py:515
  47.9 0.6 choose.1
  48.5 14.6 %all_to_all.30 = bf16[32,16,128]{2,1,0:T(8,128)(2,1)S(1)} all-to-all(bf16[32,16,128]{2,1,0:T(8,128)(2,1)S(1)} %choose.1), channel_id=1, replica_groups=mesh['z'=8,'c'=2,'b'=32] {'b'}, dimensions={0} | all-to-all | bytes 262144 | tf_op jit(solution)/shard_map/all_to_all | solution.py:492
  63.1 2.3 %other_half.1 = (f32[864,128]{1,0:T(8,128)S(1)}, bf16[4,128,512]{2,1,0:T(8,128)(2,1)S(1)}, f32[1,128]{1,0:T(1,128)S(1)}) custom-call(f32[4,128,512]{2,1,0:T(8,128)S(1)} %copy-done, bf16[1,576,640]{2,1,0:T(8,128)(2,1)S(1)} %copy-done.1, bf16[3,576,640]{2,1,0:T(8,128)(2,1)S(1)} %get-tuple-element.23.second_stacked, bf16[512,128]{1,0:T(8,128)(2,1)S(1)} %bitcast.22), custom_call_target="tpu_custom_call" | custom-call | flops 1000000 | bytes 1000000 | tf_op jit(solution)/shard_map/other_half/pallas_call | solution.py:422
  65.5 4.1 %collective-permute-start.2 = (f32[864,128]{1,0:T(8,128)S(1)}, f32[864,128]{1,0:T(8,128)S(1)}, u32[]{:S(2)}, u32[]{:S(2)}) collective-permute-start(f32[864,128]{1,0:T(8,128)S(1)} %get-tuple-element.27), channel_id=1, source_target_pairs={{0,32},{32,0},{1,33},{33,1},{2,34},{34,2},{3,35},{35,3},{4,36},{36... | collective-permute-start | bytes 1327112 | tf_op jit(solution)/shard_map/ppermute | solution.py:528
  69.5 1.3 own_half.1.mine_ref
  70.8 0.1 collective-permute-done.2.got_ref
  70.9 0.5 share.1
  71.4 12.9 %all_to_all.31.pieces_ref = bf16[32,32,128]{2,1,0:T(8,128)(2,1)S(1)} all-to-all(bf16[32,32,128]{2,1,0:T(8,128)(2,1)S(1)} %share.1), channel_id=1, replica_groups=mesh['z'=8,'c'=2,'b'=32] {'b'}, dimensions={0} | all-to-all | bytes 524288 | tf_op jit(solution)/shard_map/all_to_all | solution.py:492
  84.3 0.3 over_block.1
  84.6 15.0 %all_to_all.32 = bf16[8,192,128]{2,1,0:T(8,128)(2,1)S(1)} all-to-all(bf16[8,192,128]{2,1,0:T(8,128)(2,1)S(1)} %bitcast.21), channel_id=1, replica_groups=mesh['z'=8,'c'=2,'b'=32] {'z'}, dimensions={0} | all-to-all | bytes 786432 | tf_op jit(solution)/shard_map/all_to_all | solution.py:492
  99.6 0.7 over_z.1
  100.3 9.3 %all-to-all-start.5 = ((bf16[32,14,2,128]{3,2,1,0:T(2,128)(2,1)}), bf16[32,14,2,128]{3,2,1,0:T(2,128)(2,1)S(1)}, u32[]{:S(2)}, u32[]{:S(2)}) async-start(bf16[32,14,2,128]{3,2,1,0:T(2,128)(2,1)} %bitcast.8), calls=%async_computation.5 | async-start | bytes 458752 | tf_op jit(solution)/shard_map/all_to_all | solution.py:492
  109.6 0.2 pick.1
  109.8 4.5 %collective-permute-start.3 = (bf16[2,64,128]{2,1,0:T(8,128)(2,1)S(1)}, bf16[2,64,128]{2,1,0:T(8,128)(2,1)S(1)}, u32[]{:S(2)}, u32[]{:S(2)}) collective-permute-start(bf16[2,64,128]{2,1,0:T(8,128)(2,1)S(1)} %get-tuple-element.30), channel_id=1, source_target_pairs={{0,32},{32,0},{1,33},{33,1},{2,34},{34,2},{3,35},{35,3},{4,36},{36... | collective-permute-start | bytes 98312 | tf_op jit(solution)/shard_map/ppermute | solution.py:547
  114.3 0.8 collective-permute-done.3
  115.2 0.7 copy.13
  115.8 3.3 %all-to-all-done.5 = bf16[32,14,2,128]{3,2,1,0:T(2,128)(2,1)S(1)} async-done(((bf16[32,14,2,128]{3,2,1,0:T(2,128)(2,1)}), bf16[32,14,2,128]{3,2,1,0:T(2,128)(2,1)S(1)}, u32[]{:S(2)}, u32[]{:S(2)}) %all-to-all-start.5) | async-done | bytes 229408 | tf_op jit(solution)/shard_map/all_to_all | solution.py:492
  119.1 5.7 %all_gather.7 = bf16[64,14,2,128]{3,2,1,0:T(2,128)(2,1)S(1)} all-gather(bf16[32,14,2,128]{3,2,1,0:T(2,128)(2,1)S(1)} %all-to-all-done.5), channel_id=1, replica_groups=mesh['z'=8,'c'=2,'b'=32] {'c'}, dimensions={0}, use_global_device_ids=true | all-gather | bytes 688128 | tf_op jit(solution)/shard_map/all_gather | solution.py:548
  124.8 1.2 finish.1
  (5 shorter events, 0.0 us)
Async XLA Ops:
  2.5 19.4 %all-to-all-start = ((bf16[32,8,128]{2,1,0:T(8,128)(2,1)}), bf16[32,8,128]{2,1,0:T(8,128)(2,1)S(1)}, u32[]{:S(2)}, u32[]{:S(2)}) async-start(bf16[32,8,128]{2,1,0:T(8,128)(2,1)} %bitcast), calls=%async_computation | async-start | bytes 131072 | tf_op jit(solution)/shard_map/all_to_all | solution.py:492
  13.0 19.8 %collective-permute-start.1 = (bf16[4,64,128]{2,1,0:T(8,128)(2,1)S(1)}, bf16[4,64,128]{2,1,0:T(8,128)(2,1)S(1)}, u32[]{:S(2)}, u32[]{:S(2)}) collective-permute-start(bf16[4,64,128]{2,1,0:T(8,128)(2,1)S(1)} %get-tuple-element.20), channel_id=1, source_target_pairs={{1,0},{2,1},{3,2},{4,3},{5,4},{6,5},{7,6},{8,7},{9,8},{10,9},{11,1... | collective-permute-start | bytes 196616 | tf_op jit(solution)/shard_map/ppermute | solution.py:509
  14.3 18.5 %collective-permute-start = (bf16[4,64,128]{2,1,0:T(8,128)(2,1)S(1)}, bf16[4,64,128]{2,1,0:T(8,128)(2,1)S(1)}, u32[]{:S(2)}, u32[]{:S(2)}) collective-permute-start(bf16[4,64,128]{2,1,0:T(8,128)(2,1)S(1)} %get-tuple-element.20), channel_id=1, source_target_pairs={{0,1},{1,2},{2,3},{3,4},{4,5},{5,6},{6,7},{7,8},{8,9},{9,10},{10,1... | collective-permute-start | bytes 196616 | tf_op jit(solution)/shard_map/ppermute | solution.py:508
  22.7 19.6 %all-to-all-start.1 = ((bf16[8,128,128]{2,1,0:T(8,128)(2,1)}), bf16[8,128,128]{2,1,0:T(8,128)(2,1)}, u32[]{:S(2)}, u32[]{:S(2)}) async-start(bf16[8,128,128]{2,1,0:T(8,128)(2,1)} %spread.1), calls=%async_computation.1 | async-start | bytes 524288 | tf_op jit(solution)/shard_map/all_to_all | solution.py:492
  40.9 22.2 %copy-start = (f32[4,128,512]{2,1,0:T(8,128)S(1)}, f32[4,128,512]{2,1,0:T(8,128)}, u32[]{:S(2)}) copy-start(f32[4,128,512]{2,1,0:T(8,128)} %get-tuple-element.21.slope_ref) | copy-start | bytes 3145732
  42.3 20.8 %copy-start.1 = (bf16[1,576,640]{2,1,0:T(8,128)(2,1)S(1)}, bf16[1,576,640]{2,1,0:T(8,128)(2,1)}, u32[]{:S(2)}) copy-start(bf16[1,576,640]{2,1,0:T(8,128)(2,1)} %get-tuple-element.22.first_stacked) | copy-start | bytes 2211844
  65.5 5.5 %collective-permute-start.2 = (f32[864,128]{1,0:T(8,128)S(1)}, f32[864,128]{1,0:T(8,128)S(1)}, u32[]{:S(2)}, u32[]{:S(2)}) collective-permute-start(f32[864,128]{1,0:T(8,128)S(1)} %get-tuple-element.27), channel_id=1, source_target_pairs={{0,32},{32,0},{1,33},{33,1},{2,34},{34,2},{3,35},{35,3},{4,36},{36... | collective-permute-start | bytes 1327112 | tf_op jit(solution)/shard_map/ppermute | solution.py:528
  100.3 18.8 %all-to-all-start.5 = ((bf16[32,14,2,128]{3,2,1,0:T(2,128)(2,1)}), bf16[32,14,2,128]{3,2,1,0:T(2,128)(2,1)S(1)}, u32[]{:S(2)}, u32[]{:S(2)}) async-start(bf16[32,14,2,128]{3,2,1,0:T(2,128)(2,1)} %bitcast.8), calls=%async_computation.5 | async-start | bytes 458752 | tf_op jit(solution)/shard_map/all_to_all | solution.py:492
  109.8 5.3 %collective-permute-start.3 = (bf16[2,64,128]{2,1,0:T(8,128)(2,1)S(1)}, bf16[2,64,128]{2,1,0:T(8,128)(2,1)S(1)}, u32[]{:S(2)}, u32[]{:S(2)}) collective-permute-start(bf16[2,64,128]{2,1,0:T(8,128)(2,1)S(1)} %get-tuple-element.30), channel_id=1, source_target_pairs={{0,32},{32,0},{1,33},{33,1},{2,34},{34,2},{3,35},{35,3},{4,36},{36... | collective-permute-start | bytes 98312 | tf_op jit(solution)/shard_map/ppermute | solution.py:547

commit v9 on v8

--- a/solution.py
+++ b/solution.py
@@ -224,7 +224,7 @@
     frames = pltpu.make_async_copy(first_ref, first_stacked, out_sems.at[SLOTS])
     frames.start()
 
-    @pl.loop(1, SLOTS)
+    @pl.loop(1, SLOTS, unroll=True)
     def _(slot):
         one(slot, second_stacked, slot - 1)
 

time: 127 us -> 126 us (level)
    all_to_all x3, waiting for transfers between devices: 8.07 us -> 9.37 us  [exchange(): return lax.all_to_all(message, axis, 0, 0, tiled=True)]
  transfers between devices with their start and end apart: 7 -> 7, of which waited for: 5 -> 4; matrix products, arithmetic and copies ran while one was open for 1% -> 1% of each run, Pallas kernels for 8% -> 8%
where the time goes in v9:
time: 126 us; the launch traced here: 125 us
  blocking collectives  52.6 us (42%)
  starting transfers between devices  43.9 us (35%)
  Pallas kernels  17.1 us (14%)
  waiting for transfers between devices  10.2 us (8%)
    all_to_all x3, blocking collectives, exchange(): return lax.all_to_all(message, axis, 0, 0, tiled=True)  41.3 us
    all_to_all x3, starting transfers between devices, exchange(): return lax.all_to_all(message, axis, 0, 0, tiled=True)  30.1 us
    pallas_call x11, Pallas kernels, call(): pl.pallas_call(kernel, out_shape=[pltpu.VMEM(shape, dtype) if kept else j...  10.1 us
    all_to_all x3, waiting for transfers between devices, exchange(): return lax.all_to_all(message, axis, 0, 0, tiled=True)  9.37 us
    pallas_call x1, Pallas kernels, forward(): pl.pallas_call(forward_kernel, out_shape=[jax.ShapeDtypeStruct((8 * BLOCK...  6.97 us
    all_gather x1, blocking collectives, per_device(): lax.all_gather(totals, 'c', tiled=True).reshape(2 * ROWS * BLOCK, 128)  5.7 us
    all_gather x1, blocking collectives, per_device(): adjoint = lax.all_gather(adjoint, 'c', tiled=True).reshape(64 * BLOCK, 128)  5.57 us
    ppermute x1, starting transfers between devices, per_device(): pooled = pooled_mine + lax.ppermute(pooled_other, 'c', [(0, 1), (1, 0)])  4.4 us
  transfers between devices with their start and end apart: 7, of which 4 were waited for; matrix products, arithmetic and copies ran while one was open for 1% of the time, Pallas kernels for 8%

profile of v9, /device:TPU:1, one launch (start us, length us, event | category | flops | bytes accessed | tf_op | source)
XLA Modules:
  0.0 125.1 jit_solution(13898357019510463517)
XLA Ops:
  0.6 1.8 %begin.1 = (bf16[4,64,128]{2,1,0:T(8,128)(2,1)S(1)}, bf16[256,128]{1,0:T(8,128)(2,1)}) custom-call(s32[4]{0:T(128)} %refs_0_.1, s32[4]{0:T(128)} %rebalance_hbm.1, s32[4]{0:T(128)} %owner_hbm.1, bf16[4,64,512]{2,1,0:T(8,128)(2,1)} %refs_3_.1, bf16[2,8192]{1,0:T(2,128)(2,1)} %adjoint_hbm.1), custom_call_target="tpu_custom_call" | custom-call | flops 1000000 | bytes 1000000 | tf_op jit(solution)/shard_map/begin/pallas_call | solution.py:422
  2.5 10.5 %all-to-all-start = ((bf16[32,8,128]{2,1,0:T(8,128)(2,1)}), bf16[32,8,128]{2,1,0:T(8,128)(2,1)S(1)}, u32[]{:S(2)}, u32[]{:S(2)}) async-start(bf16[32,8,128]{2,1,0:T(8,128)(2,1)} %bitcast), calls=%async_computation | async-start | bytes 131072 | tf_op jit(solution)/shard_map/all_to_all | solution.py:492
  13.0 1.3 %collective-permute-start.1 = (bf16[4,64,128]{2,1,0:T(8,128)(2,1)S(1)}, bf16[4,64,128]{2,1,0:T(8,128)(2,1)S(1)}, u32[]{:S(2)}, u32[]{:S(2)}) collective-permute-start(bf16[4,64,128]{2,1,0:T(8,128)(2,1)S(1)} %get-tuple-element.20), channel_id=1, source_target_pairs={{1,0},{2,1},{3,2},{4,3},{5,4},{6,5},{7,6},{8,7},{9,8},{10,9},{11,1... | collective-permute-start | bytes 196616 | tf_op jit(solution)/shard_map/ppermute | solution.py:509
  14.3 4.0 %collective-permute-start = (bf16[4,64,128]{2,1,0:T(8,128)(2,1)S(1)}, bf16[4,64,128]{2,1,0:T(8,128)(2,1)S(1)}, u32[]{:S(2)}, u32[]{:S(2)}) collective-permute-start(bf16[4,64,128]{2,1,0:T(8,128)(2,1)S(1)} %get-tuple-element.20), channel_id=1, source_target_pairs={{0,1},{1,2},{2,3},{3,4},{4,5},{5,6},{6,7},{7,8},{8,9},{9,10},{10,1... | collective-permute-start | bytes 196616 | tf_op jit(solution)/shard_map/ppermute | solution.py:508
  18.3 3.6 %all-to-all-done = bf16[32,8,128]{2,1,0:T(8,128)(2,1)S(1)} async-done(((bf16[32,8,128]{2,1,0:T(8,128)(2,1)}), bf16[32,8,128]{2,1,0:T(8,128)(2,1)S(1)}, u32[]{:S(2)}, u32[]{:S(2)}) %all-to-all-start) | async-done | bytes 65568 | tf_op jit(solution)/shard_map/all_to_all | solution.py:492
  21.8 0.9 spread.1
  22.7 10.0 %all-to-all-start.1 = ((bf16[8,128,128]{2,1,0:T(8,128)(2,1)}), bf16[8,128,128]{2,1,0:T(8,128)(2,1)}, u32[]{:S(2)}, u32[]{:S(2)}) async-start(bf16[8,128,128]{2,1,0:T(8,128)(2,1)} %spread.1), calls=%async_computation.1 | async-start | bytes 524288 | tf_op jit(solution)/shard_map/all_to_all | solution.py:492
  32.8 0.0 collective-permute-done.1.refs_5_
  32.8 0.0 collective-permute-done.refs_4_
  32.8 7.0 %forward.1 = (bf16[256,128]{1,0:T(8,128)(2,1)S(1)}, bf16[1,576,640]{2,1,0:T(8,128)(2,1)}, bf16[3,576,640]{2,1,0:T(8,128)(2,1)S(1)}, f32[4,128,512]{2,1,0:T(8,128)}) custom-call(s32[4]{0:T(128)} %refs_0_.1, s32[4,26]{1,0:T(4,128)} %refs_1_.1, f32[1,128]{1,0:T(1,128)} %bitcast.29, bf16[4,64,512]{2,1,0:T(8,128)(2,1)} %refs_3_.1, ...), custom_call_target="tpu_custom_call" | custom-call | flops 40000000000 | bytes 4000000 | tf_op jit(solution)/shard_map/forward/pallas_call | solution.py:460
  39.8 0.1 tags.1.tags_ref
  39.9 2.4 %all-to-all-done.1 = bf16[8,128,128]{2,1,0:T(8,128)(2,1)} async-done(((bf16[8,128,128]{2,1,0:T(8,128)(2,1)}), bf16[8,128,128]{2,1,0:T(8,128)(2,1)}, u32[]{:S(2)}, u32[]{:S(2)}) %all-to-all-start.1) | async-done | bytes 262176 | tf_op jit(solution)/shard_map/all_to_all | solution.py:492
  42.3 5.6 %all_gather.6 = bf16[16,128,128]{2,1,0:T(8,128)(2,1)S(1)} all-gather(bf16[8,128,128]{2,1,0:T(8,128)(2,1)} %all-to-all-done.1), channel_id=1, replica_groups=mesh['z'=8,'c'=2,'b'=32] {'c'}, dimensions={0}, use_global_device_ids=true | all-gather | bytes 786432 | tf_op jit(solution)/shard_map/all_gather | solution.py:515
  47.9 0.6 choose.1
  48.5 14.6 %all_to_all.30 = bf16[32,16,128]{2,1,0:T(8,128)(2,1)S(1)} all-to-all(bf16[32,16,128]{2,1,0:T(8,128)(2,1)S(1)} %choose.1), channel_id=1, replica_groups=mesh['z'=8,'c'=2,'b'=32] {'b'}, dimensions={0} | all-to-all | bytes 262144 | tf_op jit(solution)/shard_map/all_to_all | solution.py:492
  63.1 2.3 %other_half.1 = (f32[864,128]{1,0:T(8,128)S(1)}, bf16[4,128,512]{2,1,0:T(8,128)(2,1)S(1)}, f32[1,128]{1,0:T(1,128)S(1)}) custom-call(f32[4,128,512]{2,1,0:T(8,128)S(1)} %copy-done, bf16[1,576,640]{2,1,0:T(8,128)(2,1)S(1)} %copy-done.1, bf16[3,576,640]{2,1,0:T(8,128)(2,1)S(1)} %get-tuple-element.23.second_stacked, bf16[512,128]{1,0:T(8,128)(2,1)S(1)} %bitcast.22), custom_call_target="tpu_custom_call" | custom-call | flops 1000000 | bytes 1000000 | tf_op jit(solution)/shard_map/other_half/pallas_call | solution.py:422
  65.5 4.1 %collective-permute-start.2 = (f32[864,128]{1,0:T(8,128)S(1)}, f32[864,128]{1,0:T(8,128)S(1)}, u32[]{:S(2)}, u32[]{:S(2)}) collective-permute-start(f32[864,128]{1,0:T(8,128)S(1)} %get-tuple-element.27), channel_id=1, source_target_pairs={{0,32},{32,0},{1,33},{33,1},{2,34},{34,2},{3,35},{35,3},{4,36},{36... | collective-permute-start | bytes 1327112 | tf_op jit(solution)/shard_map/ppermute | solution.py:528
  69.5 1.4 %own_half.1.mine_ref = f32[864,128]{1,0:T(8,128)S(1)} custom-call(bf16[4,128,512]{2,1,0:T(8,128)(2,1)S(1)} %get-tuple-element.26.grads_ref, bf16[1,576,640]{2,1,0:T(8,128)(2,1)S(1)} %copy-done.1, bf16[3,576,640]{2,1,0:T(8,128)(2,1)S(1)} %get-tuple-element.23.second_stacked), custom_call_target="tpu_custom_call" | custom-call | flops 2000000000 | bytes 1000000 | tf_op jit(solution)/shard_map/own_half/pallas_call | solution.py:422
  71.0 0.0 collective-permute-done.2.got_ref
  71.0 0.5 share.1
  71.4 12.9 %all_to_all.31.pieces_ref = bf16[32,32,128]{2,1,0:T(8,128)(2,1)S(1)} all-to-all(bf16[32,32,128]{2,1,0:T(8,128)(2,1)S(1)} %share.1), channel_id=1, replica_groups=mesh['z'=8,'c'=2,'b'=32] {'b'}, dimensions={0} | all-to-all | bytes 524288 | tf_op jit(solution)/shard_map/all_to_all | solution.py:492
  84.4 0.3 over_block.1
  84.7 13.8 %all_to_all.32 = bf16[8,192,128]{2,1,0:T(8,128)(2,1)S(1)} all-to-all(bf16[8,192,128]{2,1,0:T(8,128)(2,1)S(1)} %bitcast.21), channel_id=1, replica_groups=mesh['z'=8,'c'=2,'b'=32] {'z'}, dimensions={0} | all-to-all | bytes 786432 | tf_op jit(solution)/shard_map/all_to_all | solution.py:492
  98.5 0.7 over_z.1
  99.2 9.6 %all-to-all-start.5 = ((bf16[32,14,2,128]{3,2,1,0:T(2,128)(2,1)}), bf16[32,14,2,128]{3,2,1,0:T(2,128)(2,1)S(1)}, u32[]{:S(2)}, u32[]{:S(2)}) async-start(bf16[32,14,2,128]{3,2,1,0:T(2,128)(2,1)} %bitcast.8), calls=%async_computation.5 | async-start | bytes 458752 | tf_op jit(solution)/shard_map/all_to_all | solution.py:492
  108.7 0.2 pick.1
  109.0 4.4 %collective-permute-start.3 = (bf16[2,64,128]{2,1,0:T(8,128)(2,1)S(1)}, bf16[2,64,128]{2,1,0:T(8,128)(2,1)S(1)}, u32[]{:S(2)}, u32[]{:S(2)}) collective-permute-start(bf16[2,64,128]{2,1,0:T(8,128)(2,1)S(1)} %get-tuple-element.30), channel_id=1, source_target_pairs={{0,32},{32,0},{1,33},{33,1},{2,34},{34,2},{3,35},{35,3},{4,36},{36... | collective-permute-start | bytes 98312 | tf_op jit(solution)/shard_map/ppermute | solution.py:547
  113.4 0.8 collective-permute-done.3
  114.2 0.7 copy.13
  114.9 3.4 %all-to-all-done.5 = bf16[32,14,2,128]{3,2,1,0:T(2,128)(2,1)S(1)} async-done(((bf16[32,14,2,128]{3,2,1,0:T(2,128)(2,1)}), bf16[32,14,2,128]{3,2,1,0:T(2,128)(2,1)S(1)}, u32[]{:S(2)}, u32[]{:S(2)}) %all-to-all-start.5) | async-done | bytes 229408 | tf_op jit(solution)/shard_map/all_to_all | solution.py:492
  118.3 5.7 %all_gather.7 = bf16[64,14,2,128]{3,2,1,0:T(2,128)(2,1)S(1)} all-gather(bf16[32,14,2,128]{3,2,1,0:T(2,128)(2,1)S(1)} %all-to-all-done.5), channel_id=1, replica_groups=mesh['z'=8,'c'=2,'b'=32] {'c'}, dimensions={0}, use_global_device_ids=true | all-gather | bytes 688128 | tf_op jit(solution)/shard_map/all_gather | solution.py:548
  124.0 1.2 finish.1
  (5 shorter events, 0.0 us)
Async XLA Ops:
  2.5 19.4 %all-to-all-start = ((bf16[32,8,128]{2,1,0:T(8,128)(2,1)}), bf16[32,8,128]{2,1,0:T(8,128)(2,1)S(1)}, u32[]{:S(2)}, u32[]{:S(2)}) async-start(bf16[32,8,128]{2,1,0:T(8,128)(2,1)} %bitcast), calls=%async_computation | async-start | bytes 131072 | tf_op jit(solution)/shard_map/all_to_all | solution.py:492
  13.0 19.8 %collective-permute-start.1 = (bf16[4,64,128]{2,1,0:T(8,128)(2,1)S(1)}, bf16[4,64,128]{2,1,0:T(8,128)(2,1)S(1)}, u32[]{:S(2)}, u32[]{:S(2)}) collective-permute-start(bf16[4,64,128]{2,1,0:T(8,128)(2,1)S(1)} %get-tuple-element.20), channel_id=1, source_target_pairs={{1,0},{2,1},{3,2},{4,3},{5,4},{6,5},{7,6},{8,7},{9,8},{10,9},{11,1... | collective-permute-start | bytes 196616 | tf_op jit(solution)/shard_map/ppermute | solution.py:509
  14.3 18.5 %collective-permute-start = (bf16[4,64,128]{2,1,0:T(8,128)(2,1)S(1)}, bf16[4,64,128]{2,1,0:T(8,128)(2,1)S(1)}, u32[]{:S(2)}, u32[]{:S(2)}) collective-permute-start(bf16[4,64,128]{2,1,0:T(8,128)(2,1)S(1)} %get-tuple-element.20), channel_id=1, source_target_pairs={{0,1},{1,2},{2,3},{3,4},{4,5},{5,6},{6,7},{7,8},{8,9},{9,10},{10,1... | collective-permute-start | bytes 196616 | tf_op jit(solution)/shard_map/ppermute | solution.py:508
  22.7 19.6 %all-to-all-start.1 = ((bf16[8,128,128]{2,1,0:T(8,128)(2,1)}), bf16[8,128,128]{2,1,0:T(8,128)(2,1)}, u32[]{:S(2)}, u32[]{:S(2)}) async-start(bf16[8,128,128]{2,1,0:T(8,128)(2,1)} %spread.1), calls=%async_computation.1 | async-start | bytes 524288 | tf_op jit(solution)/shard_map/all_to_all | solution.py:492
  39.7 23.4 %copy-start = (f32[4,128,512]{2,1,0:T(8,128)S(1)}, f32[4,128,512]{2,1,0:T(8,128)}, u32[]{:S(2)}) copy-start(f32[4,128,512]{2,1,0:T(8,128)} %get-tuple-element.21.slope_ref) | copy-start | bytes 3145732
  42.3 20.8 %copy-start.1 = (bf16[1,576,640]{2,1,0:T(8,128)(2,1)S(1)}, bf16[1,576,640]{2,1,0:T(8,128)(2,1)}, u32[]{:S(2)}) copy-start(bf16[1,576,640]{2,1,0:T(8,128)(2,1)} %get-tuple-element.22.first_stacked) | copy-start | bytes 2211844
  65.5 5.5 %collective-permute-start.2 = (f32[864,128]{1,0:T(8,128)S(1)}, f32[864,128]{1,0:T(8,128)S(1)}, u32[]{:S(2)}, u32[]{:S(2)}) collective-permute-start(f32[864,128]{1,0:T(8,128)S(1)} %get-tuple-element.27), channel_id=1, source_target_pairs={{0,32},{32,0},{1,33},{33,1},{2,34},{34,2},{3,35},{35,3},{4,36},{36... | collective-permute-start | bytes 1327112 | tf_op jit(solution)/shard_map/ppermute | solution.py:528
  99.2 19.1 %all-to-all-start.5 = ((bf16[32,14,2,128]{3,2,1,0:T(2,128)(2,1)}), bf16[32,14,2,128]{3,2,1,0:T(2,128)(2,1)S(1)}, u32[]{:S(2)}, u32[]{:S(2)}) async-start(bf16[32,14,2,128]{3,2,1,0:T(2,128)(2,1)} %bitcast.8), calls=%async_computation.5 | async-start | bytes 458752 | tf_op jit(solution)/shard_map/all_to_all | solution.py:492
  109.0 5.3 %collective-permute-start.3 = (bf16[2,64,128]{2,1,0:T(8,128)(2,1)S(1)}, bf16[2,64,128]{2,1,0:T(8,128)(2,1)S(1)}, u32[]{:S(2)}, u32[]{:S(2)}) collective-permute-start(bf16[2,64,128]{2,1,0:T(8,128)(2,1)S(1)} %get-tuple-element.30), channel_id=1, source_target_pairs={{0,32},{32,0},{1,33},{33,1},{2,34},{34,2},{3,35},{35,3},{4,36},{36... | collective-permute-start | bytes 98312 | tf_op jit(solution)/shard_map/ppermute | solution.py:547
